TPU v7x, 32 devices: a whole 2x2x4 slice. The times are simulated.
32 devices in a mesh: seq: 8 (over z, y), tp: 4 (over x, core).
Axes of the slice: x: 2, y: 2, z: 4, core: 2. Of those that a mesh axis runs over, the one named last changes fastest.
Arguments:
- inputs: bfloat16 [512, 8, 2048], P('seq'), may hold values from -6 to 6
- cotangent: bfloat16 [512, 8, 2048], P('seq'), may hold values from -6 to 6
- lengths: int32 [8], replicated, may hold values from 128 to 512, as said below
- norm_params: float32 [4, 2048], P(None, 'seq')
- entry_weight: float32 [2048, 3, 2048], P('seq', None, 'tp'), may hold values from -0.125 to 0.125
- entry_bias: float32 [3, 32, 64], P(None, 'tp', 'seq'), may hold values from -1.8 to 1.8
- output_weight: float32 [2048, 2048], P('seq', 'tp'), may hold values from -1 to 1
- gate_weight: float32 [2048, 2, 5632], P('seq', None, 'tp'), may hold values from -0.125 to 0.125
- down_weight: float32 [2048, 5632], P('seq', 'tp'), may hold values from -0.078125 to 0.078125
- moment_norm: float32 [4, 2048], P(None, 'seq'), may hold values from -112 to 112
- moment_entry: float32 [2048, 3, 2048], P('seq', None, 'tp'), may hold values from -48 to 48
- moment_bias: float32 [3, 32, 64], P(None, 'tp', 'seq'), may hold values from -48 to 48
- moment_output: float32 [2048, 2048], P('seq', 'tp'), may hold values from -16 to 16
- moment_gate: float32 [2048, 2, 5632], P('seq', None, 'tp'), may hold values from -10 to 10
- moment_down: float32 [2048, 5632], P('seq', 'tp'), may hold values from -20 to 20
- average_norm: float32 [4, 2048], P(None, 'seq')
- average_entry: float32 [2048, 3, 2048], P('seq', None, 'tp'), may hold values from -0.125 to 0.125
- average_bias: float32 [3, 32, 64], P(None, 'tp', 'seq'), may hold values from -1.8 to 1.8
- average_output: float32 [2048, 2048], P('seq', 'tp'), may hold values from -1 to 1
- average_gate: float32 [2048, 2, 5632], P('seq', None, 'tp'), may hold values from -0.125 to 0.125
- average_down: float32 [2048, 5632], P('seq', 'tp'), may hold values from -0.078125 to 0.078125
Outputs:
- layer_out: bfloat16 [512, 8, 2048], P('seq')
- input_grad: bfloat16 [512, 8, 2048], P('seq')
- momentum_norm: float32 [4, 2048], P(None, 'seq')
- momentum_entry: float32 [2048, 3, 2048], P('seq', None, 'tp')
- momentum_bias: float32 [3, 32, 64], P(None, 'tp', 'seq')
- momentum_output: float32 [2048, 2048], P('seq', 'tp')
- momentum_gate: float32 [2048, 2, 5632], P('seq', None, 'tp')
- momentum_down: float32 [2048, 5632], P('seq', 'tp')
- weight_norm: float32 [4, 2048], P(None, 'seq')
- weight_entry: float32 [2048, 3, 2048], P('seq', None, 'tp')
- weight_bias: float32 [3, 32, 64], P(None, 'tp', 'seq')
- weight_output: float32 [2048, 2048], P('seq', 'tp')
- weight_gate: float32 [2048, 2, 5632], P('seq', None, 'tp')
- weight_down: float32 [2048, 5632], P('seq', 'tp')
- smooth_norm: float32 [4, 2048], P(None, 'seq')
- smooth_entry: float32 [2048, 3, 2048], P('seq', None, 'tp')
- smooth_bias: float32 [3, 32, 64], P(None, 'tp', 'seq')
- smooth_output: float32 [2048, 2048], P('seq', 'tp')
- smooth_gate: float32 [2048, 2, 5632], P('seq', None, 'tp')
- smooth_down: float32 [2048, 5632], P('seq', 'tp')
- copy_norm: bfloat16 [4, 2048], P(None, 'seq')
- copy_entry: bfloat16 [2048, 3, 2048], P('seq', None, 'tp')
- copy_bias: bfloat16 [3, 32, 64], P(None, 'tp', 'seq')
- copy_output: bfloat16 [2048, 2048], P('seq', 'tp')
- copy_gate: bfloat16 [2048, 2, 5632], P('seq', None, 'tp')
- copy_down: bfloat16 [2048, 5632], P('seq', 'tp')
Inputs may be any that keep to these rules, and one draw needn't show every extreme that they name: `lengths`: in each micro-batch of 4 rows, at least one row is 512 tokens long.
All inputs are finite; a program needn't handle non-finite values.
Results may differ from a plain program's by a relative error of at most 0.025.
Values may be sent and summed in bfloat16 or wider, within the bound.
No kernel may reach another device: no remote copies, remote signals or barrier semaphores. Data moves between devices by JAX's collectives and lax.ppermute only.
A program may use at most 192 MiB of HBM per device.

v0:
```python
import jax
import jax.numpy as jnp
from jax import lax
from jax.sharding import PartitionSpec as P

HD = 64
ROT = 16
MICRO = 2
STEP = 10


eps = 1e-05
rates = (0.0005, 0.0002, 0.0025, 0.004, 0.0002, 6e-05)
decays = (0.0, 0.0001, 0.0, 0.0001, 0.0001, 0.0001)


def shifted(array, axis, by):
    devices = lax.axis_size(axis)
    pairs = [(i, i + by) for i in range(devices) if 0 <= i + by < devices]
    return lax.ppermute(array, axis, pairs)


def passed_along(value, axis, steps):
    count = lax.axis_size(axis)
    pairs = [(source, (source + steps) % count) for source in range(count)]
    return lax.ppermute(value, axis, pairs)


def layer_norm(values, gain, shift):
    center = values - jnp.mean(values, -1, keepdims=True)
    var = jnp.mean(center * center, -1, keepdims=True)
    inverse = lax.rsqrt(var + eps)
    normed = center * inverse
    return (normed * gain + shift, normed, inverse)


def norm_back(grad, normed, inverse, gain):
    scaled = grad * gain
    inner = (
        scaled
        - jnp.mean(scaled, -1, keepdims=True)
        - normed * jnp.mean(scaled * normed, -1, keepdims=True)
    )
    return inner * inverse


def turning(positions):
    half = ROT // 2
    freq = 10000.0 ** (-jnp.arange(half).astype(jnp.float32) / half)
    angle = positions.astype(jnp.float32)[:, None] * freq[None, :]
    return (jnp.cos(angle)[:, None, None, :], jnp.sin(angle)[:, None, None, :])


def rotate(values, cosine, sine):
    half = ROT // 2
    first = values[..., :half]
    second = values[..., half:ROT]
    return jnp.concatenate(
        [first * cosine - second * sine, second * cosine + first * sine, values[..., ROT:]], -1
    )


def allowed(key_pos, query_pos, lens):
    return (key_pos[None, None, None, :] <= query_pos[None, None, :, None]) & (
        key_pos[None, None, None, :] < lens[:, None, None, None]
    )


def body(
    inputs,
    cotangent,
    lengths,
    norm_params,
    entry_weight,
    entry_bias,
    output_weight,
    gate_weight,
    down_weight,
    moment_norm,
    moment_entry,
    moment_bias,
    moment_output,
    moment_gate,
    moment_down,
    average_norm,
    average_entry,
    average_bias,
    average_output,
    average_gate,
    average_down,
):
    bf16 = jnp.bfloat16
    f32 = jnp.float32
    w_norm, w_entry, b_entry, w_output, w_gate, w_down = (
        lax.all_gather(norm_params.astype(bf16), "seq", axis=1, tiled=True),
        lax.all_gather(entry_weight.astype(bf16), "seq", axis=0, tiled=True),
        lax.all_gather(entry_bias.astype(bf16), "seq", axis=2, tiled=True),
        lax.all_gather(output_weight.astype(bf16), "seq", axis=0, tiled=True),
        lax.all_gather(gate_weight.astype(bf16), "seq", axis=0, tiled=True),
        lax.all_gather(down_weight.astype(bf16), "seq", axis=0, tiled=True),
    )
    block_len = inputs.shape[0]
    width = inputs.shape[2]
    per_micro = inputs.shape[1] // MICRO
    local_width = w_entry.shape[2]
    heads_here = local_width // HD
    seq_count = lax.axis_size("seq")
    seq_rank = lax.axis_index("seq")
    tokens = block_len * per_micro
    gains = w_norm.astype(f32)
    entry_shift = b_entry.astype(f32).reshape(3, local_width)
    query_pos = seq_rank * block_len + jnp.arange(block_len, dtype=jnp.int32)
    cosine, sine = turning(query_pos)
    grad_norm = jnp.zeros((4, width), f32)
    grad_entry = jnp.zeros(w_entry.shape, f32)
    grad_bias = jnp.zeros((3, local_width), f32)
    grad_output = jnp.zeros(w_output.shape, f32)
    grad_gate = jnp.zeros(w_gate.shape, f32)
    grad_down = jnp.zeros(w_down.shape, f32)
    outputs = []
    input_grads = []
    for micro in range(MICRO):
        lo_row = micro * per_micro
        lens = lengths[lo_row : lo_row + per_micro]
        longest = jnp.max(lens)
        resid = inputs[:, lo_row : lo_row + per_micro].astype(f32).reshape(tokens, width)
        h_first, n_first, i_first = layer_norm(resid, gains[0], gains[1])
        a_first = h_first.astype(bf16)
        mixed = (
            jnp.einsum("td,dcf->tcf", a_first, w_entry, preferred_element_type=f32) + entry_shift
        )
        heads = mixed.reshape(block_len, per_micro, 3, heads_here, HD)
        query = (rotate(heads[:, :, 0], cosine, sine) * 0.125).astype(bf16)
        keys = rotate(heads[:, :, 1], cosine, sine).astype(bf16)
        vals = heads[:, :, 2].astype(bf16)
        key_flat = keys.reshape(block_len, per_micro, local_width)
        val_flat = vals.reshape(block_len, per_micro, local_width)
        start_state = (
            jnp.full((per_micro, heads_here, block_len), -1e30, f32),
            jnp.zeros((per_micro, heads_here, block_len), f32),
            jnp.zeros((per_micro, heads_here, block_len, HD), f32),
        )
        piece = (
            lax.all_gather(key_flat, "seq", axis=0, tiled=True),
            lax.all_gather(val_flat, "seq", axis=0, tiled=True),
        )
        first = jnp.int32(0)
        count = piece[0].shape[0]
        key_h = piece[0].reshape(count, per_micro, heads_here, HD)
        val_h = piece[1].reshape(count, per_micro, heads_here, HD)

        def update(state):
            top, total, acc = state
            valid = allowed(jnp.arange(count, dtype=jnp.int32), query_pos, lens)
            scores = jnp.einsum("qrhd,krhd->rhqk", query, key_h, preferred_element_type=f32)
            scores = jnp.where(valid, scores, -1e30)
            new_top = jnp.maximum(top, jnp.max(scores, -1))
            weights = jnp.where(valid, jnp.exp(scores - new_top[..., None]), 0.0)
            total = jnp.sum(weights, -1)
            acc = jnp.einsum(
                "rhqk,krhd->rhqd", weights.astype(bf16), val_h, preferred_element_type=f32
            )
            return (new_top, total, acc)

        active = (first <= query_pos[-1]) & (first < longest)
        top, total, acc = lax.cond(active, update, lambda state: state, start_state)
        attended = jnp.transpose(acc / total[..., None], (2, 0, 1, 3))
        att_low = attended.reshape(tokens, local_width).astype(bf16)
        attn_part = jnp.einsum("th,dh->td", att_low, w_output, preferred_element_type=f32)
        second = resid + lax.psum(attn_part.astype(jnp.bfloat16), "tp").astype(jnp.float32)
        h_second, n_second, i_second = layer_norm(second, gains[2], gains[3])
        a_second = h_second.astype(bf16)
        gated = jnp.einsum("td,dgf->tgf", a_second, w_gate, preferred_element_type=f32)
        gate = gated[:, 0]
        upper = gated[:, 1]
        sigma = jax.nn.sigmoid(gate)
        active_gate = gate * sigma
        hidden = (active_gate * upper).astype(bf16)
        ffn_part = jnp.einsum("tf,df->td", hidden, w_down, preferred_element_type=f32)
        result = second + lax.psum(ffn_part.astype(jnp.bfloat16), "tp").astype(jnp.float32)
        outputs.append(result.astype(bf16).reshape(block_len, per_micro, width))
        real = (query_pos[:, None] < lens[None, :]).reshape(tokens, 1)
        grad_y = jnp.where(
            real, cotangent[:, lo_row : lo_row + per_micro].astype(f32).reshape(tokens, width), 0.0
        )
        grad_y_low = grad_y.astype(bf16)
        grad_down = grad_down + jnp.einsum(
            "td,tf->df", grad_y_low, hidden, preferred_element_type=f32
        )
        grad_hidden = jnp.einsum(
            "td,df->tf", grad_y_low, w_down, preferred_element_type=f32
        ).astype(bf16)
        grad_gate_val = grad_hidden * upper * (sigma * (1.0 + gate * (1.0 - sigma)))
        grad_up_val = grad_hidden * active_gate
        grad_gated = jnp.stack([grad_gate_val, grad_up_val], 1).astype(bf16)
        grad_gate = grad_gate + jnp.einsum(
            "td,tgf->dgf", a_second, grad_gated, preferred_element_type=f32
        )
        grad_h2 = lax.psum(
            jnp.einsum("tgf,dgf->td", grad_gated, w_gate, preferred_element_type=f32).astype(
                jnp.bfloat16
            ),
            "tp",
        ).astype(jnp.float32)
        grad_second = grad_y + norm_back(grad_h2, n_second, i_second, gains[2])
        grad_second_low = grad_second.astype(bf16)
        grad_output = grad_output + jnp.einsum(
            "td,th->dh", grad_second_low, att_low, preferred_element_type=f32
        )
        grad_att = jnp.einsum(
            "td,dh->th", grad_second_low, w_output, preferred_element_type=f32
        ).astype(bf16)
        grad_att4 = grad_att.reshape(block_len, per_micro, heads_here, HD)
        delta = jnp.transpose(jnp.sum(grad_att4.astype(f32) * attended, -1), (1, 2, 0))

        def pair_grads(
            q_block,
            ga_block,
            top_block,
            total_block,
            delta_block,
            qpos_block,
            key_piece,
            val_piece,
            first,
        ):
            count = key_piece.shape[0]
            key_h = key_piece.reshape(count, per_micro, heads_here, HD)
            val_h = val_piece.reshape(count, per_micro, heads_here, HD)
            valid = allowed(first + jnp.arange(count, dtype=jnp.int32), qpos_block, lens)
            scores = jnp.einsum("qrhd,krhd->rhqk", q_block, key_h, preferred_element_type=f32)
            probs = jnp.where(
                valid, jnp.exp(scores - top_block[..., None]) / total_block[..., None], 0.0
            )
            grad_val = jnp.einsum(
                "rhqk,qrhd->krhd", probs.astype(bf16), ga_block, preferred_element_type=f32
            )
            grad_prob = jnp.einsum("qrhd,krhd->rhqk", ga_block, val_h, preferred_element_type=f32)
            grad_score = (probs * (grad_prob - delta_block[..., None])).astype(bf16)
            grad_query = jnp.einsum(
                "rhqk,krhd->qrhd", grad_score, key_h, preferred_element_type=f32
            )
            grad_key = jnp.einsum(
                "rhqk,qrhd->krhd", grad_score, q_block, preferred_element_type=f32
            )
            both = jnp.stack(
                [
                    grad_key.reshape(count, per_micro, local_width),
                    grad_val.reshape(count, per_micro, local_width),
                ],
                2,
            )
            return (grad_query, both)

        def block_grads(key_piece, val_piece, first):
            return pair_grads(
                query, grad_att4, top, total, delta, query_pos, key_piece, val_piece, first
            )

        kv_pair = jnp.stack([key_flat, val_flat])
        zero_query = jnp.zeros((block_len, per_micro, heads_here, HD), f32)
        zero_kv = jnp.zeros((block_len, per_micro, 2, local_width), f32)

        def circle_turn(index, carry):
            pair_now, grads_now, grad_query = carry
            owner = (seq_rank - index) % seq_count
            first = owner * block_len
            active = (owner <= seq_rank) & (first < longest)

            def work(state):
                part_query, part_kv = block_grads(pair_now[0], pair_now[1], first)
                return (state[0] + part_query, state[1] + part_kv)

            grad_query, grads_now = lax.cond(
                active, work, lambda state: state, (grad_query, grads_now)
            )
            pair_now = shifted(pair_now, "seq", 1)
            grads_now = passed_along(grads_now.astype(jnp.bfloat16), "seq", 1).astype(
                grads_now.dtype
            )
            return (pair_now, grads_now, grad_query)

        pair_end, grad_kv, grad_query = lax.fori_loop(
            0, seq_count, circle_turn, (kv_pair, zero_kv, zero_query)
        )
        grad_q_raw = rotate(grad_query * 0.125, cosine, -sine)
        grad_k_raw = rotate(
            grad_kv[:, :, 0].reshape(block_len, per_micro, heads_here, HD), cosine, -sine
        )
        grad_v_raw = grad_kv[:, :, 1].reshape(block_len, per_micro, heads_here, HD)
        grad_mixed = (
            jnp.stack([grad_q_raw, grad_k_raw, grad_v_raw], 2)
            .reshape(tokens, 3, local_width)
            .astype(bf16)
        )
        grad_bias = grad_bias + jnp.sum(grad_mixed.astype(f32), 0)
        grad_entry = grad_entry + jnp.einsum(
            "td,tcf->dcf", a_first, grad_mixed, preferred_element_type=f32
        )
        grad_h1 = lax.psum(
            jnp.einsum("tcf,dcf->td", grad_mixed, w_entry, preferred_element_type=f32).astype(
                jnp.bfloat16
            ),
            "tp",
        ).astype(jnp.float32)
        grad_norm = grad_norm + jnp.stack(
            [
                jnp.sum(grad_h1 * n_first, 0),
                jnp.sum(grad_h1, 0),
                jnp.sum(grad_h2 * n_second, 0),
                jnp.sum(grad_h2, 0),
            ]
        )
        grad_input = grad_second + norm_back(grad_h1, n_first, i_first, gains[0])
        input_grads.append(grad_input.astype(bf16).reshape(block_len, per_micro, width))
    reduced = (
        lax.psum_scatter(
            grad_norm.astype(jnp.bfloat16), "seq", scatter_dimension=1, tiled=True
        ).astype(jnp.float32),
        lax.psum_scatter(
            grad_entry.astype(jnp.bfloat16), "seq", scatter_dimension=0, tiled=True
        ).astype(jnp.float32),
        lax.psum_scatter(
            grad_bias.reshape(3, heads_here, HD).astype(jnp.bfloat16),
            "seq",
            scatter_dimension=2,
            tiled=True,
        ).astype(jnp.float32),
        lax.psum_scatter(
            grad_output.astype(jnp.bfloat16), "seq", scatter_dimension=0, tiled=True
        ).astype(jnp.float32),
        lax.psum_scatter(
            grad_gate.astype(jnp.bfloat16), "seq", scatter_dimension=0, tiled=True
        ).astype(jnp.float32),
        lax.psum_scatter(
            grad_down.astype(jnp.bfloat16), "seq", scatter_dimension=0, tiled=True
        ).astype(jnp.float32),
    )
    masters = (norm_params, entry_weight, entry_bias, output_weight, gate_weight, down_weight)
    moments = (moment_norm, moment_entry, moment_bias, moment_output, moment_gate, moment_down)
    averages = (
        average_norm,
        average_entry,
        average_bias,
        average_output,
        average_gate,
        average_down,
    )
    beta = min(0.999, (1 + STEP) / (10 + STEP))
    news, weights, smooths, copies = ([], [], [], [])
    for index in range(6):
        grad = reduced[index] + decays[index] * masters[index]
        moment = 0.9 * moments[index] + grad
        weight = masters[index] - rates[index] * (grad + 0.9 * moment)
        news.append(moment)
        weights.append(weight)
        smooths.append(beta * averages[index] + (1.0 - beta) * weight)
        copies.append(weight.astype(bf16))
    return (
        jnp.concatenate(outputs, 1),
        jnp.concatenate(input_grads, 1),
        news[0],
        news[1],
        news[2],
        news[3],
        news[4],
        news[5],
        weights[0],
        weights[1],
        weights[2],
        weights[3],
        weights[4],
        weights[5],
        smooths[0],
        smooths[1],
        smooths[2],
        smooths[3],
        smooths[4],
        smooths[5],
        copies[0],
        copies[1],
        copies[2],
        copies[3],
        copies[4],
        copies[5],
    )


def solution(mesh):
    in_specs = (
        P("seq", None, None),
        P("seq", None, None),
        P(),
        P(None, "seq"),
        P("seq", None, "tp"),
        P(None, "tp", "seq"),
        P("seq", "tp"),
        P("seq", None, "tp"),
        P("seq", "tp"),
        P(None, "seq"),
        P("seq", None, "tp"),
        P(None, "tp", "seq"),
        P("seq", "tp"),
        P("seq", None, "tp"),
        P("seq", "tp"),
        P(None, "seq"),
        P("seq", None, "tp"),
        P(None, "tp", "seq"),
        P("seq", "tp"),
        P("seq", None, "tp"),
        P("seq", "tp"),
    )
    out_specs = (
        P("seq", None, None),
        P("seq", None, None),
        P(None, "seq"),
        P("seq", None, "tp"),
        P(None, "tp", "seq"),
        P("seq", "tp"),
        P("seq", None, "tp"),
        P("seq", "tp"),
        P(None, "seq"),
        P("seq", None, "tp"),
        P(None, "tp", "seq"),
        P("seq", "tp"),
        P("seq", None, "tp"),
        P("seq", "tp"),
        P(None, "seq"),
        P("seq", None, "tp"),
        P(None, "tp", "seq"),
        P("seq", "tp"),
        P("seq", None, "tp"),
        P("seq", "tp"),
        P(None, "seq"),
        P("seq", None, "tp"),
        P(None, "tp", "seq"),
        P("seq", "tp"),
        P("seq", None, "tp"),
        P("seq", "tp"),
    )
    return jax.shard_map(body, mesh=mesh, in_specs=in_specs, out_specs=out_specs, check_vma=False)
```

profile of v0, /device:TPU:16, one launch (start us, length us, event | category | flops | bytes accessed | tf_op | source)
XLA Modules:
  0.0 2115.8 jit_solution(7547203087381342570)
XLA Ops:
  16.0 26.5 %all_gather.32 = bf16[3,8,64]{1,0,2:T(4,128)(2,1)S(1)} all-gather(bf16[3,8,8]{1,0,2:T(4,128)(2,1)S(1)} %copy.260), channel_id=1, replica_groups=mesh['seq'=8,'tp'=4] {'seq'}, dimensions={2}, use_global_device_ids=true | all-gather | bytes 3456 | tf_op jit(solution)/shard_map/all_gather | solution.py:97
  54.4 28.5 %all_gather.30 = bf16[4,2048]{1,0:T(4,128)(2,1)S(1)} all-gather(bf16[4,256]{1,0:T(4,128)(2,1)S(1)} %convert_element_type.423), channel_id=1, replica_groups=mesh['seq'=8,'tp'=4] {'seq'}, dimensions={1}, use_global_device_ids=true | all-gather | bytes 18432 | tf_op jit(solution)/shard_map/all_gather | solution.py:95
  83.0 27.9 %all-gather.9.cloned.1.call-done = bf16[2048,3,512]{2,0,1:T(8,128)(2,1)} async-done(((bf16[256,3,512]{2,0,1:T(8,128)(2,1)}), bf16[2048,3,512]{2,0,1:T(8,128)(2,1)}) %all-gather.9.cloned.1.call-update) | async-done | bytes 6291472 | tf_op jit(solution)/shard_map/all_gather | solution.py:96
  139.8 11.3 all-gather.11.cloned.1.call-start
  163.5 21.8 %all-gather.21.cloned.1.call-done = bf16[512,4,512]{2,0,1:T(8,128)(2,1)} async-done(((bf16[64,4,512]{2,0,1:T(8,128)(2,1)}), bf16[512,4,512]{2,0,1:T(8,128)(2,1)}) %all-gather.21.cloned.1.call-update) | async-done | bytes 2097168 | tf_op jit(solution)/shard_map/all_gather | solution.py:144
  185.3 50.5 %all-gather.23.cloned.1.call-done = bf16[512,4,512]{2,1,0:T(4,128)(2,1)} async-done(((bf16[64,4,512]{2,1,0:T(4,128)(2,1)}), bf16[512,4,512]{2,1,0:T(4,128)(2,1)}) %all-gather.23.cloned.1.call-update) | async-done | bytes 2097168 | tf_op jit(solution)/shard_map/all_gather | solution.py:145
  235.8 13.9 conditional.5
  250.8 35.4 %all-gather.11.cloned.1.call-done = bf16[512,4,512]{2,0,1:T(8,128)(2,1)} async-done(((bf16[64,4,512]{2,0,1:T(8,128)(2,1)}), bf16[512,4,512]{2,0,1:T(8,128)(2,1)}) %all-gather.11.cloned.1.call-update) | async-done | bytes 2097168 | tf_op jit(solution)/shard_map/all_gather | solution.py:144
  286.2 50.4 %all-gather.13.cloned.1.call-done = bf16[512,4,512]{2,1,0:T(4,128)(2,1)} async-done(((bf16[64,4,512]{2,1,0:T(4,128)(2,1)}), bf16[512,4,512]{2,1,0:T(4,128)(2,1)}) %all-gather.13.cloned.1.call-update) | async-done | bytes 2097168 | tf_op jit(solution)/shard_map/all_gather | solution.py:145
  336.6 13.9 conditional.4
  351.5 35.4 %all-gather.15.cloned.1.call-done = bf16[2048,512]{1,0:T(8,128)(2,1)} async-done(((bf16[256,512]{1,0:T(8,128)(2,1)}), bf16[2048,512]{1,0:T(8,128)(2,1)}) %all-gather.15.cloned.1.call-update) | async-done | bytes 2097168 | tf_op jit(solution)/shard_map/all_gather | solution.py:98
  399.1 43.9 %all-reduce.12.cloned.1.call-done = (bf16[256,2048]{1,0:T(8,128)(2,1)}, bf16[256,2048]{1,0:T(8,128)(2,1)}) async-done(((bf16[256,2048]{1,0:T(8,128)(2,1)}, bf16[256,2048]{1,0:T(8,128)(2,1)}), (bf16[256,2048]{1,0:T(8,128)(2,1)}, bf16[256,2048]{1,0:T(8,128)(2,1)})) %all-reduce.12.cloned.1.call-update) | async-done | bytes 2097168 | tf_op jit(solution)/shard_map/psum | solution.py:170
  447.6 161.2 %all-gather.17.cloned.1.call-done = bf16[2048,2,1408]{2,0,1:T(8,128)(2,1)} async-done(((bf16[256,2,1408]{2,0,1:T(8,128)(2,1)}), bf16[2048,2,1408]{2,0,1:T(8,128)(2,1)}) %all-gather.17.cloned.1.call-update) | async-done | bytes 11534352 | tf_op jit(solution)/shard_map/all_gather | solution.py:99
  631.5 109.0 %reduce-scatter.15.cloned.1.call-done = bf16[256,1408]{1,0:T(8,128)(2,1)} async-done(((bf16[2048,1408]{1,0:T(8,128)(2,1)}), bf16[256,1408]{1,0:T(8,128)(2,1)}) %reduce-scatter.15.cloned.1.call-update) | async-done | bytes 720912 | tf_op jit(solution)/shard_map/reduce_scatter | solution.py:335
  767.2 69.2 %all-gather.19.cloned.1.call-done = bf16[2048,1408]{1,0:T(8,128)(2,1)} async-done(((bf16[256,1408]{1,0:T(8,128)(2,1)}), bf16[2048,1408]{1,0:T(8,128)(2,1)}) %all-gather.19.cloned.1.call-update) | async-done | bytes 5767184 | tf_op jit(solution)/shard_map/all_gather | solution.py:100
  878.4 38.4 %all-reduce.10.cloned.1.call-done = (bf16[256,2048]{1,0:T(8,128)(2,1)}, bf16[256,2048]{1,0:T(8,128)(2,1)}) async-done(((bf16[256,2048]{1,0:T(8,128)(2,1)}, bf16[256,2048]{1,0:T(8,128)(2,1)}), (bf16[256,2048]{1,0:T(8,128)(2,1)}, bf16[256,2048]{1,0:T(8,128)(2,1)})) %all-reduce.10.cloned.1.call-update) | async-done | bytes 2097168 | tf_op jit(solution)/shard_map/psum | solution.py:199
  935.9 294.2 %while.41 = (s32[]{:T(128)}, bf16[2,64,4,512]{3,1,2,0:T(8,128)(2,1)S(1)}, f32[64,4,2,512]{3,0,1,2:T(8,128)}, f32[64,4,8,64]{3,0,2,1:T(8,128)}, s32[]{:T(128)}, /...) while((s32[]{:T(128)}, ...), condition=%wide.region_40.41_spmd.clone, body=%wide.region_37.40_spmd.clone.sunk | while | flops 86266256 | bytes 29428624 | solution.py:283
  937.5 13.5 conditional.11
  956.0 10.9 collective-permute-done.3
  979.8 13.5 conditional.11
  998.3 10.9 collective-permute-done.3
  1021.1 13.5 conditional.11
  1039.6 10.9 collective-permute-done.3
  1061.6 13.5 conditional.11
  1080.1 10.9 collective-permute-done.3
  1101.1 13.5 conditional.11
  1119.6 10.9 collective-permute-done.3
  1139.8 13.2 collective-permute-start.3
  1177.2 18.7 collective-permute-start.2
  1234.9 263.2 %while.40 = (s32[]{:T(128)}, bf16[2,64,4,512]{3,1,2,0:T(8,128)(2,1)S(1)}, f32[64,4,2,512]{3,0,1,2:T(8,128)S(1)}, f32[64,4,8,64]{3,0,2,1:T(8,128)}, s32[]{:T(128)...) while((s32[]{:T(128)}, ...), condition=%wide.region_29.30_spmd.clone, body=%wide.region_26.29_spmd.clone.sunk | while | flops 86266256 | bytes 30477236 | solution.py:283
  1236.8 13.2 conditional.10
  1259.2 9.3 collective-permute-start
  1278.8 13.3 conditional.10
  1315.3 13.2 conditional.10
  1350.8 13.2 conditional.10
  1366.8 11.3 collective-permute-done.1
  1385.3 13.2 conditional.10
  1400.7 11.1 collective-permute-done.1
  1422.0 9.8 collective-permute-start.1
  1440.9 10.0 collective-permute-done
  1455.1 12.4 collective-permute-start
  1538.4 95.8 %all-reduce.8.cloned.1.call-done = (bf16[256,2048]{1,0:T(8,128)(2,1)}, bf16[256,2048]{1,0:T(8,128)(2,1)}, bf16[256,2048]{1,0:T(8,128)(2,1)}, bf16[256,2048]{1,0:T(8,128)(2,1)}) async-done(((bf16[256,2048]{1,0:T(8,128)(2,1)}, bf16[256,2048]{1,0:T(8,128)(2,1)}, bf16[256,2048]{1,0:T(8,128)(2,1)}, bf16[256,2048]{1,0:T(8,128)(2,1)}), (bf16[256,2048]{1,0:T(8,128)(2,1)}, bf16[256,2048]{1,0:T(8,128)(2,1)}, ...) | async-done | bytes 4194320 | tf_op jit(solution)/shard_map/psum | solution.py:180
  1659.0 10.9 fusion.120
  1670.0 13.2 add_convert_fusion
  1688.3 16.3 all-reduce
  1730.0 45.0 %reduce-scatter.11.cloned.1.call-done = bf16[256,512]{1,0:T(8,128)(2,1)} async-done(((bf16[2048,512]{1,0:T(8,128)(2,1)}), bf16[256,512]{1,0:T(8,128)(2,1)}) %reduce-scatter.11.cloned.1.call-update) | async-done | bytes 262160 | tf_op jit(solution)/shard_map/reduce_scatter | solution.py:329
  1779.1 116.9 %reduce-scatter.9.cloned.1.call-done = bf16[256,3,512]{2,0,1:T(8,128)(2,1)} async-done(((bf16[2048,3,512]{2,0,1:T(8,128)(2,1)}), bf16[256,3,512]{2,0,1:T(8,128)(2,1)}) %reduce-scatter.9.cloned.1.call-update) | async-done | bytes 786448 | tf_op jit(solution)/shard_map/reduce_scatter | solution.py:320
  1902.4 188.8 %reduce-scatter.13.cloned.1.call-done = bf16[256,2,1408]{2,0,1:T(8,128)(2,1)} async-done(((bf16[2048,2,1408]{2,0,1:T(8,128)(2,1)}), bf16[256,2,1408]{2,0,1:T(8,128)(2,1)}) %reduce-scatter.13.cloned.1.call-update) | async-done | bytes 1441808 | tf_op jit(solution)/shard_map/reduce_scatter | solution.py:332
  (927 shorter events, 736.9 us)
Async XLA Ops:
  7.2 103.7 %all-gather.9.cloned.1.call-start = ((), (), s32[]{:S(2)}) async-start(), calls=%async_computation.5 | async-start | bytes 7077888 | tf_op jit(solution)/shard_map/all_gather | solution.py:96
  9.8 175.5 %all-gather.21.cloned.1.call-start = ((), (), s32[]{:S(2)}) async-start(), calls=%async_computation.11 | async-start | bytes 2359296 | tf_op jit(solution)/shard_map/all_gather | solution.py:144
  137.4 98.4 %all-gather.23.cloned.1.call-start = ((), (), s32[]{:S(2)}) async-start(), calls=%async_computation.12 | async-start | bytes 2359296 | tf_op jit(solution)/shard_map/all_gather | solution.py:145
  139.8 146.4 %all-gather.11.cloned.1.call-start = ((), (), s32[]{:S(2)}) async-start(), calls=%async_computation.6 | async-start | bytes 2359296 | tf_op jit(solution)/shard_map/all_gather | solution.py:144
  152.9 183.7 %all-gather.13.cloned.1.call-start = ((), (), s32[]{:S(2)}) async-start(), calls=%async_computation.7 | async-start | bytes 2359296 | tf_op jit(solution)/shard_map/all_gather | solution.py:145
  155.3 231.6 %all-gather.15.cloned.1.call-start = ((), (), s32[]{:S(2)}) async-start(), calls=%async_computation.8 | async-start | bytes 2359296 | tf_op jit(solution)/shard_map/all_gather | solution.py:98
  156.2 286.8 %all-reduce.12.cloned.1.call-start = ((), (), s32[]{:S(2)}) async-start(), calls=%async_computation.20 | async-start | bytes 4194304 | tf_op jit(solution)/shard_map/psum | solution.py:170
  392.2 216.7 %all-gather.17.cloned.1.call-start = ((), (), s32[]{:S(2)}) async-start(), calls=%async_computation.9 | async-start | bytes 12976128 | tf_op jit(solution)/shard_map/all_gather | solution.py:99
  393.8 346.6 %reduce-scatter.15.cloned.1.call-start = ((), (), s32[]{:S(2)}) async-start(), calls=%async_computation.16 | async-start | bytes 6488064 | tf_op jit(solution)/shard_map/reduce_scatter | solution.py:335
  631.4 205.0 %all-gather.19.cloned.1.call-start = ((), (), s32[]{:S(2)}) async-start(), calls=%async_computation.10 | async-start | bytes 6488064 | tf_op jit(solution)/shard_map/all_gather | solution.py:100
  744.6 172.2 %all-reduce.10.cloned.1.call-start = ((), (), s32[]{:S(2)}) async-start(), calls=%async_computation.19 | async-start | bytes 4194304 | tf_op jit(solution)/shard_map/psum | solution.py:199
  866.0 768.2 %all-reduce.8.cloned.1.call-start = ((), (), s32[]{:S(2)}) async-start(), calls=%async_computation.18 | async-start | bytes 8388608 | tf_op jit(solution)/shard_map/psum | solution.py:180
  951.1 15.8 collective-permute-start.3
  952.6 24.3 %collective-permute-start.2 = (bf16[2,64,4,512]{3,1,2,0:T(8,128)(2,1)}, bf16[2,64,4,512]{3,1,2,0:T(8,128)(2,1)S(1)}, u32[]{:S(2)}, u32[]{:S(2)}) collective-permute-start(bf16[2,64,4,512]{3,1,2,0:T(8,128)(2,1)} %copy.405), channel_id=1, source_target_pairs={{0,4},{4,8},{8,12},{12,16},{16,20},{20,24},{24,28},{1,5},{5,9},{9,... | collective-permute-start | bytes 1572872 | tf_op jit(solution)/shard_map/while/body/eval_jaxpr/ppermute | solution.py:20
  993.4 15.8 collective-permute-start.3
  994.0 24.3 %collective-permute-start.2 = (bf16[2,64,4,512]{3,1,2,0:T(8,128)(2,1)}, bf16[2,64,4,512]{3,1,2,0:T(8,128)(2,1)S(1)}, u32[]{:S(2)}, u32[]{:S(2)}) collective-permute-start(bf16[2,64,4,512]{3,1,2,0:T(8,128)(2,1)} %copy.405), channel_id=1, source_target_pairs={{0,4},{4,8},{8,12},{12,16},{16,20},{20,24},{24,28},{1,5},{5,9},{9,... | collective-permute-start | bytes 1572872 | tf_op jit(solution)/shard_map/while/body/eval_jaxpr/ppermute | solution.py:20
  1034.7 15.8 collective-permute-start.3
  1034.8 23.9 %collective-permute-start.2 = (bf16[2,64,4,512]{3,1,2,0:T(8,128)(2,1)}, bf16[2,64,4,512]{3,1,2,0:T(8,128)(2,1)S(1)}, u32[]{:S(2)}, u32[]{:S(2)}) collective-permute-start(bf16[2,64,4,512]{3,1,2,0:T(8,128)(2,1)} %copy.405), channel_id=1, source_target_pairs={{0,4},{4,8},{8,12},{12,16},{16,20},{20,24},{24,28},{1,5},{5,9},{9,... | collective-permute-start | bytes 1572872 | tf_op jit(solution)/shard_map/while/body/eval_jaxpr/ppermute | solution.py:20
  1075.2 15.8 collective-permute-start.3
  1075.3 23.0 %collective-permute-start.2 = (bf16[2,64,4,512]{3,1,2,0:T(8,128)(2,1)}, bf16[2,64,4,512]{3,1,2,0:T(8,128)(2,1)S(1)}, u32[]{:S(2)}, u32[]{:S(2)}) collective-permute-start(bf16[2,64,4,512]{3,1,2,0:T(8,128)(2,1)} %copy.405), channel_id=1, source_target_pairs={{0,4},{4,8},{8,12},{12,16},{16,20},{20,24},{24,28},{1,5},{5,9},{9,... | collective-permute-start | bytes 1572872 | tf_op jit(solution)/shard_map/while/body/eval_jaxpr/ppermute | solution.py:20
  1114.7 15.8 collective-permute-start.3
  1114.8 22.1 %collective-permute-start.2 = (bf16[2,64,4,512]{3,1,2,0:T(8,128)(2,1)}, bf16[2,64,4,512]{3,1,2,0:T(8,128)(2,1)S(1)}, u32[]{:S(2)}, u32[]{:S(2)}) collective-permute-start(bf16[2,64,4,512]{3,1,2,0:T(8,128)(2,1)} %copy.405), channel_id=1, source_target_pairs={{0,4},{4,8},{8,12},{12,16},{16,20},{20,24},{24,28},{1,5},{5,9},{9,... | collective-permute-start | bytes 1572872 | tf_op jit(solution)/shard_map/while/body/eval_jaxpr/ppermute | solution.py:20
  1139.8 25.4 %collective-permute-start.3 = (bf16[64,4,2,512]{3,0,1,2:T(8,128)(2,1)S(1)}, bf16[64,4,2,512]{3,0,1,2:T(8,128)(2,1)S(1)}, u32[]{:S(2)}, u32[]{:S(2)}) collective-permute-start(bf16[64,4,2,512]{3,0,1,2:T(8,128)(2,1)S(1)} %convert_element_type.792), channel_id=1, source_target_pairs={{0,4},{4,8},{8,12},{12,16},{16,20},{20,24},{24,28},{28,0},{1,5},{5... | collective-permute-start | bytes 1572872 | tf_op jit(solution)/shard_map/while/body/eval_jaxpr/ppermute | solution.py:26
  1153.0 17.9 collective-permute-start.2
  1173.9 22.0 %collective-permute-start.3 = (bf16[64,4,2,512]{3,0,1,2:T(8,128)(2,1)S(1)}, bf16[64,4,2,512]{3,0,1,2:T(8,128)(2,1)S(1)}, u32[]{:S(2)}, u32[]{:S(2)}) collective-permute-start(bf16[64,4,2,512]{3,0,1,2:T(8,128)(2,1)S(1)} %convert_element_type.792), channel_id=1, source_target_pairs={{0,4},{4,8},{8,12},{12,16},{16,20},{20,24},{24,28},{28,0},{1,5},{5... | collective-permute-start | bytes 1572872 | tf_op jit(solution)/shard_map/while/body/eval_jaxpr/ppermute | solution.py:26
  1177.2 25.7 %collective-permute-start.2 = (bf16[2,64,4,512]{3,1,2,0:T(8,128)(2,1)}, bf16[2,64,4,512]{3,1,2,0:T(8,128)(2,1)S(1)}, u32[]{:S(2)}, u32[]{:S(2)}) collective-permute-start(bf16[2,64,4,512]{3,1,2,0:T(8,128)(2,1)} %copy.405), channel_id=1, source_target_pairs={{0,4},{4,8},{8,12},{12,16},{16,20},{20,24},{24,28},{1,5},{5,9},{9,... | collective-permute-start | bytes 1572872 | tf_op jit(solution)/shard_map/while/body/eval_jaxpr/ppermute | solution.py:20
  1205.9 18.4 collective-permute-start.3
  1214.0 16.0 collective-permute-start.2
  1250.1 20.4 collective-permute-start.1
  1259.2 18.0 collective-permute-start
  1292.2 15.8 collective-permute-start.1
  1297.0 16.6 collective-permute-start
  1328.6 14.9 collective-permute-start.1
  1330.1 19.0 collective-permute-start
  1364.1 14.0 collective-permute-start.1
  1364.2 19.6 collective-permute-start
  1398.7 13.1 collective-permute-start.1
  1398.8 21.5 %collective-permute-start = (bf16[2,64,4,512]{3,1,2,0:T(8,128)(2,1)}, bf16[2,64,4,512]{3,1,2,0:T(8,128)(2,1)S(1)}, u32[]{:S(2)}, u32[]{:S(2)}) collective-permute-start(bf16[2,64,4,512]{3,1,2,0:T(8,128)(2,1)} %copy.417), channel_id=1, source_target_pairs={{0,4},{4,8},{8,12},{12,16},{16,20},{20,24},{24,28},{1,5},{5,9},{9,... | collective-permute-start | bytes 1572872 | tf_op jit(solution)/shard_map/while/body/eval_jaxpr/ppermute | solution.py:20
  1422.0 18.8 collective-permute-start.1
  1431.8 19.2 collective-permute-start
  1452.7 14.9 collective-permute-start.1
  1455.1 21.7 %collective-permute-start = (bf16[2,64,4,512]{3,1,2,0:T(8,128)(2,1)}, bf16[2,64,4,512]{3,1,2,0:T(8,128)(2,1)S(1)}, u32[]{:S(2)}, u32[]{:S(2)}) collective-permute-start(bf16[2,64,4,512]{3,1,2,0:T(8,128)(2,1)} %copy.417), channel_id=1, source_target_pairs={{0,4},{4,8},{8,12},{12,16},{16,20},{20,24},{24,28},{1,5},{5,9},{9,... | collective-permute-start | bytes 1572872 | tf_op jit(solution)/shard_map/while/body/eval_jaxpr/ppermute | solution.py:20
  1478.5 13.9 collective-permute-start.1
  1485.7 12.4 collective-permute-start
  1534.1 193.8 %reduce-scatter.17.cloned.1.call-start = ((), (), s32[]{:S(2)}) async-start(), calls=%async_computation.17 | async-start | bytes 589824
  1643.2 131.8 %reduce-scatter.11.cloned.1.call-start = ((), (), s32[]{:S(2)}) async-start(), calls=%async_computation.14 | async-start | bytes 2359296 | tf_op jit(solution)/shard_map/reduce_scatter | solution.py:329
  1648.2 247.8 %reduce-scatter.9.cloned.1.call-start = ((), (), s32[]{:S(2)}) async-start(), calls=%async_computation.13 | async-start | bytes 7077888 | tf_op jit(solution)/shard_map/reduce_scatter | solution.py:320
  1657.5 433.8 %reduce-scatter.13.cloned.1.call-start = ((), (), s32[]{:S(2)}) async-start(), calls=%async_computation.15 | async-start | bytes 12976128 | tf_op jit(solution)/shard_map/reduce_scatter | solution.py:332
  (185 other events, 6459.8 us)
Sparse Core Ops, SparseCore 0:
  10.8 100.0 all-gather.8
  137.5 47.7 all-gather.20
  188.0 47.7 all-gather.22
  238.4 47.7 all-gather.10
  288.8 47.7 all-gather.12
  339.1 47.7 all-gather.14
  392.3 50.6 all-reduce.11
  446.0 162.8 all-gather.16
  631.5 108.8 reduce-scatter.14
  744.7 91.7 all-gather.18
  866.1 50.6 all-reduce.9
  1534.2 99.9 all-reduce.7
  1643.3 60.9 reduce-scatter.16
  1708.3 66.6 reduce-scatter.10
  1778.4 117.5 reduce-scatter.8
  1899.5 191.7 reduce-scatter.12
where the time goes:
time: 2130 us; the launch traced here: 2120 us
  waiting for transfers between devices  1310 us (62%)
  matrix products  212 us (10%)
  local copies, waits for them, and re-layouts  176 us (8%)
  starting transfers between devices  170 us (8%)
  other arithmetic  143 us (7%)
  blocking collectives  71.3 us (3%)
    reduce_scatter x1, waiting for transfers between devices, body(): lax.psum_scatter(grad_gate.astype(jnp.bfloat16), 'seq', scatter_dimension...  189 us
    all_gather x1, waiting for transfers between devices, body(): lax.all_gather(gate_weight.astype(bf16), 'seq', axis=0, tiled=True)  161 us
    reduce_scatter x1, waiting for transfers between devices, body(): lax.psum_scatter(grad_entry.astype(jnp.bfloat16), 'seq', scatter_dimensio...  117 us
    ppermute x16, waiting for transfers between devices, passed_along(): return lax.ppermute(value, axis, pairs)  113 us
    reduce_scatter x1, waiting for transfers between devices, body(): lax.psum_scatter(grad_down.astype(jnp.bfloat16), 'seq', scatter_dimension...  109 us
    ppermute x16, waiting for transfers between devices, shifted(): return lax.ppermute(array, axis, pairs)  107 us
    all_gather x2, waiting for transfers between devices, body(): lax.all_gather(val_flat, 'seq', axis=0, tiled=True)  101 us
    psum x1, waiting for transfers between devices, body(): lax.psum(ffn_part.astype(jnp.bfloat16), 'tp').astype(jnp.float32)  95.8 us
  transfers between devices with their start and end apart: 48, of which 45 were waited for; matrix products, arithmetic and copies ran while one was open for 9% of the time, Pallas kernels for 0%

commit v1 on v0

v1 whole, which is shorter than its diff:
```python
import numpy as np

import jax
import jax.numpy as jnp
from jax import lax
from jax.sharding import PartitionSpec as P

HD = 64
ROT = 16
STEP = 10

eps = 1e-05
rates = (0.0005, 0.0002, 0.0025, 0.004, 0.0002, 6e-05)
decays = (0.0, 0.0001, 0.0, 0.0001, 0.0001, 0.0001)
bf16 = jnp.bfloat16
f32 = jnp.float32


def swap(array, axis, mask):
    pairs = [(i, i ^ mask) for i in range(lax.axis_size(axis))]
    return lax.ppermute(array, axis, pairs)


def pick(parts, flags):
    count = len(parts)
    for place, flag in enumerate(flags):
        bit = count >> (place + 1)
        parts = [jnp.where(flag, parts[j ^ bit], parts[j]) for j in range(count)]
    return parts


def joined(parts, axis=0):
    return parts[0] if len(parts) == 1 else jnp.concatenate(parts, axis)


def gather(piece, steps):
    pieces = {0: piece}
    rows = piece.shape[0]
    for axis, mask, bit in steps:
        keys = sorted(pieces)
        got = swap(joined([pieces[k] for k in keys]), axis, mask)
        for place, k in enumerate(keys):
            pieces[k | bit] = got[place * rows : (place + 1) * rows]
    return pieces


def scatter(pieces, steps):
    for axis, mask, bit in steps:
        keys = sorted(k for k in pieces if k & bit)
        got = swap(joined([pieces[k].astype(bf16) for k in keys]), axis, mask)
        rows = got.shape[0] // len(keys)
        kept = {k: v for k, v in pieces.items() if not k & bit}
        for place, k in enumerate(keys):
            kept[k ^ bit] = kept[k ^ bit].astype(f32) + got[place * rows : (place + 1) * rows].astype(f32)
        pieces = kept
    return pieces[0]


class Plan:
    def __init__(self, rows):
        self.n_seq = lax.axis_size("seq")
        self.n_tp = lax.axis_size("tp")
        self.seq = lax.axis_index("seq")
        self.tp = lax.axis_index("tp")
        bits = self.n_seq.bit_length() - 1
        self.inner = [2 << i for i in range(bits // 2)][::-1]
        self.outer = [1 << i for i in range(bits) if (1 << i) not in self.inner]
        self.groups = 1 << len(self.outer)
        self.parts = 1 << len(self.inner)
        self.rows = rows // self.groups
        self.group_flags = [(self.seq & m) != 0 for m in self.outer]
        self.part_flags = [(self.seq & m) != 0 for m in self.inner]
        self.tp_masks = [1 << i for i in range(self.n_tp.bit_length() - 1)]
        self.tp_flags = [(self.tp & m) != 0 for m in self.tp_masks[::-1]]
        self.group = self.index(self.group_flags)
        order = [("tp", m) for m in self.tp_masks] + [("seq", m) for m in self.inner]
        self.members = 1 << len(order)
        self.steps = [(axis, mask, self.members >> (i + 1)) for i, (axis, mask) in enumerate(order)]
        self.group_steps = [("seq", m, self.groups >> (i + 1)) for i, m in enumerate(self.outer)]

    def index(self, flags):
        value = jnp.int32(0)
        for flag in flags:
            value = value * 2 + flag.astype(jnp.int32)
        return value

    def outer_mask(self, j):
        return sum(m for i, m in enumerate(self.outer) if j & (self.groups >> (i + 1)))

    def inner_mask(self, j):
        return sum(m for i, m in enumerate(self.inner) if j & (self.parts >> (i + 1)))

    def member_masks(self, k):
        seq = sum(m for a, m, bit in self.steps if a == "seq" and k & bit)
        tp = sum(m for a, m, bit in self.steps if a == "tp" and k & bit)
        return seq, tp

    def arranged(self, array):
        wide = array.shape[-1] // self.n_seq
        sets = []
        for g in range(self.groups):
            places = [self.outer_mask(g) | self.inner_mask(h) for h in range(self.parts)]
            sets.append(joined([array[..., p * wide : (p + 1) * wide] for p in places], -1))
        return joined(pick(sets, self.group_flags), -1)

    def restored(self, array):
        wide = array.shape[-1] // self.groups
        sets = pick([array[..., g * wide : (g + 1) * wide] for g in range(self.groups)], self.group_flags)
        block = wide // self.parts
        blocks = [None] * self.n_seq
        for g in range(self.groups):
            for h in range(self.parts):
                blocks[self.outer_mask(g) | self.inner_mask(h)] = sets[g][..., h * block : (h + 1) * block]
        return joined(blocks, -1)

    def inputs_of_rows(self, array):
        part = array.shape[0] // self.n_tp
        own = lax.dynamic_slice_in_dim(array, self.tp * part, part, 0)
        got = []
        for j in range(self.groups):
            piece = lax.dynamic_slice_in_dim(own, (self.group ^ j) * self.rows, self.rows, 1)
            got.append(swap(piece, "seq", self.outer_mask(j)) if j else piece)
        stacked = jnp.swapaxes(jnp.concatenate(got, 0), 0, 1)
        return self.arranged(stacked.reshape(-1, array.shape[2]))

    def outputs_of_rows(self, tokens, part):
        width = tokens.shape[-1]
        table = self.restored(tokens).reshape(self.rows, self.groups, part, width)
        got = []
        for j in range(self.groups):
            piece = jnp.swapaxes(table[:, j], 0, 1)
            got.append(swap(piece, "seq", self.outer_mask(j)) if j else piece)
        own = joined(pick(got, self.group_flags), 1)
        steps = [("tp", m, m) for m in self.tp_masks[::-1]]
        pieces = gather(own, steps)
        return joined(pick([pieces[k] for k in range(self.n_tp)], self.tp_flags), 0)

    def gather_tokens(self, piece):
        half = piece.shape[0] // 2
        far = self.steps[1:]
        first = gather(piece[:half], far[::-1])
        second = gather(piece[half:], far)
        chips = 1 << len(far)
        near = joined([x for k in range(chips) for x in (first[k], second[k])])
        axis, mask, _ = self.steps[0]
        return jnp.concatenate([near, swap(near, axis, mask)], 0)

    def sum_tokens(self, product):
        total = self.total
        half = total // 2
        axis, mask, _ = self.steps[0]
        got = swap(product(half, total).astype(bf16), axis, mask)
        near = product(0, half) + got.astype(f32)
        far = self.steps[1:]
        chips = 1 << len(far)
        rows = half // chips
        first = {k: near[k * rows : k * rows + rows // 2] for k in range(chips)}
        second = {k: near[k * rows + rows // 2 : (k + 1) * rows] for k in range(chips)}
        return jnp.concatenate([scatter(first, far), scatter(second, far[::-1])], 0)

    def spread_weight(self, parts):
        mine = pick(parts, self.part_flags)
        got = [mine[0]] + [swap(mine[j], "seq", self.inner_mask(j)) for j in range(1, self.parts)]
        block = joined(pick(got, self.part_flags), 0)
        pieces = {0: block}
        for axis, mask, bit in self.group_steps[::-1]:
            for k in sorted(pieces):
                pieces[k | bit] = swap(pieces[k], axis, mask)
        return joined([pieces[k] for k in range(self.groups)], 0)

    def collect_grad(self, left, right, axis=-1):
        width = left.shape[1]
        block = width // self.groups
        half = width // 2

        def product(lo, hi):
            return jnp.einsum("td,tf->df", left[:, lo:hi], right, preferred_element_type=f32)

        axis_name, mask, _ = self.group_steps[0]
        got = swap(product(half, width).astype(bf16), axis_name, mask)
        kept = product(0, half) + got.astype(f32)
        pieces = {j: kept[j * block : (j + 1) * block] for j in range(self.groups // 2)}
        block_sum = scatter(pieces, self.group_steps[1:])
        rows = block // self.parts
        blocks = [block_sum[h * rows : (h + 1) * rows] for h in range(self.parts)]
        mine = pick(blocks, self.part_flags)
        got = [mine[0]] + [
            swap(mine[j].astype(bf16), "seq", self.inner_mask(j)).astype(f32) for j in range(1, self.parts)
        ]
        return pick(got, self.part_flags)


def layer_norm(values, gain, shift):
    center = values - jnp.mean(values, -1, keepdims=True)
    var = jnp.mean(center * center, -1, keepdims=True)
    inverse = lax.rsqrt(var + eps)
    normed = center * inverse
    return (normed * gain + shift, normed, inverse)


def norm_back(grad, normed, inverse, gain):
    scaled = grad * gain
    inner = (
        scaled
        - jnp.mean(scaled, -1, keepdims=True)
        - normed * jnp.mean(scaled * normed, -1, keepdims=True)
    )
    return inner * inverse


def turning(positions):
    half = ROT // 2
    freq = 10000.0 ** (-jnp.arange(half).astype(f32) / half)
    angle = positions.astype(f32)[:, None] * freq[None, :]
    return (jnp.cos(angle)[:, None, :], jnp.sin(angle)[:, None, :])


def rotate(values, cosine, sine):
    half = ROT // 2
    first = values[..., :half]
    second = values[..., half:ROT]
    return jnp.concatenate(
        [first * cosine - second * sine, second * cosine + first * sine, values[..., ROT:]], -1
    )


def body(
    inputs,
    cotangent,
    lengths,
    norm_params,
    entry_weight,
    entry_bias,
    output_weight,
    gate_weight,
    down_weight,
    moment_norm,
    moment_entry,
    moment_bias,
    moment_output,
    moment_gate,
    moment_down,
    average_norm,
    average_entry,
    average_bias,
    average_output,
    average_gate,
    average_down,
):
    plan = Plan(inputs.shape[1])
    groups, parts, rows = plan.groups, plan.parts, plan.rows
    block_len, _, width = inputs.shape
    tp_width = entry_weight.shape[2]
    head_width = tp_width // parts
    heads_here = head_width // HD
    hidden = gate_weight.shape[2] // parts
    quarter = block_len // plan.n_tp
    share = rows * groups * quarter
    plan.total = share * plan.members
    length = block_len * plan.n_seq

    member_seq = np.array([plan.member_masks(k)[0] for k in range(plan.members)], np.int32)
    member_tp = np.array([plan.member_masks(k)[1] for k in range(plan.members)], np.int32)
    sender = np.array([plan.outer_mask(j) for j in range(groups)], np.int32)
    seq_at = plan.seq ^ (member_seq[:, None] | sender[None, :])
    tp_at = plan.tp ^ member_tp
    position = (
        (seq_at * block_len)[:, :, None]
        + (tp_at * quarter)[:, None, None]
        + np.arange(quarter, dtype=np.int32)[None, None, :]
    )
    row_position = position.reshape(length)
    own_position = position[0].reshape(groups * quarter)
    lens = lax.dynamic_slice_in_dim(lengths, plan.group * rows, rows, 0)

    packed = jnp.concatenate([norm_params.reshape(-1), entry_bias.reshape(-1)]).astype(bf16)
    small = gather(packed[None], plan.group_steps[::-1])
    small = jnp.concatenate([small[j] for j in range(groups)], 0)[None]
    got = [small] + [swap(small, "seq", plan.inner_mask(h)) for h in range(1, parts)]
    small = jnp.stack(pick([g[0] for g in got], plan.part_flags), 1)
    n_norm = norm_params.size
    w_norm = small[:, :, :n_norm].reshape(groups, parts, 4, -1)
    gains = jnp.transpose(w_norm, (2, 0, 1, 3)).reshape(4, width).astype(f32)
    b_all = small[:, :, n_norm:].reshape((groups * parts,) + entry_bias.shape)
    b_all = pick([b_all[g * parts : (g + 1) * parts] for g in range(groups)], plan.group_flags)
    ordered = [None] * plan.n_seq
    for g in range(groups):
        for h in range(parts):
            ordered[plan.outer_mask(g) | plan.inner_mask(h)] = b_all[g][h]
    b_entry = jnp.concatenate(ordered, -1)
    part_at = plan.index(plan.part_flags)
    b_entry = lax.dynamic_slice_in_dim(b_entry, part_at * heads_here, heads_here, 1)
    entry_shift = b_entry.astype(f32).reshape(3 * head_width)

    def columns(array, h, size):
        return array[..., h * size : (h + 1) * size].astype(bf16).reshape(array.shape[0], -1)

    resid = plan.inputs_of_rows(inputs).astype(f32)
    w_attn = plan.spread_weight(
        [
            jnp.concatenate(
                [columns(entry_weight, h, head_width), columns(output_weight, h, head_width)], 1
            )
            for h in range(parts)
        ]
    )
    w_gate = plan.spread_weight([columns(gate_weight, h, hidden) for h in range(parts)])
    w_down = plan.spread_weight([columns(down_weight, h, hidden) for h in range(parts)])
    w_entry = w_attn[:, : 3 * head_width]
    w_output = w_attn[:, 3 * head_width :]

    h_first, n_first, i_first = layer_norm(resid, gains[0], gains[1])
    a_first = plan.gather_tokens(h_first.astype(bf16))
    mixed = jnp.einsum("td,df->tf", a_first, w_entry, preferred_element_type=f32) + entry_shift
    heads = mixed.reshape(plan.members, rows, groups * quarter, 3, heads_here, HD)
    heads = jnp.swapaxes(heads, 0, 1).reshape(rows, length, 3, heads_here, HD)
    cosine, sine = turning(row_position)
    query = (rotate(heads[:, :, 0], cosine, sine) * 0.125).astype(bf16)
    keys = rotate(heads[:, :, 1], cosine, sine).astype(bf16)
    vals = heads[:, :, 2].astype(bf16)
    valid = (row_position[None, :] <= row_position[:, None])[None, None] & (
        row_position[None, None, None, :] < lens[:, None, None, None]
    )
    scores = jnp.einsum("rqhd,rkhd->rhqk", query, keys, preferred_element_type=f32)
    scores = jnp.where(valid, scores, -1e30)
    top = jnp.max(scores, -1)
    weights = jnp.where(valid, jnp.exp(scores - top[..., None]), 0.0)
    total = jnp.sum(weights, -1)
    probs = weights / total[..., None]
    attended = jnp.einsum("rhqk,rkhd->rqhd", probs.astype(bf16), vals, preferred_element_type=f32)

    def by_member(array):
        wide = array.shape[2:]
        array = array.reshape((rows, plan.members, groups * quarter) + wide)
        return jnp.swapaxes(array, 0, 1).reshape(plan.total, -1)

    att_low = by_member(attended.astype(bf16))
    second = resid + plan.sum_tokens(
        lambda lo, hi: jnp.einsum("th,dh->td", att_low[lo:hi], w_output, preferred_element_type=f32)
    )
    h_second, n_second, i_second = layer_norm(second, gains[2], gains[3])
    a_second = plan.gather_tokens(h_second.astype(bf16))
    gated = jnp.einsum("td,df->tf", a_second, w_gate, preferred_element_type=f32)
    gate = gated[:, :hidden]
    upper = gated[:, hidden:]
    sigma = jax.nn.sigmoid(gate)
    active_gate = gate * sigma
    hid = (active_gate * upper).astype(bf16)
    result = second + plan.sum_tokens(
        lambda lo, hi: jnp.einsum("tf,df->td", hid[lo:hi], w_down, preferred_element_type=f32)
    )
    layer_out = plan.outputs_of_rows(result.astype(bf16), quarter)

    real = (own_position[None, :] < lens[:, None]).reshape(share, 1)
    grad_y = jnp.where(real, plan.inputs_of_rows(cotangent).astype(f32), 0.0)
    grad_y_all = plan.gather_tokens(grad_y.astype(bf16))
    grad_hidden = jnp.einsum(
        "td,df->tf", grad_y_all, w_down, preferred_element_type=f32
    ).astype(bf16)
    grad_gate_val = grad_hidden * upper * (sigma * (1.0 + gate * (1.0 - sigma)))
    grad_up_val = grad_hidden * active_gate
    grad_gated = jnp.concatenate([grad_gate_val, grad_up_val], 1).astype(bf16)
    grad_down = plan.collect_grad(grad_y_all, hid)
    grad_h2 = plan.sum_tokens(
        lambda lo, hi: jnp.einsum("tf,df->td", grad_gated[lo:hi], w_gate, preferred_element_type=f32)
    )
    grad_gate = plan.collect_grad(a_second, grad_gated)
    grad_second = grad_y + norm_back(grad_h2, n_second, i_second, gains[2])
    grad_second_all = plan.gather_tokens(grad_second.astype(bf16))
    grad_att = jnp.einsum(
        "td,dh->th", grad_second_all, w_output, preferred_element_type=f32
    ).astype(bf16)
    grad_output = plan.collect_grad(grad_second_all, att_low)
    grad_att = jnp.swapaxes(
        grad_att.reshape(plan.members, rows, groups * quarter, heads_here, HD), 0, 1
    ).reshape(rows, length, heads_here, HD)
    delta = jnp.transpose(jnp.sum(grad_att.astype(f32) * attended, -1), (0, 2, 1))
    grad_val = jnp.einsum(
        "rhqk,rqhd->rkhd", probs.astype(bf16), grad_att, preferred_element_type=f32
    )
    grad_prob = jnp.einsum("rqhd,rkhd->rhqk", grad_att, vals, preferred_element_type=f32)
    grad_score = (probs * (grad_prob - delta[..., None])).astype(bf16)
    grad_query = jnp.einsum("rhqk,rkhd->rqhd", grad_score, keys, preferred_element_type=f32)
    grad_key = jnp.einsum("rhqk,rqhd->rkhd", grad_score, query, preferred_element_type=f32)
    grad_q_raw = rotate(grad_query * 0.125, cosine, -sine)
    grad_k_raw = rotate(grad_key, cosine, -sine)
    grad_mixed = by_member(jnp.stack([grad_q_raw, grad_k_raw, grad_val], 2).astype(bf16))
    grad_h1 = plan.sum_tokens(
        lambda lo, hi: jnp.einsum("tf,df->td", grad_mixed[lo:hi], w_entry, preferred_element_type=f32)
    )
    grad_entry = plan.collect_grad(a_first, grad_mixed)
    grad_input = grad_second + norm_back(grad_h1, n_first, i_first, gains[0])
    input_grad = plan.outputs_of_rows(grad_input.astype(bf16), quarter)

    sums = jnp.stack(
        [
            jnp.sum(grad_h1 * n_first, 0),
            jnp.sum(grad_h1, 0),
            jnp.sum(grad_h2 * n_second, 0),
            jnp.sum(grad_h2, 0),
        ]
    )
    bias_sum = jnp.sum(grad_mixed.astype(f32), 0)
    for mask in plan.outer:
        bias_sum = bias_sum + swap(bias_sum, "seq", mask)
    bias_sum = bias_sum.reshape(3, heads_here, HD)
    got = [bias_sum] + [swap(bias_sum, "seq", plan.inner_mask(j)) for j in range(1, parts)]
    bias_sum = joined(pick(got, plan.part_flags), 1)
    slim = entry_bias.shape[2]
    grad_bias = lax.dynamic_slice_in_dim(bias_sum, plan.seq * slim, slim, 2)
    set_width = width // groups
    pieces = {j: sums[:, j * set_width : (j + 1) * set_width] for j in range(groups)}
    for axis, mask, bit in plan.group_steps:
        keys_sent = sorted(k for k in pieces if k & bit)
        got = swap(jnp.stack([pieces[k] for k in keys_sent]), axis, mask)
        pieces = {
            **{k: v for k, v in pieces.items() if not k & bit and k | bit not in keys_sent},
            **{k ^ bit: pieces[k ^ bit] + got[i] for i, k in enumerate(keys_sent)},
        }
    slim = set_width // parts
    mine = pick([pieces[0][:, h * slim : (h + 1) * slim] for h in range(parts)], plan.part_flags)
    grad_norm = mine[0]
    for j in range(1, parts):
        grad_norm = grad_norm + swap(mine[j], "seq", plan.inner_mask(j))
    for mask in plan.tp_masks:
        grad_norm = grad_norm + swap(grad_norm, "tp", mask)

    def whole(blocks, shape):
        middle = shape[1:-1]
        return jnp.concatenate([b.reshape((b.shape[0],) + middle + (-1,)) for b in blocks], -1)

    reduced = (
        grad_norm,
        whole(grad_entry, entry_weight.shape),
        grad_bias,
        whole(grad_output, output_weight.shape),
        whole(grad_gate, gate_weight.shape),
        whole(grad_down, down_weight.shape),
    )
    masters = (norm_params, entry_weight, entry_bias, output_weight, gate_weight, down_weight)
    moments = (moment_norm, moment_entry, moment_bias, moment_output, moment_gate, moment_down)
    averages = (
        average_norm,
        average_entry,
        average_bias,
        average_output,
        average_gate,
        average_down,
    )
    beta = min(0.999, (1 + STEP) / (10 + STEP))
    news, new_weights, smooths, copies = ([], [], [], [])
    for index in range(6):
        grad = reduced[index] + decays[index] * masters[index]
        moment = 0.9 * moments[index] + grad
        weight = masters[index] - rates[index] * (grad + 0.9 * moment)
        news.append(moment)
        new_weights.append(weight)
        smooths.append(beta * averages[index] + (1.0 - beta) * weight)
        copies.append(weight.astype(bf16))
    return (layer_out, input_grad, *news, *new_weights, *smooths, *copies)


def solution(mesh):
    in_specs = (
        P("seq", None, None),
        P("seq", None, None),
        P(),
        P(None, "seq"),
        P("seq", None, "tp"),
        P(None, "tp", "seq"),
        P("seq", "tp"),
        P("seq", None, "tp"),
        P("seq", "tp"),
        P(None, "seq"),
        P("seq", None, "tp"),
        P(None, "tp", "seq"),
        P("seq", "tp"),
        P("seq", None, "tp"),
        P("seq", "tp"),
        P(None, "seq"),
        P("seq", None, "tp"),
        P(None, "tp", "seq"),
        P("seq", "tp"),
        P("seq", None, "tp"),
        P("seq", "tp"),
    )
    out_specs = (
        P("seq", None, None),
        P("seq", None, None),
        P(None, "seq"),
        P("seq", None, "tp"),
        P(None, "tp", "seq"),
        P("seq", "tp"),
        P("seq", None, "tp"),
        P("seq", "tp"),
        P(None, "seq"),
        P("seq", None, "tp"),
        P(None, "tp", "seq"),
        P("seq", "tp"),
        P("seq", None, "tp"),
        P("seq", "tp"),
        P(None, "seq"),
        P("seq", None, "tp"),
        P(None, "tp", "seq"),
        P("seq", "tp"),
        P("seq", None, "tp"),
        P("seq", "tp"),
        P(None, "seq"),
        P("seq", None, "tp"),
        P(None, "tp", "seq"),
        P("seq", "tp"),
        P("seq", None, "tp"),
        P("seq", "tp"),
    )
    return jax.shard_map(body, mesh=mesh, in_specs=in_specs, out_specs=out_specs, check_vma=False)
```

time: 2130 us -> 853 us (0.40)
  waiting for transfers between devices: 1310 us -> 315 us
  matrix products: 212 us -> 111 us
  blocking collectives: 71.3 us -> 0 us
  starting transfers between devices: 170 us -> 117 us
  other arithmetic: 143 us -> 98.5 us
  local copies, waits for them, and re-layouts: 176 us -> 198 us
    reduce_scatter x4 -> x0, waiting for transfers between devices: 460 us -> none  [the longest x1 189 us: body(): lax.psum_scatter(grad_gate.astype(jnp.bfloat16), 'seq', scatter_dimension...]
    all_gather x8 -> x0, waiting for transfers between devices: 452 us -> none  [the longest x1 161 us: body(): lax.all_gather(gate_weight.astype(bf16), 'seq', axis=0, tiled=True)]
    psum x3 -> x0, waiting for transfers between devices: 178 us -> none  [the longest x1 95.8 us: body(): lax.psum(ffn_part.astype(jnp.bfloat16), 'tp').astype(jnp.float32)]
    dot_general x78 -> x25, matrix products: 212 us -> 105 us  [the longest x8 34.2 us: product(): jnp.einsum('td,tf->df', left[:, lo:hi], right, preferred_element_type=f32)]
    ppermute x32 -> x91, waiting for transfers between devices: 220 us -> 315 us  [swap(): return lax.ppermute(array, axis, pairs)]
    all_gather x2 -> x0, blocking collectives: 55 us -> none  [the longest x1 28.5 us: body(): lax.all_gather(norm_params.astype(bf16), 'seq', axis=1, tiled=True)]
    unnamed x306 -> x366, local copies, waits for them, and re-layouts: 39.8 us -> 93.7 us
    ppermute x32 -> x91, starting transfers between devices: 157 us -> 117 us  [swap(): return lax.ppermute(array, axis, pairs)]
  transfers between devices with their start and end apart: 48 -> 91, of which waited for: 45 -> 39; matrix products, arithmetic and copies ran while one was open for 9% -> 45% of each run, Pallas kernels for 0% -> 0%
where the time goes in v1:
time: 853 us; the launch traced here: 843 us
  waiting for transfers between devices  315 us (37%)
  local copies, waits for them, and re-layouts  198 us (23%)
  starting transfers between devices  117 us (14%)
  matrix products  111 us (13%)
  other arithmetic  98.5 us (12%)
    ppermute x91, waiting for transfers between devices, swap(): return lax.ppermute(array, axis, pairs)  315 us
    ppermute x91, starting transfers between devices, swap(): return lax.ppermute(array, axis, pairs)  117 us
    unnamed x366, local copies, waits for them, and re-layouts  93.7 us
    dot_general x8, matrix products, product(): jnp.einsum('td,tf->df', left[:, lo:hi], right, preferred_element_type=f32)  34.2 us
  transfers between devices with their start and end apart: 91, of which 39 were waited for; matrix products, arithmetic and copies ran while one was open for 45% of the time, Pallas kernels for 0%

profile of v1, /device:TPU:16, one launch (start us, length us, event | category | flops | bytes accessed | tf_op | source)
XLA Modules:
  0.0 842.9 jit_solution(966479295942969766)
XLA Ops:
  18.5 4.3 copy.277
  98.1 4.9 collective-permute-done.29
  109.5 4.2 collective-permute-done.6
  131.6 19.9 %collective-permute-done.8 = bf16[128,2048]{1,0:T(8,128)(2,1)S(1)} collective-permute-done((bf16[128,2048]{1,0:T(8,128)(2,1)S(1)}, bf16[128,2048]{1,0:T(8,128)(2,1)S(1)}, u32[]{:S(2)}, u32[]{:S(2)}) %collective-permute-start.8) | collective-permute-done | bytes 524320 | tf_op jit(solution)/shard_map/ppermute | solution.py:21
  151.9 7.3 collective-permute-done.48
  161.1 39.2 %collective-permute-done.12 = bf16[512,1024]{0,1:T(8,128)(2,1)S(1)} collective-permute-done((bf16[512,1024]{0,1:T(8,128)(2,1)S(1)}, bf16[512,1024]{0,1:T(8,128)(2,1)S(1)}, u32[]{:S(2)}, u32[]{:S(2)}) %collective-permute-start.12) | collective-permute-done | bytes 1048608 | tf_op jit(solution)/shard_map/ppermute | solution.py:21
  206.7 8.8 %collective-permute-done.14 = bf16[512,1024]{0,1:T(8,128)(2,1)S(1)} collective-permute-done((bf16[512,1024]{0,1:T(8,128)(2,1)S(1)}, bf16[512,1024]{0,1:T(8,128)(2,1)S(1)}, u32[]{:S(2)}, u32[]{:S(2)}) %collective-permute-start.14) | collective-permute-done | bytes 1048608 | tf_op jit(solution)/shard_map/ppermute | solution.py:21
  219.7 5.1 fusion.31
  224.8 6.5 reshape.628
  231.3 7.6 copy.274
  239.0 6.3 reshape.629
  247.3 5.8 fusion.156
  253.2 4.6 fusion.6
  284.2 9.0 %collective-permute-done.16 = bf16[128,2048]{1,0:T(8,128)(2,1)S(1)} collective-permute-done((bf16[128,2048]{1,0:T(8,128)(2,1)S(1)}, bf16[128,2048]{1,0:T(8,128)(2,1)S(1)}, u32[]{:S(2)}, u32[]{:S(2)}) %collective-permute-start.16) | collective-permute-done | bytes 524320 | tf_op jit(solution)/shard_map/ppermute | solution.py:21
  313.3 19.5 %collective-permute-done.27 = bf16[512,1408]{1,0:T(8,128)(2,1)S(1)} collective-permute-done((bf16[512,1408]{1,0:T(8,128)(2,1)}, bf16[512,1408]{1,0:T(8,128)(2,1)S(1)}, u32[]{:S(2)}, u32[]{:S(2)}) %collective-permute-start.27) | collective-permute-done | bytes 1441824 | tf_op jit(solution)/shard_map/ppermute | solution.py:21
  335.3 7.1 collective-permute-done.20
  344.1 6.7 collective-permute-done.22
  352.1 10.0 %collective-permute-done.28 = bf16[512,1408]{1,0:T(8,128)(2,1)S(1)} collective-permute-done((bf16[512,1408]{1,0:T(8,128)(2,1)}, bf16[512,1408]{1,0:T(8,128)(2,1)S(1)}, u32[]{:S(2)}, u32[]{:S(2)}) %collective-permute-start.28) | collective-permute-done | bytes 1441824 | tf_op jit(solution)/shard_map/ppermute | solution.py:21
  362.6 8.5 %fusion.166 = f32[1024,1408]{1,0:T(8,128)} fusion(bf16[1024,2048]{1,0:T(8,128)(2,1)S(1)} %constant_dynamic-update-slice_fusion.17, bf16[2048,1408]{1,0:T(8,128)(2,1)S(1)} %constant_dynamic-update-slice_fusion.21), kind=kOutput, calls=%fused_computation.543 | convolution fusion | flops 5905580032 | bytes 15728640 | tf_op jit(solution)/shard_map/td,df->tf/dot_general | solution.py:343
  371.1 6.4 fusion.9
  377.5 4.8 convolution_convert_fusion.4
  387.8 5.6 copy.309
  398.3 5.6 copy.319
  408.2 4.0 convolution_convert_fusion.3
  412.5 7.1 convolution_convert_fusion
  426.8 6.7 fusion.163
  440.7 16.9 %collective-permute-done.89 = bf16[512,704]{0,1:T(8,128)(2,1)S(1)} collective-permute-done((bf16[512,704]{0,1:T(8,128)(2,1)S(1)}, bf16[512,704]{0,1:T(8,128)(2,1)S(1)}, u32[]{:S(2)}, u32[]{:S(2)}) %collective-permute-start.89) | collective-permute-done | bytes 720928 | tf_op jit(solution)/shard_map/ppermute | solution.py:21
  463.8 7.1 collective-permute-done.90
  489.4 7.0 convert_add_fusion
  502.8 5.3 collective-permute-done.55
  518.6 4.4 collective-permute-done.57
  529.5 8.3 collective-permute-done.56
  539.3 9.6 %collective-permute-done.58 = bf16[128,2048]{1,0:T(8,128)(2,1)S(1)} collective-permute-done((bf16[128,2048]{1,0:T(8,128)(2,1)S(1)}, bf16[128,2048]{1,0:T(8,128)(2,1)S(1)}, u32[]{:S(2)}, u32[]{:S(2)}) %collective-permute-start.58) | collective-permute-done | bytes 524320 | tf_op jit(solution)/shard_map/ppermute | solution.py:21
  552.6 12.3 %collective-permute-done.86 = bf16[512,1408]{1,0:T(8,128)(2,1)S(1)} collective-permute-done((bf16[512,1408]{1,0:T(8,128)(2,1)S(1)}, bf16[512,1408]{1,0:T(8,128)(2,1)S(1)}, u32[]{:S(2)}, u32[]{:S(2)}) %collective-permute-start.86) | collective-permute-done | bytes 1441824 | tf_op jit(solution)/shard_map/ppermute | solution.py:21
  568.8 15.6 %collective-permute-done.87 = bf16[256,1408]{1,0:T(8,128)(2,1)S(1)} collective-permute-done((bf16[256,1408]{1,0:T(8,128)(2,1)S(1)}, bf16[256,1408]{1,0:T(8,128)(2,1)S(1)}, u32[]{:S(2)}, u32[]{:S(2)}) %collective-permute-start.87) | collective-permute-done | bytes 720928 | tf_op jit(solution)/shard_map/ppermute | solution.py:21
  592.1 6.5 fusion.120
  598.7 5.7 copy.322
  611.6 5.6 copy.328
  629.2 4.4 fusion.59
  633.9 4.7 multiply_convert_fusion
  650.6 5.6 convert_reduce_fusion
  677.8 5.0 fusion.34
  691.2 10.2 %collective-permute-done.83 = bf16[512,256]{0,1:T(8,128)(2,1)S(1)} collective-permute-done((bf16[512,256]{0,1:T(8,128)(2,1)S(1)}, bf16[512,256]{0,1:T(8,128)(2,1)S(1)}, u32[]{:S(2)}, u32[]{:S(2)}) %collective-permute-start.83) | collective-permute-done | bytes 262176 | tf_op jit(solution)/shard_map/ppermute | solution.py:21
  708.8 12.1 %collective-permute-done.76 = bf16[1024,768]{0,1:T(8,128)(2,1)} collective-permute-done((bf16[1024,768]{0,1:T(8,128)(2,1)}, bf16[1024,768]{0,1:T(8,128)(2,1)}, u32[]{:S(2)}, u32[]{:S(2)}) %collective-permute-start.76) | collective-permute-done | bytes 1572896 | tf_op jit(solution)/shard_map/ppermute | solution.py:21
  732.3 26.2 %collective-permute-done.77 = bf16[512,768]{0,1:T(8,128)(2,1)S(1)} collective-permute-done((bf16[512,768]{0,1:T(8,128)(2,1)S(1)}, bf16[512,768]{0,1:T(8,128)(2,1)S(1)}, u32[]{:S(2)}, u32[]{:S(2)}) %collective-permute-start.77) | collective-permute-done | bytes 786464 | tf_op jit(solution)/shard_map/ppermute | solution.py:21
  768.3 7.4 collective-permute-done.63
  813.5 6.1 collective-permute-done.41
  825.5 9.8 %collective-permute-done.69 = bf16[16,8,2048]{2,1,0:T(8,128)(2,1)S(1)} collective-permute-done((bf16[16,8,2048]{2,1,0:T(8,128)(2,1)S(1)}, bf16[16,8,2048]{2,1,0:T(8,128)(2,1)S(1)}, u32[]{:S(2)}, u32[]{:S(2)}) %collective-permute-start.69) | collective-permute-done | bytes 524320 | tf_op jit(solution)/shard_map/ppermute | solution.py:21
  (763 shorter events, 417.5 us)
Async XLA Ops:
  2.3 29.5 %collective-permute-start.3 = (bf16[1,1216]{1,0:T(2,128)(2,1)S(1)}, bf16[1,1216]{1,0:T(2,128)(2,1)}, u32[]{:S(2)}, u32[]{:S(2)}) collective-permute-start(bf16[1,1216]{1,0:T(2,128)(2,1)S(1)} %constant_dynamic-update-slice_fusion), channel_id=1, source_target_pairs={{0,16},{4,20},{8,24},{12,28},{16,0},{20,4},{24,8},{28,12},{1,17},{... | collective-permute-start | bytes 7304 | tf_op jit(solution)/shard_map/ppermute | solution.py:21
  6.2 75.0 %collective-permute-start.2 = (bf16[16,2,2048]{2,0,1:T(8,128)(2,1)}, bf16[16,2,2048]{2,0,1:T(8,128)(2,1)}, u32[]{:S(2)}, u32[]{:S(2)}) collective-permute-start(bf16[16,2,2048]{2,0,1:T(8,128)(2,1)} %copy.345), channel_id=1, source_target_pairs={{0,20},{4,16},{8,28},{12,24},{16,4},{20,0},{24,12},{28,8},{1,21},{... | collective-permute-start | bytes 393224 | tf_op jit(solution)/shard_map/ppermute | solution.py:21
  10.7 73.2 %collective-permute-start.1 = (bf16[16,2,2048]{2,0,1:T(8,128)(2,1)}, bf16[16,2,2048]{2,0,1:T(8,128)(2,1)}, u32[]{:S(2)}, u32[]{:S(2)}) collective-permute-start(bf16[16,2,2048]{2,0,1:T(8,128)(2,1)} %copy.344), channel_id=1, source_target_pairs={{0,4},{4,0},{8,12},{12,8},{16,20},{20,16},{24,28},{28,24},{1,5},{5... | collective-permute-start | bytes 393224 | tf_op jit(solution)/shard_map/ppermute | solution.py:21
  11.9 73.4 %collective-permute-start = (bf16[16,2,2048]{2,0,1:T(8,128)(2,1)}, bf16[16,2,2048]{2,0,1:T(8,128)(2,1)}, u32[]{:S(2)}, u32[]{:S(2)}) collective-permute-start(bf16[16,2,2048]{2,0,1:T(8,128)(2,1)} %copy.343), channel_id=1, source_target_pairs={{0,16},{4,20},{8,24},{12,28},{16,0},{20,4},{24,8},{28,12},{1,17},{... | collective-permute-start | bytes 393224 | tf_op jit(solution)/shard_map/ppermute | solution.py:21
  15.4 107.5 %collective-permute-start.11 = (bf16[256,1024]{0,1:T(8,128)(2,1)}, bf16[256,1024]{0,1:T(8,128)(2,1)}, u32[]{:S(2)}, u32[]{:S(2)}) collective-permute-start(bf16[256,1024]{0,1:T(8,128)(2,1)} %broadcast_select_fusion.7), channel_id=1, source_target_pairs={{0,8},{4,12},{8,0},{12,4},{16,24},{20,28},{24,16},{28,20},{1,9},{5... | collective-permute-start | bytes 1572872 | tf_op jit(solution)/shard_map/ppermute | solution.py:21
  52.9 74.0 %collective-permute-start.25 = (bf16[256,1408]{1,0:T(8,128)(2,1)}, bf16[256,1408]{1,0:T(8,128)(2,1)}, u32[]{:S(2)}, u32[]{:S(2)}) collective-permute-start(bf16[256,1408]{1,0:T(8,128)(2,1)} %copy.278), channel_id=1, source_target_pairs={{0,8},{4,12},{8,0},{12,4},{16,24},{20,28},{24,16},{28,20},{1,9},{5... | collective-permute-start | bytes 2162696 | tf_op jit(solution)/shard_map/ppermute | solution.py:21
  94.1 19.7 %collective-permute-start.6 = (bf16[64,2048]{1,0:T(8,128)(2,1)S(1)}, bf16[64,2048]{1,0:T(8,128)(2,1)S(1)}, u32[]{:S(2)}, u32[]{:S(2)}) collective-permute-start(bf16[64,2048]{1,0:T(8,128)(2,1)S(1)} %get-tuple-element.345), channel_id=1, source_target_pairs={{0,8},{4,12},{8,0},{12,4},{16,24},{20,28},{24,16},{28,20},{1,9},{5... | collective-permute-start | bytes 786440 | tf_op jit(solution)/shard_map/ppermute | solution.py:21
  103.0 17.2 %collective-permute-start.46 = (bf16[64,2048]{1,0:T(8,128)(2,1)S(1)}, bf16[64,2048]{1,0:T(8,128)(2,1)S(1)}, u32[]{:S(2)}, u32[]{:S(2)}) collective-permute-start(bf16[64,2048]{1,0:T(8,128)(2,1)S(1)} %get-tuple-element.313), channel_id=1, source_target_pairs={{0,8},{4,12},{8,0},{12,4},{16,24},{20,28},{24,16},{28,20},{1,9},{5... | collective-permute-start | bytes 786440 | tf_op jit(solution)/shard_map/ppermute | solution.py:21
  113.7 166.6 %collective-permute-start.30 = (bf16[512,704]{0,1:T(8,128)(2,1)}, bf16[512,704]{0,1:T(8,128)(2,1)}, u32[]{:S(2)}, u32[]{:S(2)}) collective-permute-start(bf16[512,704]{0,1:T(8,128)(2,1)} %pad_maximum_fusion.11), channel_id=1, source_target_pairs={{0,16},{4,20},{8,24},{12,28},{16,0},{20,4},{24,8},{28,12},{1,17},{... | collective-permute-start | bytes 2162696 | tf_op jit(solution)/shard_map/ppermute | solution.py:21
  116.9 34.6 %collective-permute-start.8 = (bf16[128,2048]{1,0:T(8,128)(2,1)S(1)}, bf16[128,2048]{1,0:T(8,128)(2,1)S(1)}, u32[]{:S(2)}, u32[]{:S(2)}) collective-permute-start(bf16[128,2048]{1,0:T(8,128)(2,1)S(1)} %pad_maximum_fusion.14), channel_id=1, source_target_pairs={{0,8},{4,12},{8,0},{12,4},{16,24},{20,28},{24,16},{28,20},{1,9},{5... | collective-permute-start | bytes 1572872 | tf_op jit(solution)/shard_map/ppermute | solution.py:21
  120.2 31.4 %collective-permute-start.9 = (bf16[128,2048]{1,0:T(8,128)(2,1)S(1)}, bf16[128,2048]{1,0:T(8,128)(2,1)S(1)}, u32[]{:S(2)}, u32[]{:S(2)}) collective-permute-start(bf16[128,2048]{1,0:T(8,128)(2,1)S(1)} %pad_maximum_fusion.15), channel_id=1, source_target_pairs={{0,2},{1,3},{2,0},{3,1},{4,6},{5,7},{6,4},{7,5},{8,10},{9,11},{10,... | collective-permute-start | bytes 1572872 | tf_op jit(solution)/shard_map/ppermute | solution.py:21
  122.8 36.3 %collective-permute-start.48 = (bf16[128,2048]{1,0:T(8,128)(2,1)S(1)}, bf16[128,2048]{1,0:T(8,128)(2,1)S(1)}, u32[]{:S(2)}, u32[]{:S(2)}) collective-permute-start(bf16[128,2048]{1,0:T(8,128)(2,1)S(1)} %pad_maximum_fusion.28), channel_id=1, source_target_pairs={{0,8},{4,12},{8,0},{12,4},{16,24},{20,28},{24,16},{28,20},{1,9},{5... | collective-permute-start | bytes 1572872 | tf_op jit(solution)/shard_map/ppermute | solution.py:21
  126.9 75.8 %collective-permute-start.49 = (bf16[128,2048]{1,0:T(8,128)(2,1)S(1)}, bf16[128,2048]{1,0:T(8,128)(2,1)S(1)}, u32[]{:S(2)}, u32[]{:S(2)}) collective-permute-start(bf16[128,2048]{1,0:T(8,128)(2,1)S(1)} %pad_maximum_fusion.29), channel_id=1, source_target_pairs={{0,2},{1,3},{2,0},{3,1},{4,6},{5,7},{6,4},{7,5},{8,10},{9,11},{10,... | collective-permute-start | bytes 1572872 | tf_op jit(solution)/shard_map/ppermute | solution.py:21
  151.6 48.7 %collective-permute-start.12 = (bf16[512,1024]{0,1:T(8,128)(2,1)S(1)}, bf16[512,1024]{0,1:T(8,128)(2,1)S(1)}, u32[]{:S(2)}, u32[]{:S(2)}) collective-permute-start(bf16[512,1024]{0,1:T(8,128)(2,1)S(1)} %pad_maximum_fusion.6), channel_id=1, source_target_pairs={{0,16},{4,20},{8,24},{12,28},{16,0},{20,4},{24,8},{28,12},{1,17},{... | collective-permute-start | bytes 3145736 | tf_op jit(solution)/shard_map/ppermute | solution.py:21
  151.7 64.0 %collective-permute-start.10 = (bf16[512,2048]{1,0:T(8,128)(2,1)S(1)}, bf16[512,2048]{1,0:T(8,128)(2,1)S(1)}, u32[]{:S(2)}, u32[]{:S(2)}) collective-permute-start(bf16[512,2048]{1,0:T(8,128)(2,1)S(1)} %get-tuple-element.342), channel_id=1, source_target_pairs={{0,1},{1,0},{2,3},{3,2},{4,5},{5,4},{6,7},{7,6},{8,9},{9,8},{10,11... | collective-permute-start | bytes 6291464 | tf_op jit(solution)/shard_map/ppermute | solution.py:21
  159.2 43.9 %collective-permute-start.13 = (bf16[512,1024]{0,1:T(8,128)(2,1)S(1)}, bf16[512,1024]{0,1:T(8,128)(2,1)S(1)}, u32[]{:S(2)}, u32[]{:S(2)}) collective-permute-start(bf16[512,1024]{0,1:T(8,128)(2,1)S(1)} %pad_maximum_fusion.6), channel_id=1, source_target_pairs={{0,4},{4,0},{8,12},{12,8},{16,20},{20,16},{24,28},{28,24},{1,5},{5... | collective-permute-start | bytes 3145736 | tf_op jit(solution)/shard_map/ppermute | solution.py:21
  202.8 95.2 %collective-permute-start.31 = (bf16[512,704]{0,1:T(8,128)(2,1)}, bf16[512,704]{0,1:T(8,128)(2,1)}, u32[]{:S(2)}, u32[]{:S(2)}) collective-permute-start(bf16[512,704]{0,1:T(8,128)(2,1)} %pad_maximum_fusion.11), channel_id=1, source_target_pairs={{0,4},{4,0},{8,12},{12,8},{16,20},{20,16},{24,28},{28,24},{1,5},{5... | collective-permute-start | bytes 2162696 | tf_op jit(solution)/shard_map/ppermute | solution.py:21
  203.0 96.4 %collective-permute-start.26 = (bf16[512,1408]{1,0:T(8,128)(2,1)}, bf16[512,1408]{1,0:T(8,128)(2,1)}, u32[]{:S(2)}, u32[]{:S(2)}) collective-permute-start(bf16[512,1408]{1,0:T(8,128)(2,1)} %pad_maximum_fusion.5), channel_id=1, source_target_pairs={{0,16},{4,20},{8,24},{12,28},{16,0},{20,4},{24,8},{28,12},{1,17},{... | collective-permute-start | bytes 4325384 | tf_op jit(solution)/shard_map/ppermute | solution.py:21
  280.4 18.9 %collective-permute-start.32 = (bf16[512,704]{0,1:T(8,128)(2,1)}, bf16[512,704]{0,1:T(8,128)(2,1)S(1)}, u32[]{:S(2)}, u32[]{:S(2)}) collective-permute-start(bf16[512,704]{0,1:T(8,128)(2,1)} %collective-permute-done.30), channel_id=1, source_target_pairs={{0,4},{4,0},{8,12},{12,8},{16,20},{20,16},{24,28},{28,24},{1,5},{5... | collective-permute-start | bytes 2162696 | tf_op jit(solution)/shard_map/ppermute | solution.py:21
  282.3 19.2 %collective-permute-start.18 = (bf16[128,2048]{1,0:T(8,128)(2,1)S(1)}, bf16[128,2048]{1,0:T(8,128)(2,1)S(1)}, u32[]{:S(2)}, u32[]{:S(2)}) collective-permute-start(bf16[128,2048]{1,0:T(8,128)(2,1)S(1)} %pad_maximum_fusion.20), channel_id=1, source_target_pairs={{0,8},{4,12},{8,0},{12,4},{16,24},{20,28},{24,16},{28,20},{1,9},{5... | collective-permute-start | bytes 1572872 | tf_op jit(solution)/shard_map/ppermute | solution.py:21
  298.0 34.8 %collective-permute-start.27 = (bf16[512,1408]{1,0:T(8,128)(2,1)}, bf16[512,1408]{1,0:T(8,128)(2,1)S(1)}, u32[]{:S(2)}, u32[]{:S(2)}) collective-permute-start(bf16[512,1408]{1,0:T(8,128)(2,1)} %pad_maximum_fusion.5), channel_id=1, source_target_pairs={{0,4},{4,0},{8,12},{12,8},{16,20},{20,16},{24,28},{28,24},{1,5},{5... | collective-permute-start | bytes 4325384 | tf_op jit(solution)/shard_map/ppermute | solution.py:21
  299.3 52.5 %collective-permute-start.50 = (bf16[512,2048]{1,0:T(8,128)(2,1)S(1)}, bf16[512,2048]{1,0:T(8,128)(2,1)S(1)}, u32[]{:S(2)}, u32[]{:S(2)}) collective-permute-start(bf16[512,2048]{1,0:T(8,128)(2,1)S(1)} %copy-done.90), channel_id=1, source_target_pairs={{0,1},{1,0},{2,3},{3,2},{4,5},{5,4},{6,7},{7,6},{8,9},{9,8},{10,11... | collective-permute-start | bytes 6291464 | tf_op jit(solution)/shard_map/ppermute | solution.py:21
  299.5 62.6 %collective-permute-start.28 = (bf16[512,1408]{1,0:T(8,128)(2,1)}, bf16[512,1408]{1,0:T(8,128)(2,1)S(1)}, u32[]{:S(2)}, u32[]{:S(2)}) collective-permute-start(bf16[512,1408]{1,0:T(8,128)(2,1)} %collective-permute-done.26), channel_id=1, source_target_pairs={{0,4},{4,0},{8,12},{12,8},{16,20},{20,16},{24,28},{28,24},{1,5},{5... | collective-permute-start | bytes 4325384 | tf_op jit(solution)/shard_map/ppermute | solution.py:21
  311.6 22.9 %collective-permute-start.21 = (bf16[64,2048]{1,0:T(8,128)(2,1)S(1)}, bf16[64,2048]{1,0:T(8,128)(2,1)S(1)}, u32[]{:S(2)}, u32[]{:S(2)}) collective-permute-start(bf16[64,2048]{1,0:T(8,128)(2,1)S(1)} %get-tuple-element.340), channel_id=1, source_target_pairs={{0,2},{1,3},{2,0},{3,1},{4,6},{5,7},{6,4},{7,5},{8,10},{9,11},{10,... | collective-permute-start | bytes 786440 | tf_op jit(solution)/shard_map/ppermute | solution.py:21
  382.3 44.4 %collective-permute-start.51 = (bf16[512,2048]{1,0:T(8,128)(2,1)}, bf16[512,2048]{1,0:T(8,128)(2,1)}, u32[]{:S(2)}, u32[]{:S(2)}) collective-permute-start(bf16[512,2048]{1,0:T(8,128)(2,1)} %convolution_convert_fusion.4), channel_id=1, source_target_pairs={{0,1},{1,0},{2,3},{3,2},{4,5},{5,4},{6,7},{7,6},{8,9},{9,8},{10,11... | collective-permute-start | bytes 6291464 | tf_op jit(solution)/shard_map/ppermute | solution.py:21
  385.3 36.0 %collective-permute-start.88 = (bf16[1024,704]{0,1:T(8,128)(2,1)}, bf16[1024,704]{0,1:T(8,128)(2,1)}, u32[]{:S(2)}, u32[]{:S(2)}) collective-permute-start(bf16[1024,704]{0,1:T(8,128)(2,1)} %fusion.39), channel_id=1, source_target_pairs={{0,4},{4,0},{8,12},{12,8},{16,20},{20,16},{24,28},{28,24},{1,5},{5... | collective-permute-start | bytes 4325384 | tf_op jit(solution)/shard_map/ppermute | solution.py:21
  412.3 24.5 %collective-permute-start.33 = (bf16[512,2048]{1,0:T(8,128)(2,1)S(1)}, bf16[512,2048]{1,0:T(8,128)(2,1)S(1)}, u32[]{:S(2)}, u32[]{:S(2)}) collective-permute-start(bf16[512,2048]{1,0:T(8,128)(2,1)S(1)} %convolution_convert_fusion.3), channel_id=1, source_target_pairs={{0,1},{1,0},{2,3},{3,2},{4,5},{5,4},{6,7},{7,6},{8,9},{9,8},{10,11... | collective-permute-start | bytes 6291464 | tf_op jit(solution)/shard_map/ppermute | solution.py:21
  419.7 69.7 %collective-permute-start.85 = (bf16[1024,1408]{1,0:T(8,128)(2,1)}, bf16[1024,1408]{1,0:T(8,128)(2,1)}, u32[]{:S(2)}, u32[]{:S(2)}) collective-permute-start(bf16[1024,1408]{1,0:T(8,128)(2,1)} %convolution_convert_fusion), channel_id=1, source_target_pairs={{0,4},{4,0},{8,12},{12,8},{16,20},{20,16},{24,28},{28,24},{1,5},{5... | collective-permute-start | bytes 8650760 | tf_op jit(solution)/shard_map/ppermute | solution.py:21
  424.5 33.2 %collective-permute-start.89 = (bf16[512,704]{0,1:T(8,128)(2,1)S(1)}, bf16[512,704]{0,1:T(8,128)(2,1)S(1)}, u32[]{:S(2)}, u32[]{:S(2)}) collective-permute-start(bf16[512,704]{0,1:T(8,128)(2,1)S(1)} %slice.1586), channel_id=1, source_target_pairs={{0,16},{4,20},{8,24},{12,28},{16,0},{20,4},{24,8},{28,12},{1,17},{... | collective-permute-start | bytes 2162696 | tf_op jit(solution)/shard_map/ppermute | solution.py:21
  434.4 50.4 %collective-permute-start.52 = (bf16[128,2048]{1,0:T(8,128)(2,1)}, bf16[128,2048]{1,0:T(8,128)(2,1)}, u32[]{:S(2)}, u32[]{:S(2)}) collective-permute-start(bf16[128,2048]{1,0:T(8,128)(2,1)} %pad_maximum_fusion.30), channel_id=1, source_target_pairs={{0,2},{1,3},{2,0},{3,1},{4,6},{5,7},{6,4},{7,5},{8,10},{9,11},{10,... | collective-permute-start | bytes 1572872 | tf_op jit(solution)/shard_map/ppermute | solution.py:21
  436.1 61.6 %collective-permute-start.54 = (bf16[128,2048]{1,0:T(8,128)(2,1)}, bf16[128,2048]{1,0:T(8,128)(2,1)}, u32[]{:S(2)}, u32[]{:S(2)}) collective-permute-start(bf16[128,2048]{1,0:T(8,128)(2,1)} %pad_maximum_fusion.31), channel_id=1, source_target_pairs={{0,8},{4,12},{8,0},{12,4},{16,24},{20,28},{24,16},{28,20},{1,9},{5... | collective-permute-start | bytes 1572872 | tf_op jit(solution)/shard_map/ppermute | solution.py:21
  461.8 24.3 %collective-permute-start.34 = (bf16[128,2048]{1,0:T(8,128)(2,1)}, bf16[128,2048]{1,0:T(8,128)(2,1)}, u32[]{:S(2)}, u32[]{:S(2)}) collective-permute-start(bf16[128,2048]{1,0:T(8,128)(2,1)} %pad_maximum_fusion.23), channel_id=1, source_target_pairs={{0,2},{1,3},{2,0},{3,1},{4,6},{5,7},{6,4},{7,5},{8,10},{9,11},{10,... | collective-permute-start | bytes 1572872 | tf_op jit(solution)/shard_map/ppermute | solution.py:21
  470.9 29.1 %collective-permute-start.36 = (bf16[128,2048]{1,0:T(8,128)(2,1)}, bf16[128,2048]{1,0:T(8,128)(2,1)}, u32[]{:S(2)}, u32[]{:S(2)}) collective-permute-start(bf16[128,2048]{1,0:T(8,128)(2,1)} %pad_maximum_fusion.24), channel_id=1, source_target_pairs={{0,8},{4,12},{8,0},{12,4},{16,24},{20,28},{24,16},{28,20},{1,9},{5... | collective-permute-start | bytes 1572872 | tf_op jit(solution)/shard_map/ppermute | solution.py:21
  496.6 68.4 %collective-permute-start.86 = (bf16[512,1408]{1,0:T(8,128)(2,1)S(1)}, bf16[512,1408]{1,0:T(8,128)(2,1)S(1)}, u32[]{:S(2)}, u32[]{:S(2)}) collective-permute-start(bf16[512,1408]{1,0:T(8,128)(2,1)S(1)} %slice.1584), channel_id=1, source_target_pairs={{0,16},{4,20},{8,24},{12,28},{16,0},{20,4},{24,8},{28,12},{1,17},{... | collective-permute-start | bytes 4325384 | tf_op jit(solution)/shard_map/ppermute | solution.py:21
  514.8 22.9 %collective-permute-start.56 = (bf16[64,2048]{1,0:T(8,128)(2,1)S(1)}, bf16[64,2048]{1,0:T(8,128)(2,1)S(1)}, u32[]{:S(2)}, u32[]{:S(2)}) collective-permute-start(bf16[64,2048]{1,0:T(8,128)(2,1)S(1)} %get-tuple-element.309), channel_id=1, source_target_pairs={{0,8},{4,12},{8,0},{12,4},{16,24},{20,28},{24,16},{28,20},{1,9},{5... | collective-permute-start | bytes 786440 | tf_op jit(solution)/shard_map/ppermute | solution.py:21
  523.0 25.9 %collective-permute-start.58 = (bf16[128,2048]{1,0:T(8,128)(2,1)S(1)}, bf16[128,2048]{1,0:T(8,128)(2,1)S(1)}, u32[]{:S(2)}, u32[]{:S(2)}) collective-permute-start(bf16[128,2048]{1,0:T(8,128)(2,1)S(1)} %pad_maximum_fusion.32), channel_id=1, source_target_pairs={{0,8},{4,12},{8,0},{12,4},{16,24},{20,28},{24,16},{28,20},{1,9},{5... | collective-permute-start | bytes 1572872 | tf_op jit(solution)/shard_map/ppermute | solution.py:21
  524.2 276.9 %collective-permute-start.39 = (bf16[16,2,2048]{2,1,0:T(2,128)(2,1)}, bf16[16,2,2048]{2,1,0:T(2,128)(2,1)}, u32[]{:S(2)}, u32[]{:S(2)}) collective-permute-start(bf16[16,2,2048]{2,1,0:T(2,128)(2,1)} %bitcast.195), channel_id=1, source_target_pairs={{0,16},{4,20},{8,24},{12,28},{16,0},{20,4},{24,8},{28,12},{1,17},{... | collective-permute-start | bytes 393224 | tf_op jit(solution)/shard_map/ppermute | solution.py:21
  526.7 275.6 %collective-permute-start.38 = (bf16[16,2,2048]{2,1,0:T(2,128)(2,1)}, bf16[16,2,2048]{2,1,0:T(2,128)(2,1)}, u32[]{:S(2)}, u32[]{:S(2)}) collective-permute-start(bf16[16,2,2048]{2,1,0:T(2,128)(2,1)} %bitcast.196), channel_id=1, source_target_pairs={{0,20},{4,16},{8,28},{12,24},{16,4},{20,0},{24,12},{28,8},{1,21},{... | collective-permute-start | bytes 393224 | tf_op jit(solution)/shard_map/ppermute | solution.py:21
  552.6 67.8 %collective-permute-start.60 = (bf16[512,2048]{1,0:T(8,128)(2,1)}, bf16[512,2048]{1,0:T(8,128)(2,1)}, u32[]{:S(2)}, u32[]{:S(2)}) collective-permute-start(bf16[512,2048]{1,0:T(8,128)(2,1)} %get-tuple-element.306), channel_id=1, source_target_pairs={{0,1},{1,0},{2,3},{3,2},{4,5},{5,4},{6,7},{7,6},{8,9},{9,8},{10,11... | collective-permute-start | bytes 6291464 | tf_op jit(solution)/shard_map/ppermute | solution.py:21
  565.7 18.7 %collective-permute-start.87 = (bf16[256,1408]{1,0:T(8,128)(2,1)S(1)}, bf16[256,1408]{1,0:T(8,128)(2,1)S(1)}, u32[]{:S(2)}, u32[]{:S(2)}) collective-permute-start(bf16[256,1408]{1,0:T(8,128)(2,1)S(1)} %select_convert_fusion), channel_id=1, source_target_pairs={{0,8},{4,12},{8,0},{12,4},{16,24},{20,28},{24,16},{28,20},{1,9},{5... | collective-permute-start | bytes 2162696 | tf_op jit(solution)/shard_map/ppermute | solution.py:21
  667.8 17.3 %collective-permute-start.82 = (bf16[1024,256]{0,1:T(8,128)(2,1)}, bf16[1024,256]{0,1:T(8,128)(2,1)}, u32[]{:S(2)}, u32[]{:S(2)}) collective-permute-start(bf16[1024,256]{0,1:T(8,128)(2,1)} %fusion.50), channel_id=1, source_target_pairs={{0,4},{4,0},{8,12},{12,8},{16,20},{20,16},{24,28},{28,24},{1,5},{5... | collective-permute-start | bytes 1572872 | tf_op jit(solution)/shard_map/ppermute | solution.py:21
  674.4 50.4 %collective-permute-start.61 = (bf16[512,2048]{1,0:T(8,128)(2,1)}, bf16[512,2048]{1,0:T(8,128)(2,1)}, u32[]{:S(2)}, u32[]{:S(2)}) collective-permute-start(bf16[512,2048]{1,0:T(8,128)(2,1)} %convolution_convert_fusion.2), channel_id=1, source_target_pairs={{0,1},{1,0},{2,3},{3,2},{4,5},{5,4},{6,7},{7,6},{8,9},{9,8},{10,11... | collective-permute-start | bytes 6291464 | tf_op jit(solution)/shard_map/ppermute | solution.py:21
  684.0 36.9 %collective-permute-start.76 = (bf16[1024,768]{0,1:T(8,128)(2,1)}, bf16[1024,768]{0,1:T(8,128)(2,1)}, u32[]{:S(2)}, u32[]{:S(2)}) collective-permute-start(bf16[1024,768]{0,1:T(8,128)(2,1)} %fusion.34), channel_id=1, source_target_pairs={{0,4},{4,0},{8,12},{12,8},{16,20},{20,16},{24,28},{28,24},{1,5},{5... | collective-permute-start | bytes 4718600 | tf_op jit(solution)/shard_map/ppermute | solution.py:21
  724.4 34.1 %collective-permute-start.77 = (bf16[512,768]{0,1:T(8,128)(2,1)S(1)}, bf16[512,768]{0,1:T(8,128)(2,1)S(1)}, u32[]{:S(2)}, u32[]{:S(2)}) collective-permute-start(bf16[512,768]{0,1:T(8,128)(2,1)S(1)} %slice.1585), channel_id=1, source_target_pairs={{0,16},{4,20},{8,24},{12,28},{16,0},{20,4},{24,8},{28,12},{1,17},{... | collective-permute-start | bytes 2359304 | tf_op jit(solution)/shard_map/ppermute | solution.py:21
  728.4 33.3 %collective-permute-start.62 = (bf16[128,2048]{1,0:T(8,128)(2,1)S(1)}, bf16[128,2048]{1,0:T(8,128)(2,1)S(1)}, u32[]{:S(2)}, u32[]{:S(2)}) collective-permute-start(bf16[128,2048]{1,0:T(8,128)(2,1)S(1)} %pad_maximum_fusion.36), channel_id=1, source_target_pairs={{0,2},{1,3},{2,0},{3,1},{4,6},{5,7},{6,4},{7,5},{8,10},{9,11},{10,... | collective-permute-start | bytes 1572872 | tf_op jit(solution)/shard_map/ppermute | solution.py:21
  730.5 36.0 %collective-permute-start.64 = (bf16[128,2048]{1,0:T(8,128)(2,1)}, bf16[128,2048]{1,0:T(8,128)(2,1)}, u32[]{:S(2)}, u32[]{:S(2)}) collective-permute-start(bf16[128,2048]{1,0:T(8,128)(2,1)} %pad_maximum_fusion.37), channel_id=1, source_target_pairs={{0,8},{4,12},{8,0},{12,4},{16,24},{20,28},{24,16},{28,20},{1,9},{5... | collective-permute-start | bytes 1572872 | tf_op jit(solution)/shard_map/ppermute | solution.py:21
  759.5 19.0 %collective-permute-start.78 = (bf16[256,768]{0,1:T(8,128)(2,1)}, bf16[256,768]{0,1:T(8,128)(2,1)}, u32[]{:S(2)}, u32[]{:S(2)}) collective-permute-start(bf16[256,768]{0,1:T(8,128)(2,1)} %select_convert_fusion.1), channel_id=1, source_target_pairs={{0,8},{4,12},{8,0},{12,4},{16,24},{20,28},{24,16},{28,20},{1,9},{5... | collective-permute-start | bytes 1179656 | tf_op jit(solution)/shard_map/ppermute | solution.py:21
  766.5 35.8 %collective-permute-start.40 = (bf16[16,2,2048]{2,1,0:T(2,128)(2,1)S(1)}, bf16[16,2,2048]{2,1,0:T(2,128)(2,1)}, u32[]{:S(2)}, u32[]{:S(2)}) collective-permute-start(bf16[16,2,2048]{2,1,0:T(2,128)(2,1)S(1)} %bitcast.224), channel_id=1, source_target_pairs={{0,4},{4,0},{8,12},{12,8},{16,20},{20,16},{24,28},{28,24},{1,5},{5... | collective-permute-start | bytes 393224 | tf_op jit(solution)/shard_map/ppermute | solution.py:21
  (177 other events, 1898.0 us)

commit v2 on v1

v2 whole, which is shorter than its diff:
```python
import numpy as np

import jax
import jax.numpy as jnp
from jax import lax
from jax.experimental import pallas as pl
from jax.experimental.layout import Layout, with_layout_constraint
from jax.experimental.pallas import tpu as pltpu
from jax.sharding import PartitionSpec as P

HD = 64
ROT = 16
STEP = 10

eps = 1e-05
rates = (0.0005, 0.0002, 0.0025, 0.004, 0.0002, 6e-05)
decays = (0.0, 0.0001, 0.0, 0.0001, 0.0001, 0.0001)
bf16 = jnp.bfloat16
f32 = jnp.float32


def swap(array, axis, mask):
    pairs = [(i, i ^ mask) for i in range(lax.axis_size(axis))]
    return lax.ppermute(array, axis, pairs)


def pick(parts, flags):
    count = len(parts)
    for place, flag in enumerate(flags):
        bit = count >> (place + 1)
        parts = [jnp.where(flag, parts[j ^ bit], parts[j]) for j in range(count)]
    return parts


def joined(parts, axis=0):
    return parts[0] if len(parts) == 1 else jnp.concatenate(parts, axis)


def gather(piece, steps):
    pieces = {0: piece}
    rows = piece.shape[0]
    for axis, mask, bit in steps:
        keys = sorted(pieces)
        got = swap(joined([pieces[k] for k in keys]), axis, mask)
        for place, k in enumerate(keys):
            pieces[k | bit] = got[place * rows : (place + 1) * rows]
    return pieces


def scatter(pieces, steps):
    for axis, mask, bit in steps:
        keys = sorted(k for k in pieces if k & bit)
        got = swap(joined([pieces[k].astype(bf16) for k in keys]), axis, mask)
        rows = got.shape[0] // len(keys)
        kept = {k: v for k, v in pieces.items() if not k & bit}
        for place, k in enumerate(keys):
            kept[k ^ bit] = kept[k ^ bit].astype(f32) + got[place * rows : (place + 1) * rows].astype(f32)
        pieces = kept
    return pieces[0]


class Plan:
    def __init__(self, rows):
        self.n_seq = lax.axis_size("seq")
        self.n_tp = lax.axis_size("tp")
        self.seq = lax.axis_index("seq")
        self.tp = lax.axis_index("tp")
        bits = self.n_seq.bit_length() - 1
        self.inner = [1 << i for i in range(bits // 2)][::-1]
        self.outer = [1 << i for i in range(bits) if (1 << i) not in self.inner][::-1]
        self.groups = 1 << len(self.outer)
        self.parts = 1 << len(self.inner)
        self.rows = rows // self.groups
        self.group_flags = [(self.seq & m) != 0 for m in self.outer]
        self.part_flags = [(self.seq & m) != 0 for m in self.inner]
        self.tp_masks = [1 << i for i in range(self.n_tp.bit_length() - 1)]
        self.tp_flags = [(self.tp & m) != 0 for m in self.tp_masks[::-1]]
        self.group = self.index(self.group_flags)
        order = [("tp", m) for m in self.tp_masks] + [("seq", m) for m in self.inner]
        self.members = 1 << len(order)
        self.steps = [(axis, mask, self.members >> (i + 1)) for i, (axis, mask) in enumerate(order)]
        self.group_steps = [("seq", m, self.groups >> (i + 1)) for i, m in enumerate(self.outer)]

    def index(self, flags):
        value = jnp.int32(0)
        for flag in flags:
            value = value * 2 + flag.astype(jnp.int32)
        return value

    def outer_mask(self, j):
        return sum(m for i, m in enumerate(self.outer) if j & (self.groups >> (i + 1)))

    def inner_mask(self, j):
        return sum(m for i, m in enumerate(self.inner) if j & (self.parts >> (i + 1)))

    def member_masks(self, k):
        seq = sum(m for a, m, bit in self.steps if a == "seq" and k & bit)
        tp = sum(m for a, m, bit in self.steps if a == "tp" and k & bit)
        return seq, tp

    def arranged(self, array):
        wide = array.shape[-1] // self.n_seq
        places = [self.outer_mask(g) | self.inner_mask(h) for g in range(self.groups) for h in range(self.parts)]
        return joined([array[..., p * wide : (p + 1) * wide] for p in places], -1)

    def restored(self, array):
        wide = array.shape[-1] // self.n_seq
        blocks = [None] * self.n_seq
        for g in range(self.groups):
            for h in range(self.parts):
                at = g * self.parts + h
                blocks[self.outer_mask(g) | self.inner_mask(h)] = array[..., at * wide : (at + 1) * wide]
        return joined(blocks, -1)

    def lists(self):
        return [
            [self.outer_mask(g) | self.inner_mask(h) for g in range(self.groups)] for h in range(self.parts)
        ]

    def chosen(self, j, part, all_rows):
        row = lax.broadcasted_iota(jnp.int32, (self.rows * part, part * all_rows), 0)
        column = lax.broadcasted_iota(jnp.int32, (self.rows * part, part * all_rows), 1)
        source = (row % part) * all_rows + (self.group ^ j) * self.rows + row // part
        return (column == source).astype(bf16)

    def outgoing_rows(self, array):
        block, all_rows, width = array.shape
        part = block // self.n_tp
        size = part * all_rows
        own = lax.dynamic_slice_in_dim(array.reshape(-1, width), self.tp * size, size, 0)
        return [
            jnp.dot(self.chosen(j, part, all_rows), own, preferred_element_type=f32).astype(bf16)
            for j in range(self.groups)
        ]

    def over_groups(self, pieces):
        return [swap(piece, "seq", self.outer_mask(j)) if j else piece for j, piece in enumerate(pieces)]

    def returning_rows(self, tokens):
        table = self.restored(tokens)
        size = table.shape[0] // self.groups
        return [table[j * size : (j + 1) * size] for j in range(self.groups)]

    def returned_rows(self, got, part, all_rows):
        back = jnp.concatenate([self.chosen(j, part, all_rows) for j in range(self.groups)], 0)
        return jnp.einsum("sp,sd->pd", back, jnp.concatenate(got, 0), preferred_element_type=f32).astype(bf16)

    def of_tp(self, pieces):
        return joined(pick([pieces[k] for k in range(self.n_tp)], self.tp_flags), 0)

    def chips_sides(self, piece):
        far = self.steps[1:]
        if len(far) != 2:
            return gather(piece, far)
        return [swap(piece, axis, mask) for axis, mask, _ in far]

    def chips_corner(self, piece, sides):
        far = self.steps[1:]
        if len(far) != 2:
            return sides
        half = piece.shape[0] // 2
        (axis_x, mask_x, _), (axis_z, mask_z, _) = far
        return [swap(sides[0][:half], axis_z, mask_z), swap(sides[1][half:], axis_x, mask_x)]

    def chips_near(self, piece, sides, corner):
        if len(self.steps) != 3:
            return joined([sides[k] for k in sorted(sides)])
        return jnp.concatenate([piece, sides[1], sides[0], corner[0], corner[1]], 0)

    def swap_core(self, array):
        axis, mask, _ = self.steps[0]
        return swap(array, axis, mask)

    def sum_corner(self, near):
        far = self.steps[1:]
        if len(far) != 2:
            chips = 1 << len(far)
            rows = near.shape[0] // chips
            return [scatter({k: near[k * rows : (k + 1) * rows] for k in range(chips)}, far)]
        (axis_x, mask_x, _), (axis_z, mask_z, _) = far
        rows = near.shape[0] // 4
        half = rows // 2
        corner = near[3 * rows :].astype(bf16)
        return [swap(corner[:half], axis_x, mask_x), swap(corner[half:], axis_z, mask_z)]

    def sum_sides(self, near, corner):
        far = self.steps[1:]
        if len(far) != 2:
            return corner
        (axis_x, mask_x, _), (axis_z, mask_z, _) = far
        rows = near.shape[0] // 4
        half = rows // 2
        one, two = near[rows : 2 * rows], near[2 * rows : 3 * rows]
        for_z = jnp.concatenate([one[:half] + corner[0].astype(f32), one[half:]], 0).astype(bf16)
        for_x = jnp.concatenate([two[:half], two[half:] + corner[1].astype(f32)], 0).astype(bf16)
        return [swap(for_z, axis_z, mask_z), swap(for_x, axis_x, mask_x)]

    def sum_end(self, near, sides):
        if len(self.steps) != 3:
            return sides[0]
        rows = near.shape[0] // 4
        return near[:rows] + sides[0].astype(f32) + sides[1].astype(f32)

    def spread_mine(self, mine, axis):
        got = [mine[0]] + [swap(mine[j], "seq", self.inner_mask(j)) for j in range(1, self.parts)]
        return joined(pick(got, self.part_flags), axis)

    def collect_home(self, block_sum):
        rows = block_sum.shape[0] // self.parts
        blocks = [block_sum[h * rows : (h + 1) * rows] for h in range(self.parts)]
        mine = pick(blocks, self.part_flags)
        got = [mine[0].astype(f32)] + [
            swap(mine[j].astype(bf16), "seq", self.inner_mask(j)).astype(f32) for j in range(1, self.parts)
        ]
        return pick(got, self.part_flags)

    def all_blocks(self, block):
        return lax.all_gather(block, "seq", axis_index_groups=self.lists(), axis=0, tiled=True)

    def sum_blocks(self, product):
        return lax.psum_scatter(
            product, "seq", scatter_dimension=0, axis_index_groups=self.lists(), tiled=True
        )


def hold(*values):
    return lax.optimization_barrier(values)


def layer_norm(values, gain, shift):
    center = values - jnp.mean(values, -1, keepdims=True)
    var = jnp.mean(center * center, -1, keepdims=True)
    inverse = lax.rsqrt(var + eps)
    normed = center * inverse
    return (normed * gain + shift, normed, inverse)


def norm_back(grad, normed, inverse, gain):
    scaled = grad * gain
    inner = (
        scaled
        - jnp.mean(scaled, -1, keepdims=True)
        - normed * jnp.mean(scaled * normed, -1, keepdims=True)
    )
    return inner * inverse


def turning(position):
    lane = jnp.arange(128, dtype=jnp.int32) % HD
    half = ROT // 2
    freq = 10000.0 ** (-(lane % half).astype(f32) / half)
    angle = position.astype(f32)[:, None] * jnp.where(lane < ROT, freq, 0.0)[None, :]
    return jnp.cos(angle), jnp.sin(angle) * jnp.where(lane < half, -1.0, 1.0)[None, :]


def turned(values, cosine, sine):
    wide = values.shape[1]
    half = ROT // 2
    lane = lax.broadcasted_iota(jnp.int32, values.shape, 1) & (HD - 1)
    partner = jnp.where(lane < half, pltpu.roll(values, wide - half, 1), pltpu.roll(values, half, 1))
    return values * cosine + partner * sine


def widened(table, wide):
    return table if wide == table.shape[1] else jnp.concatenate([table] * (wide // table.shape[1]), 1)


def head_lanes(shape, head):
    return lax.broadcasted_iota(jnp.int32, shape, len(shape) - 1) // HD == head


def dot(left, right, over):
    return lax.dot_general(left, right, (over, ((), ())), preferred_element_type=f32)


def forward_kernel(lens, mixed, shift, cosine, sine, column, line, qkv_ref, low_ref, full_ref, sums_ref):
    wide = mixed.shape[-1] // 3
    length = line.shape[1]
    values = mixed[...].reshape(length, 3 * wide) + shift[...]
    cos, sin = widened(cosine[...], wide), widened(sine[...], wide)
    query = (turned(values[:, :wide], cos, sin) * 0.125).astype(bf16)
    keys = turned(values[:, wide : 2 * wide], cos, sin).astype(bf16)
    vals = values[:, 2 * wide :].astype(bf16)
    for place, part in enumerate((query, keys, vals)):
        qkv_ref[:, :, :, place * wide : (place + 1) * wide] = part.reshape(qkv_ref.shape[:-1] + (wide,))
    size = min(512, length)
    blocks = mixed.shape[0] * size // length
    limit = lens[pl.program_id(0)]
    for start in range(0, length, size):
        rows = slice(start, start + size)
        valid = (line[...] <= column[rows]) & (line[...] < limit)
        out = jnp.zeros((size, wide), f32)
        kept = jnp.zeros((size, 128), f32)
        for head in range(wide // HD):
            here = head_lanes((size, wide), head)
            scores = dot(jnp.where(here, query[rows], 0), keys, ((1,), (1,)))
            scores = jnp.where(valid, scores, -1e30)
            top = jnp.max(scores, 1, keepdims=True)
            weights = jnp.exp(scores - top)
            total = jnp.sum(weights, 1, keepdims=True)
            probs = (weights * (1.0 / total)).astype(bf16)
            out = jnp.where(here, dot(probs, vals, ((1,), (0,))), out)
            lane = lax.broadcasted_iota(jnp.int32, kept.shape, 1)
            kept = jnp.where(lane == head, top + jnp.log(total), kept)
        at = slice(start // size * blocks, (start // size + 1) * blocks)
        low_ref[at] = out.astype(bf16).reshape((blocks,) + low_ref.shape[1:])
        full_ref[at] = out.reshape((blocks,) + full_ref.shape[1:])
        sums_ref[0, rows] = kept


def backward_kernel(lens, qkv, grad, full, sums, cosine, sine, column, line, out_ref, bias_ref):
    wide = grad.shape[-1]
    length = line.shape[1]
    values = qkv[...].reshape(length, 3 * wide)
    query, keys, vals = (values[:, i * wide : (i + 1) * wide] for i in range(3))
    grads = grad[...].reshape(length, wide)
    attended = full[...].reshape(length, wide)
    size = min(512, length)
    limit = lens[pl.program_id(0)]
    grad_query = []
    grad_key = jnp.zeros((length, wide), f32)
    grad_val = jnp.zeros((length, wide), f32)
    for start in range(0, length, size):
        rows = slice(start, start + size)
        valid = (line[...] <= column[rows]) & (line[...] < limit)
        both = grads[rows].astype(f32) * attended[rows]
        grad_here = jnp.zeros((size, wide), f32)
        for head in range(wide // HD):
            here = head_lanes((size, wide), head)
            own_query = jnp.where(here, query[rows], 0)
            own_grad = jnp.where(here, grads[rows], 0)
            own_keys = jnp.where(head_lanes((length, wide), head), keys, 0)
            delta = jnp.sum(jnp.where(here, both, 0.0), 1, keepdims=True)
            scores = dot(own_query, keys, ((1,), (1,)))
            probs = jnp.where(valid, jnp.exp(scores - sums[0, rows, head : head + 1]), 0.0)
            grad_val = grad_val + dot(probs.astype(bf16), own_grad, ((0,), (0,)))
            grad_prob = dot(own_grad, vals, ((1,), (1,)))
            grad_score = (probs * (grad_prob - delta)).astype(bf16)
            grad_here = grad_here + dot(grad_score, own_keys, ((1,), (0,)))
            grad_key = grad_key + dot(grad_score, own_query, ((0,), (0,)))
        grad_query.append(grad_here)
    cos, sin = widened(cosine[...], wide), -widened(sine[...], wide)
    grad_query = turned(joined(grad_query) * 0.125, cos, sin)
    grad_key = turned(grad_key, cos, sin)
    for place, part in enumerate((grad_query, grad_key, grad_val)):
        part = part.astype(bf16)
        at = slice(place * wide, (place + 1) * wide)
        out_ref[:, :, :, at] = part.reshape(out_ref.shape[:-1] + (wide,))
        bias_ref[0, :, at] = jnp.broadcast_to(jnp.sum(part.astype(f32), 0, keepdims=True), (8, wide))


def of_row(array):
    blocks, _, places, wide = array.shape
    return pl.BlockSpec((blocks, 1, places, wide), lambda r, lens: (0, r, 0, 0))


def entire(array):
    return pl.BlockSpec(array.shape, lambda r, lens: (0,) * array.ndim)


def attend_forward(mixed, shift, tables, lens):
    blocks, rows, places, wide = mixed.shape
    wide = wide // 3
    length = blocks * places
    out = [
        jax.ShapeDtypeStruct((blocks, rows, places, 3 * wide), bf16),
        jax.ShapeDtypeStruct((blocks, rows, places, wide), bf16),
        jax.ShapeDtypeStruct((blocks, rows, places, wide), f32),
        jax.ShapeDtypeStruct((rows, length, 128), f32),
    ]
    return pl.pallas_call(
        forward_kernel,
        out_shape=out,
        grid_spec=pltpu.PrefetchScalarGridSpec(
            num_scalar_prefetch=1,
            grid=(rows,),
            in_specs=[of_row(mixed), entire(shift)] + [entire(t) for t in tables],
            out_specs=[of_row(o) for o in out[:3]]
            + [pl.BlockSpec((1, length, 128), lambda r, lens: (r, 0, 0))],
        ),
        compiler_params=pltpu.CompilerParams(vmem_limit_bytes=40 << 20),
        name="attend_forward",
    )(lens, mixed, shift, *tables)


def attend_backward(qkv, grad, full, sums, tables, lens):
    blocks, rows, places, wide = grad.shape
    length = blocks * places
    out = [
        jax.ShapeDtypeStruct(qkv.shape, bf16),
        jax.ShapeDtypeStruct((rows, 8, 3 * wide), f32),
    ]
    return pl.pallas_call(
        backward_kernel,
        out_shape=out,
        grid_spec=pltpu.PrefetchScalarGridSpec(
            num_scalar_prefetch=1,
            grid=(rows,),
            in_specs=[
                of_row(qkv),
                of_row(grad),
                of_row(full),
                pl.BlockSpec((1, length, 128), lambda r, lens: (r, 0, 0)),
            ]
            + [entire(t) for t in tables],
            out_specs=[of_row(out[0]), pl.BlockSpec((1, 8, 3 * wide), lambda r, lens: (r, 0, 0))],
        ),
        compiler_params=pltpu.CompilerParams(vmem_limit_bytes=48 << 20),
        name="attend_backward",
    )(lens, qkv, grad, full, sums, *tables)


def body(
    inputs,
    cotangent,
    lengths,
    norm_params,
    entry_weight,
    entry_bias,
    output_weight,
    gate_weight,
    down_weight,
    moment_norm,
    moment_entry,
    moment_bias,
    moment_output,
    moment_gate,
    moment_down,
    average_norm,
    average_entry,
    average_bias,
    average_output,
    average_gate,
    average_down,
):
    plan = Plan(inputs.shape[1])
    groups, parts, rows = plan.groups, plan.parts, plan.rows
    block_len, _, width = inputs.shape
    tp_width = entry_weight.shape[2]
    head_width = tp_width // parts
    heads_here = head_width // HD
    hidden = gate_weight.shape[2] // parts
    quarter = block_len // plan.n_tp
    share = rows * groups * quarter
    plan.total = share * plan.members
    length = block_len * plan.n_seq

    member_seq = np.array([plan.member_masks(k)[0] for k in range(plan.members)], np.int32)
    member_tp = np.array([plan.member_masks(k)[1] for k in range(plan.members)], np.int32)
    sender = np.array([plan.outer_mask(j) for j in range(groups)], np.int32)
    seq_at = plan.seq ^ (member_seq[:, None] | sender[None, :])
    tp_at = plan.tp ^ member_tp
    position = (
        (seq_at * block_len)[:, :, None]
        + (tp_at * quarter)[:, None, None]
        + np.arange(quarter, dtype=np.int32)[None, None, :]
    )
    lens = lax.dynamic_slice_in_dim(lengths, plan.group * rows, rows, 0)

    def over_masks(array, masks):
        sums = [0]
        for mask in masks:
            sums = sums + [m | mask for m in sums]
        return [swap(array, "seq", m) for m in sums[1:]]

    def total_of(array, got):
        for other in got:
            array = array + other
        return array

    lane_block = lax.broadcasted_iota(jnp.int32, (4, width), 1) // norm_params.shape[1]
    small = jnp.where(lane_block == plan.seq, jnp.tile(norm_params.astype(bf16), (1, plan.n_seq)), 0)
    slim = entry_bias.shape[2]
    slot = lax.broadcasted_iota(jnp.int32, (slim, HD), 1) == plan.seq * slim + lax.broadcasted_iota(
        jnp.int32, (slim, HD), 0
    )
    placed = jnp.dot(entry_bias.reshape(-1, slim).astype(bf16), slot.astype(bf16), preferred_element_type=f32)
    placed = placed.astype(bf16).reshape(1, 3 * tp_width)
    placed = jnp.pad(placed, ((0, 0), (0, width - 3 * tp_width)))
    small = jnp.concatenate([small, placed], 0)
    seq_masks = [1 << i for i in range(plan.n_seq.bit_length() - 1)]
    last_mask = plan.outer[-1]
    first_masks = [m for m in seq_masks if m != last_mask]

    def columns(array, h, size):
        return array[..., h * size : (h + 1) * size].astype(bf16).reshape(array.shape[0], -1)

    def turned_columns(array, h):
        return array[:, h * hidden : (h + 1) * hidden].astype(bf16).T

    small_got = over_masks(small, first_masks)
    outgoing = plan.outgoing_rows(inputs)
    resid = plan.over_groups(outgoing)
    attn_mine = pick(
        [
            jnp.concatenate(
                [columns(entry_weight, h, head_width), columns(output_weight, h, head_width)], 1
            )
            for h in range(parts)
        ],
        plan.part_flags,
    )
    attn_block = plan.spread_mine(attn_mine, 0)
    gate_mine = pick([columns(gate_weight, h, hidden) for h in range(parts)], plan.part_flags)
    small, small_got, resid, attn_block, cotangent, gate_mine, position, down_weight = hold(
        small, small_got, resid, attn_block, cotangent, gate_mine, position, down_weight
    )

    w_attn = plan.all_blocks(attn_block)
    small = total_of(small, small_got)
    small_got = over_masks(small, [last_mask])
    gate_block = plan.spread_mine(gate_mine, 0)
    outgoing = plan.outgoing_rows(cotangent)
    small, small_got, resid, gate_block, outgoing, position, down_weight = hold(
        small, small_got, resid, gate_block, outgoing, position, down_weight
    )

    small = total_of(small, small_got)
    gains = plan.arranged(small[:4]).astype(f32)
    resid = plan.arranged(jnp.concatenate(resid, 0)).astype(f32)
    h_first, n_first, i_first = layer_norm(resid, gains[0], gains[1])
    low_first = h_first.astype(bf16)
    sides = plan.chips_sides(low_first)
    row_position = position.reshape(length)
    tables = turning(row_position) + (row_position[:, None], row_position[None, :])
    down_mine = pick([columns(down_weight, h, hidden) for h in range(parts)], plan.part_flags)
    low_first, sides, tables, down_mine, outgoing, gate_block = hold(
        low_first, sides, tables, down_mine, outgoing, gate_block
    )

    corner = plan.chips_corner(low_first, sides)
    down_block = plan.spread_mine(down_mine, 0)
    low_first, sides, corner, down_block, outgoing = hold(low_first, sides, corner, down_block, outgoing)
    near = plan.chips_near(low_first, sides, corner)
    other = plan.swap_core(near)
    grad_y = plan.over_groups(outgoing)
    near, other, grad_y, w_attn, gate_block, down_block = hold(
        near, other, grad_y, w_attn, gate_block, down_block
    )
    a_first = jnp.concatenate([near, other], 0)
    w_gate = plan.all_blocks(gate_block)
    own_position = jnp.broadcast_to(position[0][:, None, :], (groups, rows, quarter))
    real = (own_position < lens[None, :, None]).reshape(share, 1)
    grad_y = plan.arranged(jnp.concatenate(grad_y, 0))
    grad_y = jnp.where(real, grad_y, 0)
    y_sides = plan.chips_sides(grad_y)

    w_entry = w_attn[:, : 3 * head_width]
    w_output = w_attn[:, 3 * head_width :]
    mixed = jnp.einsum("td,df->tf", a_first, w_entry, preferred_element_type=f32)
    mixed = mixed.reshape(plan.members * groups, rows, quarter, 3 * head_width)
    biases = [
        jnp.concatenate(
            [
                small[4:, c * tp_width + h * head_width : c * tp_width + (h + 1) * head_width]
                for c in range(3)
            ],
            1,
        )
        for h in range(parts)
    ]
    entry_shift = pick(biases, plan.part_flags)[0].astype(f32)
    qkv, att_low, attended, score_sums = attend_forward(mixed, entry_shift, tables, lens)
    att_low = att_low.reshape(plan.total, head_width)

    def output_product(lo, hi):
        return jnp.einsum("th,dh->td", att_low[lo:hi], w_output, preferred_element_type=f32)

    half = plan.total // 2
    far_product = output_product(half, plan.total).astype(bf16)
    far_product, grad_y, y_sides, down_block = hold(far_product, grad_y, y_sides, down_block)

    got = plan.swap_core(far_product)
    product = output_product(0, half)
    y_corner = plan.chips_corner(grad_y, y_sides)
    product, got, y_corner = hold(product, got, y_corner)

    near = product + got.astype(f32)
    corner = plan.sum_corner(near)
    y_near = plan.chips_near(grad_y, y_sides, y_corner)
    near, corner, y_near = hold(near, corner, y_near)
    sides = plan.sum_sides(near, corner)
    y_other = plan.swap_core(y_near)
    near, sides, y_near, y_other, down_block = hold(near, sides, y_near, y_other, down_block)

    second = resid + plan.sum_end(near, sides)
    h_second, n_second, i_second = layer_norm(second, gains[2], gains[3])
    low_second = h_second.astype(bf16)
    sides = plan.chips_sides(low_second)
    grad_y_all = jnp.concatenate([y_near, y_other], 0)
    second, low_second, sides, grad_y_all = hold(second, low_second, sides, grad_y_all)
    corner = plan.chips_corner(low_second, sides)
    low_second, sides, corner, w_gate, down_block = hold(low_second, sides, corner, w_gate, down_block)
    w_down = plan.all_blocks(down_block)
    near = plan.chips_near(low_second, sides, corner)
    other = plan.swap_core(near)
    near, other = hold(near, other)

    a_second = jnp.concatenate([near, other], 0)
    gated = jnp.einsum("td,df->tf", a_second, w_gate, preferred_element_type=f32)
    gate = gated[:, :hidden]
    upper = gated[:, hidden:]
    sigma = jax.nn.sigmoid(gate)
    active_gate = gate * sigma
    hid = (active_gate * upper).astype(bf16)
    grad_down = jnp.einsum("td,tf->df", grad_y_all, hid, preferred_element_type=f32).astype(bf16)
    hid, grad_down, w_down = hold(hid, grad_down, w_down)
    down_sum = plan.sum_blocks(grad_down)
    grad_hidden = jnp.einsum(
        "td,df->tf", grad_y_all, w_down, preferred_element_type=f32
    ).astype(bf16)
    grad_gate_val = grad_hidden * upper * (sigma * (1.0 + gate * (1.0 - sigma)))
    grad_up_val = grad_hidden * active_gate
    grad_gated = jnp.concatenate([grad_gate_val, grad_up_val], 1).astype(bf16)

    def gate_product(lo, hi):
        return jnp.einsum("tf,df->td", grad_gated[lo:hi], w_gate, preferred_element_type=f32)

    def down_product(lo, hi):
        return jnp.einsum("tf,df->td", hid[lo:hi], w_down, preferred_element_type=f32)

    far_product = gate_product(half, plan.total).astype(bf16)
    hid, grad_gated, far_product = hold(hid, grad_gated, far_product)

    got = plan.swap_core(far_product)
    product = gate_product(0, half)
    product, got, a_second, hid, grad_gated = hold(product, got, a_second, hid, grad_gated)

    near = product + got.astype(f32)
    corner = plan.sum_corner(near)
    grad_gate = jnp.einsum("td,tf->df", a_second, grad_gated, preferred_element_type=f32).astype(bf16)
    near, corner, grad_gate, hid, down_sum = hold(near, corner, grad_gate, hid, down_sum)
    gate_sum = plan.sum_blocks(grad_gate)
    sides = plan.sum_sides(near, corner)
    out_far = down_product(half, plan.total).astype(bf16)
    near, sides, out_far, hid, down_sum = hold(near, sides, out_far, hid, down_sum)

    out_got = plan.swap_core(out_far)
    grad_h2 = plan.sum_end(near, sides)
    grad_second = grad_y.astype(f32) + norm_back(grad_h2, n_second, i_second, gains[2])
    low_grad = grad_second.astype(bf16)
    sides = plan.chips_sides(low_grad)
    out_near = down_product(0, half)
    low_grad, sides, out_near, out_got, grad_h2, grad_second = hold(
        low_grad, sides, out_near, out_got, grad_h2, grad_second
    )
    out_near = out_near + out_got.astype(f32)
    corner = plan.chips_corner(low_grad, sides)
    out_corner = plan.sum_corner(out_near)
    low_grad, sides, corner, out_corner, out_near = hold(low_grad, sides, corner, out_corner, out_near)

    near = plan.chips_near(low_grad, sides, corner)
    other = plan.swap_core(near)
    near, other = hold(near, other)
    grad_second_all = jnp.concatenate([near, other], 0)
    grad_att = jnp.einsum(
        "td,dh->th", grad_second_all, w_output, preferred_element_type=f32
    ).astype(bf16)
    grad_att = grad_att.reshape(attended.shape)
    grad_mixed, bias_sum = attend_backward(qkv, grad_att, attended, score_sums, tables, lens)
    grad_mixed = grad_mixed.reshape(plan.total, 3 * head_width)

    def entry_product(lo, hi):
        return jnp.einsum("tf,df->td", grad_mixed[lo:hi], w_entry, preferred_element_type=f32)

    far_product = entry_product(half, plan.total).astype(bf16)
    out_sides = plan.sum_sides(out_near, out_corner)
    far_product, grad_mixed, bias_sum, out_sides, out_near = hold(
        far_product, grad_mixed, bias_sum, out_sides, out_near
    )

    got = plan.swap_core(far_product)
    product = entry_product(0, half)
    grad_attn = jnp.concatenate(
        [
            jnp.einsum("td,tf->df", a_first, grad_mixed, preferred_element_type=f32).astype(bf16),
            jnp.einsum("td,tf->df", grad_second_all, att_low, preferred_element_type=f32).astype(bf16),
        ],
        1,
    )
    product, got, grad_attn, bias_sum, down_sum = hold(product, got, grad_attn, bias_sum, down_sum)

    near = product + got.astype(f32)
    corner = plan.sum_corner(near)
    near, corner, bias_sum, down_sum, grad_attn = hold(near, corner, bias_sum, down_sum, grad_attn)
    sides = plan.sum_sides(near, corner)
    result = second + plan.sum_end(out_near, out_sides)
    out_returning = plan.returning_rows(result.astype(bf16))
    near, sides, out_returning, bias_sum, down_sum, gate_sum, grad_attn = hold(
        near, sides, out_returning, bias_sum, down_sum, gate_sum, grad_attn
    )
    attn_sum = plan.sum_blocks(grad_attn)

    grad_h1 = plan.sum_end(near, sides)
    grad_input = grad_second + norm_back(grad_h1, n_first, i_first, gains[0])
    back = plan.over_groups(plan.returning_rows(grad_input.astype(bf16)))
    out_back = plan.over_groups(out_returning)
    gate_home = plan.collect_home(gate_sum)
    down_home = plan.collect_home(down_sum)
    back, out_back, grad_h1, bias_sum, gate_home, down_home = hold(
        back, out_back, grad_h1, bias_sum, gate_home, down_home
    )

    def along_tp(own, steps):
        pieces = {0: own}
        for mask in steps:
            for k in sorted(pieces):
                pieces[k | mask] = swap(pieces[k], "tp", mask)
        return pieces

    own = plan.returned_rows(back, quarter, inputs.shape[1])
    out_own = plan.returned_rows(out_back, quarter, inputs.shape[1])
    wide_masks, core_masks = plan.tp_masks[:0:-1], plan.tp_masks[:1]
    pieces = gather(own, [("tp", m, m) for m in wide_masks])
    out_pieces = gather(out_own, [("tp", m, m) for m in wide_masks])
    sums = jnp.stack(
        [
            jnp.sum(grad_h1 * n_first, 0),
            jnp.sum(grad_h1, 0),
            jnp.sum(grad_h2 * n_second, 0),
            jnp.sum(grad_h2, 0),
        ]
    )
    for mask in core_masks:
        sums = sums + swap(sums, "tp", mask)
    grad_gate, grad_down = gate_home, down_home
    pieces, out_pieces, sums = hold(pieces, out_pieces, sums)

    def across_cores(pieces):
        keys = sorted(pieces)
        got = swap(joined([pieces[k] for k in keys]), "tp", core_masks[0])
        size = got.shape[0] // len(keys)
        pieces = {**pieces, **{k | core_masks[0]: got[i * size : (i + 1) * size] for i, k in enumerate(keys)}}
        return plan.of_tp(pieces).reshape(inputs.shape)

    input_grad = across_cores(pieces)
    layer_out = across_cores(out_pieces)
    attn_home = plan.collect_home(attn_sum)
    grad_entry = [part[:, : 3 * head_width] for part in attn_home]
    grad_output = [part[:, 3 * head_width :] for part in attn_home]

    bias_sum = jnp.sum(bias_sum[:, 0], 0)
    for mask in plan.outer:
        bias_sum = bias_sum + swap(bias_sum, "seq", mask)
    bias_sum = bias_sum.reshape(3, heads_here, HD)
    got = [bias_sum] + [swap(bias_sum, "seq", plan.inner_mask(j)) for j in range(1, parts)]
    bias_sum = joined(pick(got, plan.part_flags), 1)
    grad_bias = lax.dynamic_slice_in_dim(bias_sum, plan.seq * slim, slim, 2)
    for mask in wide_masks:
        sums = sums + swap(sums, "tp", mask)
    sums = plan.restored(sums)
    for mask in seq_masks:
        sums = sums + swap(sums, "seq", mask)
    slim = norm_params.shape[1]
    grad_norm = lax.dynamic_slice_in_dim(sums, plan.seq * slim, slim, 1)

    def ordered_as(grad, *order):
        return with_layout_constraint(grad, Layout(order))

    reduced = (
        grad_norm,
        ordered_as(
            joined([part.reshape(part.shape[0], 3, head_width) for part in grad_entry], -1), 1, 0, 2
        ),
        grad_bias,
        ordered_as(joined(grad_output, -1), 0, 1),
        ordered_as(
            joined([part.reshape(part.shape[0], 2, hidden) for part in grad_gate], -1), 0, 1, 2
        ),
        ordered_as(joined(grad_down, -1), 0, 1),
    )
    masters = (norm_params, entry_weight, entry_bias, output_weight, gate_weight, down_weight)
    moments = (moment_norm, moment_entry, moment_bias, moment_output, moment_gate, moment_down)
    averages = (
        average_norm,
        average_entry,
        average_bias,
        average_output,
        average_gate,
        average_down,
    )
    beta = min(0.999, (1 + STEP) / (10 + STEP))
    news, new_weights, smooths, copies = ([], [], [], [])
    for index in range(6):
        grad = reduced[index] + decays[index] * masters[index]
        moment = 0.9 * moments[index] + grad
        weight = masters[index] - rates[index] * (grad + 0.9 * moment)
        news.append(moment)
        new_weights.append(weight)
        smooths.append(beta * averages[index] + (1.0 - beta) * weight)
        copies.append(weight.astype(bf16))
    return (layer_out, input_grad, *news, *new_weights, *smooths, *copies)


def solution(mesh):
    in_specs = (
        P("seq", None, None),
        P("seq", None, None),
        P(),
        P(None, "seq"),
        P("seq", None, "tp"),
        P(None, "tp", "seq"),
        P("seq", "tp"),
        P("seq", None, "tp"),
        P("seq", "tp"),
        P(None, "seq"),
        P("seq", None, "tp"),
        P(None, "tp", "seq"),
        P("seq", "tp"),
        P("seq", None, "tp"),
        P("seq", "tp"),
        P(None, "seq"),
        P("seq", None, "tp"),
        P(None, "tp", "seq"),
        P("seq", "tp"),
        P("seq", None, "tp"),
        P("seq", "tp"),
    )
    out_specs = (
        P("seq", None, None),
        P("seq", None, None),
        P(None, "seq"),
        P("seq", None, "tp"),
        P(None, "tp", "seq"),
        P("seq", "tp"),
        P("seq", None, "tp"),
        P("seq", "tp"),
        P(None, "seq"),
        P("seq", None, "tp"),
        P(None, "tp", "seq"),
        P("seq", "tp"),
        P("seq", None, "tp"),
        P("seq", "tp"),
        P(None, "seq"),
        P("seq", None, "tp"),
        P(None, "tp", "seq"),
        P("seq", "tp"),
        P("seq", None, "tp"),
        P("seq", "tp"),
        P(None, "seq"),
        P("seq", None, "tp"),
        P(None, "tp", "seq"),
        P("seq", "tp"),
        P("seq", None, "tp"),
        P("seq", "tp"),
    )
    return jax.shard_map(body, mesh=mesh, in_specs=in_specs, out_specs=out_specs, check_vma=False)
```

time: 853 us -> 690 us (0.81)
  local copies, waits for them, and re-layouts: 198 us -> 80.8 us
  starting transfers between devices: 117 us -> 77.9 us
  matrix products: 111 us -> 85.3 us
  Pallas kernels: 0 us -> 15.9 us
  waiting for transfers between devices: 315 us -> 301 us
  between operations: 3.97 us -> 16.5 us
    ppermute x91 -> x74, waiting for transfers between devices: 315 us -> 198 us  [swap(): return lax.ppermute(array, axis, pairs)]
    all_gather x0 -> x3, waiting for transfers between devices: none -> 69.6 us  [all_blocks(): lax.all_gather(block, 'seq', axis_index_groups=self.lists(), axis=0, tile...]
    unnamed x366 -> x291, local copies, waits for them, and re-layouts: 93.7 us -> 44.5 us
    ppermute x91 -> x74, starting transfers between devices: 117 us -> 76.6 us  [swap(): return lax.ppermute(array, axis, pairs)]
    reduce_scatter x0 -> x3, waiting for transfers between devices: none -> 33.1 us  [sum_blocks(): lax.psum_scatter(product, 'seq', scatter_dimension=0, axis_index_groups=s...]
    dot_general x21 -> x23, matrix products: 81.6 us -> 58.7 us  [the longest x2 12.2 us: gate_product(): jnp.einsum('tf,df->td', grad_gated[lo:hi], w_gate, preferred_element_type...]
    another operation x7 -> x14, other arithmetic: 2.4 us -> 21.2 us
    reshape x11 -> x8, local copies, waits for them, and re-layouts: 25.6 us -> 8.2 us  [the longest x2 6.16 us: body(): part.reshape(part.shape[0], 2, hidden)]
  transfers between devices with their start and end apart: 91 -> 80, of which waited for: 39 -> 50; matrix products, arithmetic and copies ran while one was open for 45% -> 31% of each run, Pallas kernels for 0% -> 2%
where the time goes in v2:
time: 690 us; the launch traced here: 677 us
  waiting for transfers between devices  301 us (44%)
  other arithmetic  100 us (14%)
  matrix products  85.3 us (12%)
  local copies, waits for them, and re-layouts  80.8 us (12%)
  starting transfers between devices  77.9 us (11%)
  between operations  16.5 us (2%)
  Pallas kernels  15.9 us (2%)
    ppermute x74, waiting for transfers between devices, swap(): return lax.ppermute(array, axis, pairs)  198 us
    ppermute x74, starting transfers between devices, swap(): return lax.ppermute(array, axis, pairs)  76.6 us
    all_gather x3, waiting for transfers between devices, all_blocks(): lax.all_gather(block, 'seq', axis_index_groups=self.lists(), axis=0, tile...  69.6 us
    unnamed x291, local copies, waits for them, and re-layouts  44.5 us
    reduce_scatter x3, waiting for transfers between devices, sum_blocks(): lax.psum_scatter(product, 'seq', scatter_dimension=0, axis_index_groups=s...  33.1 us
    another operation x14, other arithmetic  21.2 us
    select_n x15, other arithmetic, pick(): parts = [jnp.where(flag, parts[j ^ bit], parts[j]) for j in range(count)]  18.9 us
    convert_element_type x6, other arithmetic, body(): copies.append(weight.astype(bf16))  16.1 us
  transfers between devices with their start and end apart: 80, of which 50 were waited for; matrix products, arithmetic and copies ran while one was open for 31% of the time, Pallas kernels for 2%

profile of v2, /device:TPU:16, one launch (start us, length us, event | category | flops | bytes accessed | tf_op | source)
XLA Modules:
  0.0 677.4 jit_solution(9497421704498972560)
XLA Ops:
  26.2 5.0 copy.61
  38.7 3.6 collective-permute-done.4
  42.3 4.0 collective-permute-done.5
  56.2 8.8 %collective-permute-done.8 = bf16[256,1408]{1,0:T(8,128)(2,1)} collective-permute-done((bf16[256,1408]{1,0:T(8,128)(2,1)}, bf16[256,1408]{1,0:T(8,128)(2,1)}, u32[]{:S(2)}, u32[]{:S(2)}) %collective-permute-start.8) | collective-permute-done | bytes 720928 | tf_op jit(solution)/shard_map/ppermute | solution.py:24
  73.4 7.9 %collective-permute-done.10 = bf16[128,2048]{1,0:T(8,128)(2,1)} collective-permute-done((bf16[128,2048]{1,0:T(8,128)(2,1)S(1)}, bf16[128,2048]{1,0:T(8,128)(2,1)}, u32[]{:S(2)}, u32[]{:S(2)}) %collective-permute-start.10) | collective-permute-done | bytes 524320 | tf_op jit(solution)/shard_map/ppermute | solution.py:24
  88.3 4.5 collective-permute-done.13
  105.0 8.7 %collective-permute-done.15 = bf16[32,2048]{1,0:T(8,128)(2,1)S(1)} collective-permute-done((bf16[32,2048]{1,0:T(8,128)(2,1)}, bf16[32,2048]{1,0:T(8,128)(2,1)S(1)}, u32[]{:S(2)}, u32[]{:S(2)}) %collective-permute-start.15) | collective-permute-done | bytes 131104 | tf_op jit(solution)/shard_map/ppermute | solution.py:24
  113.7 5.2 collective-permute-done.16
  119.0 12.5 %collective-permute-done.17 = bf16[32,2048]{1,0:T(8,128)(2,1)S(1)} collective-permute-done((bf16[32,2048]{1,0:T(8,128)(2,1)}, bf16[32,2048]{1,0:T(8,128)(2,1)S(1)}, u32[]{:S(2)}, u32[]{:S(2)}) %collective-permute-start.17) | collective-permute-done | bytes 131104 | tf_op jit(solution)/shard_map/ppermute | solution.py:24
  131.4 10.3 %all-gather.4.cloned.1.call-done = bf16[2048,1024]{1,0:T(8,128)(2,1)} async-done(((bf16[512,1024]{1,0:T(8,128)(2,1)}), bf16[2048,1024]{1,0:T(8,128)(2,1)}) %all-gather.4.cloned.1.call-update) | async-done | bytes 4194320 | tf_op jit(solution)/shard_map/all_gather | solution.py:218
  148.4 3.3 constant_dynamic-update-slice_fusion.5
  151.7 5.4 fusion.7
  157.1 6.9 %attend_forward.1 = (bf16[32,2,16,768]{3,2,1,0:T(8,128)(2,1)S(1)}, bf16[32,2,16,256]{3,2,1,0:T(8,128)(2,1)S(1)}, f32[32,2,16,256]{3,2,1,0:T(8,128)S(1)}, f32[2,512,128]{2,1,0:T(8,128)S(1)}) custom-call(s32[2]{0:T(128)S(1)} %dynamic_slice.15.lens, f32[32,2,16,768]{3,2,1,0:T(8,128)S(1)} %bitcast.64, f32[1,768]{1,0:T(1,128)S(1)} %fusion.74.shift, ...), custom_call_target="tpu_custom_call" | custom-call | tf_op jit(solution)/shard_map/attend_forward/pallas_call | solution.py:371
  172.1 3.3 collective-permute-done.21
  180.0 5.6 collective-permute-done.23
  189.7 11.3 %collective-permute-done.26 = bf16[128,2048]{1,0:T(8,128)(2,1)S(1)} collective-permute-done((bf16[128,2048]{1,0:T(8,128)(2,1)S(1)}, bf16[128,2048]{1,0:T(8,128)(2,1)S(1)}, u32[]{:S(2)}, u32[]{:S(2)}) %collective-permute-start.26) | collective-permute-done | bytes 524320 | tf_op jit(solution)/shard_map/ppermute | solution.py:24
  208.6 8.6 %collective-permute-done.28 = bf16[128,2048]{1,0:T(8,128)(2,1)S(1)} collective-permute-done((bf16[128,2048]{1,0:T(8,128)(2,1)S(1)}, bf16[128,2048]{1,0:T(8,128)(2,1)S(1)}, u32[]{:S(2)}, u32[]{:S(2)}) %collective-permute-start.28) | collective-permute-done | bytes 524320 | tf_op jit(solution)/shard_map/ppermute | solution.py:24
  220.7 4.4 collective-permute-done.30
  226.4 26.6 %all-gather.6.cloned.1.call-done = bf16[2048,1408]{1,0:T(8,128)(2,1)} async-done(((bf16[512,1408]{1,0:T(8,128)(2,1)}), bf16[2048,1408]{1,0:T(8,128)(2,1)}) %all-gather.6.cloned.1.call-update) | async-done | bytes 5767184 | tf_op jit(solution)/shard_map/all_gather | solution.py:218
  261.4 4.0 collective-permute-done.32
  271.4 9.2 %fusion.128 = f32[1024,1408]{1,0:T(8,128)S(1)} fusion(bf16[1024,2048]{1,0:T(8,128)(2,1)S(1)} %constant_dynamic-update-slice_fusion.17, bf16[2048,1408]{1,0:T(8,128)(2,1)} %all-gather.6.cloned.1.call-done), kind=kOutput, calls=%fused_computation.334 | convolution fusion | flops 5905580032 | bytes 15728640 | tf_op jit(solution)/shard_map/td,df->tf/dot_general | solution.py:600
  285.9 4.9 convolution_convert_fusion.2
  290.8 32.7 %all-gather.8.cloned.1.call-done = bf16[2048,704]{1,0:T(8,128)(2,1)} async-done(((bf16[512,704]{1,0:T(8,128)(2,1)}), bf16[2048,704]{1,0:T(8,128)(2,1)}) %all-gather.8.cloned.1.call-update) | async-done | bytes 2883600 | tf_op jit(solution)/shard_map/all_gather | solution.py:218
  323.5 10.9 %fusion.1 = (bf16[1024,704]{1,0:T(8,128)(2,1)}, bf16[1024,704]{1,0:T(8,128)(2,1)}) fusion(f32[1024,1408]{1,0:T(8,128)} %copy-done.19, bf16[1024,2048]{1,0:T(8,128)(2,1)} %pad_maximum_fusion, bf16[2048,704]{1,0:T(8,128)(2,1)} %all-gather.8.cloned.1.call-done), kind=kOutput, calls=%fused_computation.15 | convolution fusion | flops 2963603456 | bytes 15728640 | tf_op jit(solution)/shard_map/td,df->tf/dot_general | solution.py:609
  334.6 6.7 convolution_convert_fusion.6
  342.3 5.5 fusion.11
  354.5 8.7 %convolution_convert_fusion = bf16[2048,1408]{1,0:T(8,128)(2,1)} fusion(bf16[1024,2048]{1,0:T(8,128)(2,1)S(1)} %copy-done.65, bf16[1024,1408]{1,0:T(8,128)(2,1)S(1)} %pad_maximum_fusion.2), kind=kOutput, calls=%fused_computation | convolution fusion | flops 5908463616 | bytes 12845056 | tf_op jit(solution)/shard_map/td,tf->df/dot_general | solution.py:631
  363.2 31.6 %reduce-scatter.4.cloned.1.call-done = bf16[512,704]{1,0:T(8,128)(2,1)} async-done(((bf16[2048,704]{1,0:T(8,128)(2,1)}), bf16[512,704]{1,0:T(8,128)(2,1)}) %reduce-scatter.4.cloned.1.call-update) | async-done | bytes 720912 | tf_op jit(solution)/shard_map/reduce_scatter | solution.py:221
  402.7 3.2 convolution_convert_fusion.5
  405.9 7.4 %collective-permute-done.37 = bf16[128,2048]{1,0:T(8,128)(2,1)S(1)} collective-permute-done((bf16[128,2048]{1,0:T(8,128)(2,1)S(1)}, bf16[128,2048]{1,0:T(8,128)(2,1)S(1)}, u32[]{:S(2)}, u32[]{:S(2)}) %collective-permute-start.37) | collective-permute-done | bytes 524320 | tf_op jit(solution)/shard_map/ppermute | solution.py:24
  415.2 3.2 fusion.109
  420.7 4.0 fusion.34
  424.6 8.4 %collective-permute-done.38 = bf16[128,2048]{1,0:T(8,128)(2,1)} collective-permute-done((bf16[128,2048]{1,0:T(8,128)(2,1)}, bf16[128,2048]{1,0:T(8,128)(2,1)}, u32[]{:S(2)}, u32[]{:S(2)}) %collective-permute-start.38) | collective-permute-done | bytes 524320 | tf_op jit(solution)/shard_map/ppermute | solution.py:24
  446.8 3.7 collective-permute-done.41
  462.4 9.1 %attend_backward.1 = (bf16[32,2,16,768]{3,2,1,0:T(8,128)(2,1)S(1)}, f32[2,8,768]{2,1,0:T(8,128)S(1)}) custom-call(s32[2]{0:T(128)S(1)} %dynamic_slice.15.lens, bf16[32,2,16,768]{3,2,1,0:T(8,128)(2,1)S(1)} %get-tuple-element.327.qkv, bf16[32,2,16,256]{3,2,1,0:T(8,128)(2,1)S(1)} %bitcast.65, f32[32,2,16,256]{3,2,1,0:T(8,128)S(1)} %get-tuple-element.340.full, ...), custom_call_target="tpu_custom_call" | custom-call | tf_op jit(solution)/shard_map/attend_backward/pallas_call | solution.py:393
  477.9 4.0 convolution_convert_fusion.1
  484.6 3.7 fusion.4
  488.5 4.6 fusion.107
  495.7 5.8 collective-permute-done.49
  512.1 8.3 %collective-permute-done.52 = bf16[128,2048]{1,0:T(8,128)(2,1)} collective-permute-done((bf16[128,2048]{1,0:T(8,128)(2,1)S(1)}, bf16[128,2048]{1,0:T(8,128)(2,1)}, u32[]{:S(2)}, u32[]{:S(2)}) %collective-permute-start.52) | collective-permute-done | bytes 524320 | tf_op jit(solution)/shard_map/ppermute | solution.py:24
  539.4 10.5 %collective-permute-done.59 = bf16[256,1408]{1,0:T(8,128)(2,1)} collective-permute-done((bf16[256,1408]{1,0:T(8,128)(2,1)}, bf16[256,1408]{1,0:T(8,128)(2,1)}, u32[]{:S(2)}, u32[]{:S(2)}) %collective-permute-start.59) | collective-permute-done | bytes 720928 | tf_op jit(solution)/shard_map/ppermute | solution.py:24
  552.9 9.8 %collective-permute-done.55 = bf16[32,2048]{1,0:T(8,128)(2,1)S(1)} collective-permute-done((bf16[32,2048]{1,0:T(8,128)(2,1)S(1)}, bf16[32,2048]{1,0:T(8,128)(2,1)S(1)}, u32[]{:S(2)}, u32[]{:S(2)}) %collective-permute-start.55) | collective-permute-done | bytes 131104 | tf_op jit(solution)/shard_map/ppermute | solution.py:24
  562.7 9.1 %collective-permute-done.57 = bf16[32,2048]{1,0:T(8,128)(2,1)S(1)} collective-permute-done((bf16[32,2048]{1,0:T(8,128)(2,1)S(1)}, bf16[32,2048]{1,0:T(8,128)(2,1)S(1)}, u32[]{:S(2)}, u32[]{:S(2)}) %collective-permute-start.57) | collective-permute-done | bytes 131104 | tf_op jit(solution)/shard_map/ppermute | solution.py:24
  571.8 12.9 %collective-permute-done.58 = bf16[32,2048]{1,0:T(8,128)(2,1)S(1)} collective-permute-done((bf16[32,2048]{1,0:T(8,128)(2,1)S(1)}, bf16[32,2048]{1,0:T(8,128)(2,1)S(1)}, u32[]{:S(2)}, u32[]{:S(2)}) %collective-permute-start.58) | collective-permute-done | bytes 131104 | tf_op jit(solution)/shard_map/ppermute | solution.py:24
  593.8 3.6 copy.78
  602.8 8.7 %fusion.102 = (bf16[256,2,1408]{2,1,0:T(2,128)(2,1)}, f32[256,2,1408]{2,1,0:T(2,128)S(1)}, f32[256,2,1408]{2,1,0:T(2,128)}) fusion(f32[256,2,1408]{2,1,0:T(2,128)S(1)} %copy-done.13, f32[256,2,704]{2,1,0:T(2,128)S(1)} %copy-done.31, f32[256,2,704]{2,1,0:T(2,128)S(1)} %copy.77, f32[256,2,1408]{2,1,0:T(2,128)} %param.37), kind=kLoop, calls=%fused_computation.308 | loop fusion | flops 7208960 | bytes 15859712 | tf_op jit(solution)/shard_map/convert_element_type | solution.py:791
  611.6 4.1 multiply_add_fusion
  654.2 5.2 collective-permute-done.70
  (605 shorter events, 271.8 us)
Async XLA Ops:
  7.2 134.6 %all-gather.4.cloned.1.call-start = ((), (), s32[]{:S(2)}) async-start(), calls=%async_computation.3 | async-start | bytes 5242880 | tf_op jit(solution)/shard_map/all_gather | solution.py:218
  9.8 25.5 %collective-permute-start = (bf16[5,2048]{1,0:T(8,128)(2,1)}, bf16[5,2048]{1,0:T(8,128)(2,1)}, u32[]{:S(2)}, u32[]{:S(2)}) collective-permute-start(bf16[5,2048]{1,0:T(8,128)(2,1)} %fusion.61), channel_id=1, source_target_pairs={{0,4},{4,0},{8,12},{12,8},{16,20},{20,16},{24,28},{28,24},{1,5},{5... | collective-permute-start | bytes 61448 | tf_op jit(solution)/shard_map/ppermute | solution.py:24
  11.3 27.3 %collective-permute-start.1 = (bf16[5,2048]{1,0:T(8,128)(2,1)}, bf16[5,2048]{1,0:T(8,128)(2,1)}, u32[]{:S(2)}, u32[]{:S(2)}) collective-permute-start(bf16[5,2048]{1,0:T(8,128)(2,1)} %fusion.61), channel_id=1, source_target_pairs={{0,16},{4,20},{8,24},{12,28},{16,0},{20,4},{24,8},{28,12},{1,17},{... | collective-permute-start | bytes 61448 | tf_op jit(solution)/shard_map/ppermute | solution.py:24
  11.7 27.0 %collective-permute-start.2 = (bf16[5,2048]{1,0:T(8,128)(2,1)}, bf16[5,2048]{1,0:T(8,128)(2,1)}, u32[]{:S(2)}, u32[]{:S(2)}) collective-permute-start(bf16[5,2048]{1,0:T(8,128)(2,1)} %fusion.61), channel_id=1, source_target_pairs={{0,20},{4,16},{8,28},{12,24},{16,4},{20,0},{24,12},{28,8},{1,21},{... | collective-permute-start | bytes 61448 | tf_op jit(solution)/shard_map/ppermute | solution.py:24
  20.1 13.5 %collective-permute-start.6 = (bf16[256,1024]{1,0:T(8,128)(2,1)}, bf16[256,1024]{1,0:T(8,128)(2,1)}, u32[]{:S(2)}, u32[]{:S(2)}) collective-permute-start(bf16[256,1024]{1,0:T(8,128)(2,1)} %broadcast_select_fusion.11), channel_id=1, source_target_pairs={{0,4},{4,0},{8,12},{12,8},{16,20},{20,16},{24,28},{28,24},{1,5},{5... | collective-permute-start | bytes 1572872 | tf_op jit(solution)/shard_map/ppermute | solution.py:24
  22.6 16.0 %collective-permute-start.3 = (bf16[32,2048]{1,0:T(8,128)(2,1)}, bf16[32,2048]{1,0:T(8,128)(2,1)S(1)}, u32[]{:S(2)}, u32[]{:S(2)}) collective-permute-start(bf16[32,2048]{1,0:T(8,128)(2,1)} %convolution_convert_fusion.16), channel_id=1, source_target_pairs={{0,8},{4,12},{8,0},{12,4},{16,24},{20,28},{24,16},{28,20},{1,9},{5... | collective-permute-start | bytes 393224 | tf_op jit(solution)/shard_map/ppermute | solution.py:24
  47.5 17.5 %collective-permute-start.8 = (bf16[256,1408]{1,0:T(8,128)(2,1)}, bf16[256,1408]{1,0:T(8,128)(2,1)}, u32[]{:S(2)}, u32[]{:S(2)}) collective-permute-start(bf16[256,1408]{1,0:T(8,128)(2,1)} %copy.62), channel_id=1, source_target_pairs={{0,4},{4,0},{8,12},{12,8},{16,20},{20,16},{24,28},{28,24},{1,5},{5... | collective-permute-start | bytes 2162696 | tf_op jit(solution)/shard_map/ppermute | solution.py:24
  50.2 17.2 %collective-permute-start.7 = (bf16[5,2048]{1,0:T(8,128)(2,1)S(1)}, bf16[5,2048]{1,0:T(8,128)(2,1)S(1)}, u32[]{:S(2)}, u32[]{:S(2)}) collective-permute-start(bf16[5,2048]{1,0:T(8,128)(2,1)S(1)} %add_add_fusion), channel_id=1, source_target_pairs={{0,8},{4,12},{8,0},{12,4},{16,24},{20,28},{24,16},{28,20},{1,9},{5... | collective-permute-start | bytes 61448 | tf_op jit(solution)/shard_map/ppermute | solution.py:24
  52.3 200.7 %all-gather.6.cloned.1.call-start = ((), (), s32[]{:S(2)}) async-start(), calls=%async_computation.4 | async-start | bytes 7208960 | tf_op jit(solution)/shard_map/all_gather | solution.py:218
  69.0 12.3 %collective-permute-start.10 = (bf16[128,2048]{1,0:T(8,128)(2,1)S(1)}, bf16[128,2048]{1,0:T(8,128)(2,1)}, u32[]{:S(2)}, u32[]{:S(2)}) collective-permute-start(bf16[128,2048]{1,0:T(8,128)(2,1)S(1)} %fusion.21), channel_id=1, source_target_pairs={{0,4},{4,0},{8,12},{12,8},{16,20},{20,16},{24,28},{28,24},{1,5},{5... | collective-permute-start | bytes 1572872 | tf_op jit(solution)/shard_map/ppermute | solution.py:24
  99.5 31.9 %collective-permute-start.14 = (bf16[512,2048]{1,0:T(8,128)(2,1)S(1)}, bf16[512,2048]{1,0:T(8,128)(2,1)}, u32[]{:S(2)}, u32[]{:S(2)}) collective-permute-start(bf16[512,2048]{1,0:T(8,128)(2,1)S(1)} %constant_dynamic-update-slice_fusion), channel_id=1, source_target_pairs={{0,1},{1,0},{2,3},{3,2},{4,5},{5,4},{6,7},{7,6},{8,9},{9,8},{10,11... | collective-permute-start | bytes 6291464 | tf_op jit(solution)/shard_map/ppermute | solution.py:24
  101.1 12.6 %collective-permute-start.15 = (bf16[32,2048]{1,0:T(8,128)(2,1)}, bf16[32,2048]{1,0:T(8,128)(2,1)S(1)}, u32[]{:S(2)}, u32[]{:S(2)}) collective-permute-start(bf16[32,2048]{1,0:T(8,128)(2,1)} %convolution_convert_fusion.12), channel_id=1, source_target_pairs={{0,8},{4,12},{8,0},{12,4},{16,24},{20,28},{24,16},{28,20},{1,9},{5... | collective-permute-start | bytes 393224 | tf_op jit(solution)/shard_map/ppermute | solution.py:24
  101.2 17.8 %collective-permute-start.16 = (bf16[32,2048]{1,0:T(8,128)(2,1)}, bf16[32,2048]{1,0:T(8,128)(2,1)S(1)}, u32[]{:S(2)}, u32[]{:S(2)}) collective-permute-start(bf16[32,2048]{1,0:T(8,128)(2,1)} %convolution_convert_fusion.11), channel_id=1, source_target_pairs={{0,16},{4,20},{8,24},{12,28},{16,0},{20,4},{24,8},{28,12},{1,17},{... | collective-permute-start | bytes 393224 | tf_op jit(solution)/shard_map/ppermute | solution.py:24
  103.9 27.5 %collective-permute-start.17 = (bf16[32,2048]{1,0:T(8,128)(2,1)}, bf16[32,2048]{1,0:T(8,128)(2,1)S(1)}, u32[]{:S(2)}, u32[]{:S(2)}) collective-permute-start(bf16[32,2048]{1,0:T(8,128)(2,1)} %convolution_convert_fusion.10), channel_id=1, source_target_pairs={{0,24},{4,28},{8,16},{12,20},{16,8},{20,12},{24,0},{28,4},{1,25},{... | collective-permute-start | bytes 393224 | tf_op jit(solution)/shard_map/ppermute | solution.py:24
  143.6 21.3 %collective-permute-start.18 = (bf16[128,2048]{1,0:T(8,128)(2,1)}, bf16[128,2048]{1,0:T(8,128)(2,1)}, u32[]{:S(2)}, u32[]{:S(2)}) collective-permute-start(bf16[128,2048]{1,0:T(8,128)(2,1)} %maximum_select_fusion), channel_id=1, source_target_pairs={{0,2},{1,3},{2,0},{3,1},{4,6},{5,7},{6,4},{7,5},{8,10},{9,11},{10,... | collective-permute-start | bytes 1572872 | tf_op jit(solution)/shard_map/ppermute | solution.py:24
  145.1 19.8 %collective-permute-start.19 = (bf16[128,2048]{1,0:T(8,128)(2,1)}, bf16[128,2048]{1,0:T(8,128)(2,1)}, u32[]{:S(2)}, u32[]{:S(2)}) collective-permute-start(bf16[128,2048]{1,0:T(8,128)(2,1)} %maximum_select_fusion), channel_id=1, source_target_pairs={{0,4},{4,0},{8,12},{12,8},{16,20},{20,16},{24,28},{28,24},{1,5},{5... | collective-permute-start | bytes 1572872 | tf_op jit(solution)/shard_map/ppermute | solution.py:24
  148.1 175.3 %all-gather.8.cloned.1.call-start = ((), (), s32[]{:S(2)}) async-start(), calls=%async_computation.5 | async-start | bytes 3932160 | tf_op jit(solution)/shard_map/all_gather | solution.py:218
  164.9 11.8 %collective-permute-start.20 = (bf16[512,2048]{1,0:T(8,128)(2,1)S(1)}, bf16[512,2048]{1,0:T(8,128)(2,1)S(1)}, u32[]{:S(2)}, u32[]{:S(2)}) collective-permute-start(bf16[512,2048]{1,0:T(8,128)(2,1)S(1)} %convolution_convert_fusion.3), channel_id=1, source_target_pairs={{0,1},{1,0},{2,3},{3,2},{4,5},{5,4},{6,7},{7,6},{8,9},{9,8},{10,11... | collective-permute-start | bytes 6291464 | tf_op jit(solution)/shard_map/ppermute | solution.py:24
  185.9 16.3 %collective-permute-start.27 = (bf16[512,2048]{1,0:T(8,128)(2,1)S(1)}, bf16[512,2048]{1,0:T(8,128)(2,1)S(1)}, u32[]{:S(2)}, u32[]{:S(2)}) collective-permute-start(bf16[512,2048]{1,0:T(8,128)(2,1)S(1)} %constant_dynamic-update-slice_fusion.7), channel_id=1, source_target_pairs={{0,1},{1,0},{2,3},{3,2},{4,5},{5,4},{6,7},{7,6},{8,9},{9,8},{10,11... | collective-permute-start | bytes 6291464 | tf_op jit(solution)/shard_map/ppermute | solution.py:24
  186.5 14.4 %collective-permute-start.26 = (bf16[128,2048]{1,0:T(8,128)(2,1)S(1)}, bf16[128,2048]{1,0:T(8,128)(2,1)S(1)}, u32[]{:S(2)}, u32[]{:S(2)}) collective-permute-start(bf16[128,2048]{1,0:T(8,128)(2,1)S(1)} %pad_maximum_fusion.12), channel_id=1, source_target_pairs={{0,2},{1,3},{2,0},{3,1},{4,6},{5,7},{6,4},{7,5},{8,10},{9,11},{10,... | collective-permute-start | bytes 1572872 | tf_op jit(solution)/shard_map/ppermute | solution.py:24
  188.1 14.1 %collective-permute-start.25 = (bf16[128,2048]{1,0:T(8,128)(2,1)S(1)}, bf16[128,2048]{1,0:T(8,128)(2,1)S(1)}, u32[]{:S(2)}, u32[]{:S(2)}) collective-permute-start(bf16[128,2048]{1,0:T(8,128)(2,1)S(1)} %pad_maximum_fusion.11), channel_id=1, source_target_pairs={{0,4},{4,0},{8,12},{12,8},{16,20},{20,16},{24,28},{28,24},{1,5},{5... | collective-permute-start | bytes 1572872 | tf_op jit(solution)/shard_map/ppermute | solution.py:24
  203.9 13.3 %collective-permute-start.28 = (bf16[128,2048]{1,0:T(8,128)(2,1)S(1)}, bf16[128,2048]{1,0:T(8,128)(2,1)S(1)}, u32[]{:S(2)}, u32[]{:S(2)}) collective-permute-start(bf16[128,2048]{1,0:T(8,128)(2,1)S(1)} %add_convert_fusion.1), channel_id=1, source_target_pairs={{0,2},{1,3},{2,0},{3,1},{4,6},{5,7},{6,4},{7,5},{8,10},{9,11},{10,... | collective-permute-start | bytes 1572872 | tf_op jit(solution)/shard_map/ppermute | solution.py:24
  204.5 13.1 %collective-permute-start.29 = (bf16[128,2048]{1,0:T(8,128)(2,1)S(1)}, bf16[128,2048]{1,0:T(8,128)(2,1)S(1)}, u32[]{:S(2)}, u32[]{:S(2)}) collective-permute-start(bf16[128,2048]{1,0:T(8,128)(2,1)S(1)} %add_convert_fusion.1), channel_id=1, source_target_pairs={{0,4},{4,0},{8,12},{12,8},{16,20},{20,16},{24,28},{28,24},{1,5},{5... | collective-permute-start | bytes 1572872 | tf_op jit(solution)/shard_map/ppermute | solution.py:24
  261.0 133.8 %reduce-scatter.4.cloned.1.call-start = ((), (), s32[]{:S(2)}) async-start(), calls=%async_computation.6 | async-start | bytes 3932160 | tf_op jit(solution)/shard_map/reduce_scatter | solution.py:221
  334.4 188.0 %reduce-scatter.6.cloned.1.call-start = ((), (), s32[]{:S(2)}) async-start(), calls=%async_computation.7 | async-start | bytes 7208960 | tf_op jit(solution)/shard_map/reduce_scatter | solution.py:221
  399.6 13.8 %collective-permute-start.37 = (bf16[128,2048]{1,0:T(8,128)(2,1)S(1)}, bf16[128,2048]{1,0:T(8,128)(2,1)S(1)}, u32[]{:S(2)}, u32[]{:S(2)}) collective-permute-start(bf16[128,2048]{1,0:T(8,128)(2,1)S(1)} %pad_maximum_fusion.14), channel_id=1, source_target_pairs={{0,2},{1,3},{2,0},{3,1},{4,6},{5,7},{6,4},{7,5},{8,10},{9,11},{10,... | collective-permute-start | bytes 1572872 | tf_op jit(solution)/shard_map/ppermute | solution.py:24
  401.2 13.5 %collective-permute-start.36 = (bf16[128,2048]{1,0:T(8,128)(2,1)S(1)}, bf16[128,2048]{1,0:T(8,128)(2,1)S(1)}, u32[]{:S(2)}, u32[]{:S(2)}) collective-permute-start(bf16[128,2048]{1,0:T(8,128)(2,1)S(1)} %pad_maximum_fusion.13), channel_id=1, source_target_pairs={{0,4},{4,0},{8,12},{12,8},{16,20},{20,16},{24,28},{28,24},{1,5},{5... | collective-permute-start | bytes 1572872 | tf_op jit(solution)/shard_map/ppermute | solution.py:24
  414.7 18.6 %collective-permute-start.40 = (bf16[512,2048]{1,0:T(8,128)(2,1)}, bf16[512,2048]{1,0:T(8,128)(2,1)}, u32[]{:S(2)}, u32[]{:S(2)}) collective-permute-start(bf16[512,2048]{1,0:T(8,128)(2,1)} %convolution_convert_fusion.5), channel_id=1, source_target_pairs={{0,1},{1,0},{2,3},{3,2},{4,5},{5,4},{6,7},{7,6},{8,9},{9,8},{10,11... | collective-permute-start | bytes 6291464 | tf_op jit(solution)/shard_map/ppermute | solution.py:24
  418.3 14.6 %collective-permute-start.38 = (bf16[128,2048]{1,0:T(8,128)(2,1)}, bf16[128,2048]{1,0:T(8,128)(2,1)}, u32[]{:S(2)}, u32[]{:S(2)}) collective-permute-start(bf16[128,2048]{1,0:T(8,128)(2,1)} %get-tuple-element.333), channel_id=1, source_target_pairs={{0,2},{1,3},{2,0},{3,1},{4,6},{5,7},{6,4},{7,5},{8,10},{9,11},{10,... | collective-permute-start | bytes 1572872 | tf_op jit(solution)/shard_map/ppermute | solution.py:24
  418.9 14.4 %collective-permute-start.39 = (bf16[128,2048]{1,0:T(8,128)(2,1)}, bf16[128,2048]{1,0:T(8,128)(2,1)}, u32[]{:S(2)}, u32[]{:S(2)}) collective-permute-start(bf16[128,2048]{1,0:T(8,128)(2,1)} %get-tuple-element.333), channel_id=1, source_target_pairs={{0,4},{4,0},{8,12},{12,8},{16,20},{20,16},{24,28},{28,24},{1,5},{5... | collective-permute-start | bytes 1572872 | tf_op jit(solution)/shard_map/ppermute | solution.py:24
  420.4 227.0 %reduce-scatter.8.cloned.1.call-start = ((), (), s32[]{:S(2)}) async-start(), calls=%async_computation.8 | async-start | bytes 5242880 | tf_op jit(solution)/shard_map/reduce_scatter | solution.py:221
  454.5 20.3 %collective-permute-start.47 = (bf16[128,2048]{1,0:T(8,128)(2,1)S(1)}, bf16[128,2048]{1,0:T(8,128)(2,1)S(1)}, u32[]{:S(2)}, u32[]{:S(2)}) collective-permute-start(bf16[128,2048]{1,0:T(8,128)(2,1)S(1)} %pad_maximum_fusion.16), channel_id=1, source_target_pairs={{0,2},{1,3},{2,0},{3,1},{4,6},{5,7},{6,4},{7,5},{8,10},{9,11},{10,... | collective-permute-start | bytes 1572872 | tf_op jit(solution)/shard_map/ppermute | solution.py:24
  455.2 19.6 %collective-permute-start.46 = (bf16[128,2048]{1,0:T(8,128)(2,1)S(1)}, bf16[128,2048]{1,0:T(8,128)(2,1)S(1)}, u32[]{:S(2)}, u32[]{:S(2)}) collective-permute-start(bf16[128,2048]{1,0:T(8,128)(2,1)S(1)} %pad_maximum_fusion.15), channel_id=1, source_target_pairs={{0,4},{4,0},{8,12},{12,8},{16,20},{20,16},{24,28},{28,24},{1,5},{5... | collective-permute-start | bytes 1572872 | tf_op jit(solution)/shard_map/ppermute | solution.py:24
  474.8 13.7 %collective-permute-start.48 = (bf16[512,2048]{1,0:T(8,128)(2,1)}, bf16[512,2048]{1,0:T(8,128)(2,1)}, u32[]{:S(2)}, u32[]{:S(2)}) collective-permute-start(bf16[512,2048]{1,0:T(8,128)(2,1)} %convolution_convert_fusion.4), channel_id=1, source_target_pairs={{0,1},{1,0},{2,3},{3,2},{4,5},{5,4},{6,7},{7,6},{8,9},{9,8},{10,11... | collective-permute-start | bytes 6291464 | tf_op jit(solution)/shard_map/ppermute | solution.py:24
  507.0 13.4 %collective-permute-start.52 = (bf16[128,2048]{1,0:T(8,128)(2,1)S(1)}, bf16[128,2048]{1,0:T(8,128)(2,1)}, u32[]{:S(2)}, u32[]{:S(2)}) collective-permute-start(bf16[128,2048]{1,0:T(8,128)(2,1)S(1)} %pad_maximum_fusion.18), channel_id=1, source_target_pairs={{0,2},{1,3},{2,0},{3,1},{4,6},{5,7},{6,4},{7,5},{8,10},{9,11},{10,... | collective-permute-start | bytes 1572872 | tf_op jit(solution)/shard_map/ppermute | solution.py:24
  508.1 12.7 %collective-permute-start.51 = (bf16[128,2048]{1,0:T(8,128)(2,1)S(1)}, bf16[128,2048]{1,0:T(8,128)(2,1)S(1)}, u32[]{:S(2)}, u32[]{:S(2)}) collective-permute-start(bf16[128,2048]{1,0:T(8,128)(2,1)S(1)} %pad_maximum_fusion.17), channel_id=1, source_target_pairs={{0,4},{4,0},{8,12},{12,8},{16,20},{20,16},{24,28},{28,24},{1,5},{5... | collective-permute-start | bytes 1572872 | tf_op jit(solution)/shard_map/ppermute | solution.py:24
  523.2 12.3 %collective-permute-start.60 = (bf16[256,704]{1,0:T(8,128)(2,1)}, bf16[256,704]{1,0:T(8,128)(2,1)}, u32[]{:S(2)}, u32[]{:S(2)}) collective-permute-start(bf16[256,704]{1,0:T(8,128)(2,1)} %broadcast_select_fusion.29), channel_id=1, source_target_pairs={{0,4},{4,0},{8,12},{12,8},{16,20},{20,16},{24,28},{28,24},{1,5},{5... | collective-permute-start | bytes 1081352 | tf_op jit(solution)/shard_map/ppermute | solution.py:24
  526.9 23.0 %collective-permute-start.59 = (bf16[256,1408]{1,0:T(8,128)(2,1)}, bf16[256,1408]{1,0:T(8,128)(2,1)}, u32[]{:S(2)}, u32[]{:S(2)}) collective-permute-start(bf16[256,1408]{1,0:T(8,128)(2,1)} %broadcast_select_fusion.1), channel_id=1, source_target_pairs={{0,4},{4,0},{8,12},{12,8},{16,20},{20,16},{24,28},{28,24},{1,5},{5... | collective-permute-start | bytes 2162696 | tf_op jit(solution)/shard_map/ppermute | solution.py:24
  531.5 21.3 %collective-permute-start.54 = (bf16[32,2048]{1,0:T(8,128)(2,1)S(1)}, bf16[32,2048]{1,0:T(8,128)(2,1)S(1)}, u32[]{:S(2)}, u32[]{:S(2)}) collective-permute-start(bf16[32,2048]{1,0:T(8,128)(2,1)S(1)} %get-tuple-element.491), channel_id=1, source_target_pairs={{0,16},{4,20},{8,24},{12,28},{16,0},{20,4},{24,8},{28,12},{1,17},{... | collective-permute-start | bytes 393224 | tf_op jit(solution)/shard_map/ppermute | solution.py:24
  532.8 29.9 %collective-permute-start.55 = (bf16[32,2048]{1,0:T(8,128)(2,1)S(1)}, bf16[32,2048]{1,0:T(8,128)(2,1)S(1)}, u32[]{:S(2)}, u32[]{:S(2)}) collective-permute-start(bf16[32,2048]{1,0:T(8,128)(2,1)S(1)} %get-tuple-element.490), channel_id=1, source_target_pairs={{0,24},{4,28},{8,16},{12,20},{16,8},{20,12},{24,0},{28,4},{1,25},{... | collective-permute-start | bytes 393224 | tf_op jit(solution)/shard_map/ppermute | solution.py:24
  535.5 27.2 %collective-permute-start.56 = (bf16[32,2048]{1,0:T(8,128)(2,1)S(1)}, bf16[32,2048]{1,0:T(8,128)(2,1)S(1)}, u32[]{:S(2)}, u32[]{:S(2)}) collective-permute-start(bf16[32,2048]{1,0:T(8,128)(2,1)S(1)} %copy-done.88), channel_id=1, source_target_pairs={{0,8},{4,12},{8,0},{12,4},{16,24},{20,28},{24,16},{28,20},{1,9},{5... | collective-permute-start | bytes 393224 | tf_op jit(solution)/shard_map/ppermute | solution.py:24
  538.3 33.5 %collective-permute-start.57 = (bf16[32,2048]{1,0:T(8,128)(2,1)S(1)}, bf16[32,2048]{1,0:T(8,128)(2,1)S(1)}, u32[]{:S(2)}, u32[]{:S(2)}) collective-permute-start(bf16[32,2048]{1,0:T(8,128)(2,1)S(1)} %copy-done.87), channel_id=1, source_target_pairs={{0,16},{4,20},{8,24},{12,28},{16,0},{20,4},{24,8},{28,12},{1,17},{... | collective-permute-start | bytes 393224 | tf_op jit(solution)/shard_map/ppermute | solution.py:24
  549.9 34.9 %collective-permute-start.58 = (bf16[32,2048]{1,0:T(8,128)(2,1)S(1)}, bf16[32,2048]{1,0:T(8,128)(2,1)S(1)}, u32[]{:S(2)}, u32[]{:S(2)}) collective-permute-start(bf16[32,2048]{1,0:T(8,128)(2,1)S(1)} %copy-done.86), channel_id=1, source_target_pairs={{0,24},{4,28},{8,16},{12,20},{16,8},{20,12},{24,0},{28,4},{1,25},{... | collective-permute-start | bytes 393224 | tf_op jit(solution)/shard_map/ppermute | solution.py:24
  597.4 18.3 %collective-permute-start.71 = (f32[768]{0:T(1024)S(1)}, f32[768]{0:T(1024)S(1)}, u32[]{:S(2)}, u32[]{:S(2)}) collective-permute-start(f32[768]{0:T(1024)S(1)} %slice_reduce_fusion), channel_id=1, source_target_pairs={{0,16},{4,20},{8,24},{12,28},{16,0},{20,4},{24,8},{28,12},{1,17},{... | collective-permute-start | bytes 9224 | tf_op jit(solution)/shard_map/ppermute | solution.py:24
  598.5 25.2 %collective-permute-start.63 = (f32[4,2048]{1,0:T(4,128)}, f32[4,2048]{1,0:T(4,128)}, u32[]{:S(2)}, u32[]{:S(2)}) collective-permute-start(f32[4,2048]{1,0:T(4,128)} %pad_maximum_fusion.19), channel_id=1, source_target_pairs={{0,1},{1,0},{2,3},{3,2},{4,5},{5,4},{6,7},{7,6},{8,9},{9,8},{10,11... | collective-permute-start | bytes 98312 | tf_op jit(solution)/shard_map/ppermute | solution.py:24
  600.3 24.3 %collective-permute-start.62 = (bf16[128,2048]{1,0:T(8,128)(2,1)S(1)}, bf16[128,2048]{1,0:T(8,128)(2,1)S(1)}, u32[]{:S(2)}, u32[]{:S(2)}) collective-permute-start(bf16[128,2048]{1,0:T(8,128)(2,1)S(1)} %convolution_convert_fusion.8), channel_id=1, source_target_pairs={{0,2},{1,3},{2,0},{3,1},{4,6},{5,7},{6,4},{7,5},{8,10},{9,11},{10,... | collective-permute-start | bytes 1572872 | tf_op jit(solution)/shard_map/ppermute | solution.py:24
  602.3 23.3 %collective-permute-start.61 = (bf16[128,2048]{1,0:T(8,128)(2,1)S(1)}, bf16[128,2048]{1,0:T(8,128)(2,1)}, u32[]{:S(2)}, u32[]{:S(2)}) collective-permute-start(bf16[128,2048]{1,0:T(8,128)(2,1)S(1)} %convolution_convert_fusion.9), channel_id=1, source_target_pairs={{0,2},{1,3},{2,0},{3,1},{4,6},{5,7},{6,4},{7,5},{8,10},{9,11},{10,... | collective-permute-start | bytes 1572872 | tf_op jit(solution)/shard_map/ppermute | solution.py:24
  628.3 15.3 %collective-permute-start.65 = (bf16[256,2048]{1,0:T(8,128)(2,1)S(1)}, bf16[256,2048]{1,0:T(8,128)(2,1)S(1)}, u32[]{:S(2)}, u32[]{:S(2)}) collective-permute-start(bf16[256,2048]{1,0:T(8,128)(2,1)S(1)} %pad_maximum_fusion.6), channel_id=1, source_target_pairs={{0,1},{1,0},{2,3},{3,2},{4,5},{5,4},{6,7},{7,6},{8,9},{9,8},{10,11... | collective-permute-start | bytes 3145736 | tf_op jit(solution)/shard_map/ppermute | solution.py:24
  (166 other events, 1553.9 us)
Sparse Core Ops, SparseCore 0:
  52.4 89.3 all-gather.3
  148.2 104.6 all-gather.5
  261.1 62.2 all-gather.7
  334.5 60.2 reduce-scatter.3
  420.5 101.8 reduce-scatter.5
  529.5 96.1 reduce-scatter.7

commit v3 on v2

--- a/solution.py
+++ b/solution.py
@@ -57,6 +57,10 @@
             kept[k ^ bit] = kept[k ^ bit].astype(f32) + got[place * rows : (place + 1) * rows].astype(f32)
         pieces = kept
     return pieces[0]
+
+
+def added(near, start, stop):
+    return near[0][start:stop] + near[1][start:stop].astype(f32)
 
 
 class Plan:
@@ -173,24 +177,23 @@
 
     def sum_corner(self, near):
         far = self.steps[1:]
+        rows = near[0].shape[0] >> len(far)
         if len(far) != 2:
-            chips = 1 << len(far)
-            rows = near.shape[0] // chips
-            return [scatter({k: near[k * rows : (k + 1) * rows] for k in range(chips)}, far)]
+            return [scatter({k: added(near, k * rows, (k + 1) * rows) for k in range(1 << len(far))}, far)]
         (axis_x, mask_x, _), (axis_z, mask_z, _) = far
-        rows = near.shape[0] // 4
-        half = rows // 2
-        corner = near[3 * rows :].astype(bf16)
-        return [swap(corner[:half], axis_x, mask_x), swap(corner[half:], axis_z, mask_z)]
+        middle = 3 * rows + rows // 2
+        one = added(near, 3 * rows, middle).astype(bf16)
+        two = added(near, middle, 4 * rows).astype(bf16)
+        return [swap(one, axis_x, mask_x), swap(two, axis_z, mask_z)]
 
     def sum_sides(self, near, corner):
         far = self.steps[1:]
         if len(far) != 2:
             return corner
         (axis_x, mask_x, _), (axis_z, mask_z, _) = far
-        rows = near.shape[0] // 4
+        rows = near[0].shape[0] // 4
         half = rows // 2
-        one, two = near[rows : 2 * rows], near[2 * rows : 3 * rows]
+        one, two = added(near, rows, 2 * rows), added(near, 2 * rows, 3 * rows)
         for_z = jnp.concatenate([one[:half] + corner[0].astype(f32), one[half:]], 0).astype(bf16)
         for_x = jnp.concatenate([two[:half], two[half:] + corner[1].astype(f32)], 0).astype(bf16)
         return [swap(for_z, axis_z, mask_z), swap(for_x, axis_x, mask_x)]
@@ -198,8 +201,8 @@
     def sum_end(self, near, sides):
         if len(self.steps) != 3:
             return sides[0]
-        rows = near.shape[0] // 4
-        return near[:rows] + sides[0].astype(f32) + sides[1].astype(f32)
+        rows = near[0].shape[0] // 4
+        return added(near, 0, rows) + sides[0].astype(f32) + sides[1].astype(f32)
 
     def spread_mine(self, mine, axis):
         got = [mine[0]] + [swap(mine[j], "seq", self.inner_mask(j)) for j in range(1, self.parts)]
@@ -434,6 +437,7 @@
     average_down,
 ):
     plan = Plan(inputs.shape[1])
+    gate_master, down_master = gate_weight, down_weight
     groups, parts, rows = plan.groups, plan.parts, plan.rows
     block_len, _, width = inputs.shape
     tp_width = entry_weight.shape[2]
@@ -488,9 +492,6 @@
     def turned_columns(array, h):
         return array[:, h * hidden : (h + 1) * hidden].astype(bf16).T
 
-    small_got = over_masks(small, first_masks)
-    outgoing = plan.outgoing_rows(inputs)
-    resid = plan.over_groups(outgoing)
     attn_mine = pick(
         [
             jnp.concatenate(
@@ -501,18 +502,26 @@
         plan.part_flags,
     )
     attn_block = plan.spread_mine(attn_mine, 0)
+    outgoing = plan.outgoing_rows(inputs)
+    attn_block, outgoing, small, gate_weight, down_weight, cotangent, position = hold(
+        attn_block, outgoing, small, gate_weight, down_weight, cotangent, position
+    )
+
+    w_attn = plan.all_blocks(attn_block)
+    small_got = over_masks(small, first_masks)
+    resid = plan.over_groups(outgoing)
     gate_mine = pick([columns(gate_weight, h, hidden) for h in range(parts)], plan.part_flags)
-    small, small_got, resid, attn_block, cotangent, gate_mine, position, down_weight = hold(
-        small, small_got, resid, attn_block, cotangent, gate_mine, position, down_weight
-    )
-
-    w_attn = plan.all_blocks(attn_block)
+    gate_block = plan.spread_mine(gate_mine, 0)
+    small, small_got, resid, gate_block, cotangent, down_weight, position = hold(
+        small, small_got, resid, gate_block, cotangent, down_weight, position
+    )
+
     small = total_of(small, small_got)
     small_got = over_masks(small, [last_mask])
-    gate_block = plan.spread_mine(gate_mine, 0)
-    outgoing = plan.outgoing_rows(cotangent)
-    small, small_got, resid, gate_block, outgoing, position, down_weight = hold(
-        small, small_got, resid, gate_block, outgoing, position, down_weight
+    down_mine = pick([columns(down_weight, h, hidden) for h in range(parts)], plan.part_flags)
+    down_block = plan.spread_mine(down_mine, 0)
+    small, small_got, down_block, gate_block, cotangent = hold(
+        small, small_got, down_block, gate_block, cotangent
     )
 
     small = total_of(small, small_got)
@@ -523,27 +532,20 @@
     sides = plan.chips_sides(low_first)
     row_position = position.reshape(length)
     tables = turning(row_position) + (row_position[:, None], row_position[None, :])
-    down_mine = pick([columns(down_weight, h, hidden) for h in range(parts)], plan.part_flags)
-    low_first, sides, tables, down_mine, outgoing, gate_block = hold(
-        low_first, sides, tables, down_mine, outgoing, gate_block
-    )
-
+    blank = jnp.zeros((down_block.shape[0], -(2 * hidden + hidden) % 128), bf16)
+    ffn_block = jnp.concatenate([gate_block, down_block, blank], 1)
+    low_first, sides, tables, ffn_block, cotangent = hold(low_first, sides, tables, ffn_block, cotangent)
     corner = plan.chips_corner(low_first, sides)
-    down_block = plan.spread_mine(down_mine, 0)
-    low_first, sides, corner, down_block, outgoing = hold(low_first, sides, corner, down_block, outgoing)
+    outgoing = plan.outgoing_rows(cotangent)
+    low_first, sides, corner, outgoing = hold(low_first, sides, corner, outgoing)
     near = plan.chips_near(low_first, sides, corner)
     other = plan.swap_core(near)
+    a_first = jnp.concatenate([near, other], 0)
+    a_first, w_attn, ffn_block, outgoing = hold(a_first, w_attn, ffn_block, outgoing)
+    w_ffn = plan.all_blocks(ffn_block)
     grad_y = plan.over_groups(outgoing)
-    near, other, grad_y, w_attn, gate_block, down_block = hold(
-        near, other, grad_y, w_attn, gate_block, down_block
-    )
-    a_first = jnp.concatenate([near, other], 0)
-    w_gate = plan.all_blocks(gate_block)
     own_position = jnp.broadcast_to(position[0][:, None, :], (groups, rows, quarter))
     real = (own_position < lens[None, :, None]).reshape(share, 1)
-    grad_y = plan.arranged(jnp.concatenate(grad_y, 0))
-    grad_y = jnp.where(real, grad_y, 0)
-    y_sides = plan.chips_sides(grad_y)
 
     w_entry = w_attn[:, : 3 * head_width]
     w_output = w_attn[:, 3 * head_width :]
@@ -568,35 +570,38 @@
 
     half = plan.total // 2
     far_product = output_product(half, plan.total).astype(bf16)
-    far_product, grad_y, y_sides, down_block = hold(far_product, grad_y, y_sides, down_block)
+    far_product, grad_y = hold(far_product, grad_y)
 
     got = plan.swap_core(far_product)
     product = output_product(0, half)
+    grad_y = plan.arranged(jnp.concatenate(grad_y, 0))
+    grad_y = jnp.where(real, grad_y, 0)
+    product, got, grad_y = hold(product, got, grad_y)
+
+    near = (product, got)
+    corner = plan.sum_corner(near)
+    y_sides = plan.chips_sides(grad_y)
+    near, corner, y_sides = hold(near, corner, y_sides)
+    sides = plan.sum_sides(near, corner)
     y_corner = plan.chips_corner(grad_y, y_sides)
-    product, got, y_corner = hold(product, got, y_corner)
-
-    near = product + got.astype(f32)
-    corner = plan.sum_corner(near)
-    y_near = plan.chips_near(grad_y, y_sides, y_corner)
-    near, corner, y_near = hold(near, corner, y_near)
-    sides = plan.sum_sides(near, corner)
-    y_other = plan.swap_core(y_near)
-    near, sides, y_near, y_other, down_block = hold(near, sides, y_near, y_other, down_block)
+    near, sides, y_corner = hold(near, sides, y_corner)
 
     second = resid + plan.sum_end(near, sides)
     h_second, n_second, i_second = layer_norm(second, gains[2], gains[3])
     low_second = h_second.astype(bf16)
     sides = plan.chips_sides(low_second)
+    y_near = plan.chips_near(grad_y, y_sides, y_corner)
+    y_other = plan.swap_core(y_near)
+    second, low_second, sides, y_near, y_other = hold(second, low_second, sides, y_near, y_other)
+    corner = plan.chips_corner(low_second, sides)
     grad_y_all = jnp.concatenate([y_near, y_other], 0)
-    second, low_second, sides, grad_y_all = hold(second, low_second, sides, grad_y_all)
-    corner = plan.chips_corner(low_second, sides)
-    low_second, sides, corner, w_gate, down_block = hold(low_second, sides, corner, w_gate, down_block)
-    w_down = plan.all_blocks(down_block)
+    low_second, sides, corner, grad_y_all = hold(low_second, sides, corner, grad_y_all)
     near = plan.chips_near(low_second, sides, corner)
     other = plan.swap_core(near)
-    near, other = hold(near, other)
-
     a_second = jnp.concatenate([near, other], 0)
+    a_second, w_ffn = hold(a_second, w_ffn)
+
+    w_gate = w_ffn[:, : 2 * hidden]
     gated = jnp.einsum("td,df->tf", a_second, w_gate, preferred_element_type=f32)
     gate = gated[:, :hidden]
     upper = gated[:, hidden:]
@@ -604,7 +609,8 @@
     active_gate = gate * sigma
     hid = (active_gate * upper).astype(bf16)
     grad_down = jnp.einsum("td,tf->df", grad_y_all, hid, preferred_element_type=f32).astype(bf16)
-    hid, grad_down, w_down = hold(hid, grad_down, w_down)
+    hid, grad_down, w_ffn = hold(hid, grad_down, w_ffn)
+    w_down = w_ffn[:, 2 * hidden : 3 * hidden]
     down_sum = plan.sum_blocks(grad_down)
     grad_hidden = jnp.einsum(
         "td,df->tf", grad_y_all, w_down, preferred_element_type=f32
@@ -624,13 +630,13 @@
 
     got = plan.swap_core(far_product)
     product = gate_product(0, half)
-    product, got, a_second, hid, grad_gated = hold(product, got, a_second, hid, grad_gated)
-
-    near = product + got.astype(f32)
+    grad_gate = jnp.einsum("td,tf->df", a_second, grad_gated, preferred_element_type=f32).astype(bf16)
+    product, got, hid, grad_gate, down_sum = hold(product, got, hid, grad_gate, down_sum)
+    gate_sum = plan.sum_blocks(grad_gate)
+
+    near = (product, got)
     corner = plan.sum_corner(near)
-    grad_gate = jnp.einsum("td,tf->df", a_second, grad_gated, preferred_element_type=f32).astype(bf16)
-    near, corner, grad_gate, hid, down_sum = hold(near, corner, grad_gate, hid, down_sum)
-    gate_sum = plan.sum_blocks(grad_gate)
+    near, corner, hid, down_sum = hold(near, corner, hid, down_sum)
     sides = plan.sum_sides(near, corner)
     out_far = down_product(half, plan.total).astype(bf16)
     near, sides, out_far, hid, down_sum = hold(near, sides, out_far, hid, down_sum)
@@ -644,7 +650,7 @@
     low_grad, sides, out_near, out_got, grad_h2, grad_second = hold(
         low_grad, sides, out_near, out_got, grad_h2, grad_second
     )
-    out_near = out_near + out_got.astype(f32)
+    out_near = (out_near, out_got)
     corner = plan.chips_corner(low_grad, sides)
     out_corner = plan.sum_corner(out_near)
     low_grad, sides, corner, out_corner, out_near = hold(low_grad, sides, corner, out_corner, out_near)
@@ -678,41 +684,35 @@
         ],
         1,
     )
-    product, got, grad_attn, bias_sum, down_sum = hold(product, got, grad_attn, bias_sum, down_sum)
-
-    near = product + got.astype(f32)
-    corner = plan.sum_corner(near)
-    near, corner, bias_sum, down_sum, grad_attn = hold(near, corner, bias_sum, down_sum, grad_attn)
-    sides = plan.sum_sides(near, corner)
+    bias_sum = jnp.sum(bias_sum[:, 0], 0, keepdims=True)
+    bias_got = over_masks(bias_sum, plan.outer)
     result = second + plan.sum_end(out_near, out_sides)
     out_returning = plan.returning_rows(result.astype(bf16))
-    near, sides, out_returning, bias_sum, down_sum, gate_sum, grad_attn = hold(
-        near, sides, out_returning, bias_sum, down_sum, gate_sum, grad_attn
+    product, got, grad_attn, bias_sum, bias_got, down_sum, out_returning, gate_sum = hold(
+        product, got, grad_attn, bias_sum, bias_got, down_sum, out_returning, gate_sum
     )
     attn_sum = plan.sum_blocks(grad_attn)
+
+    bias_sum = total_of(bias_sum, bias_got)
+    near = (product, got)
+    corner = plan.sum_corner(near)
+    bias_got = [swap(bias_sum, "seq", plan.inner_mask(j)) for j in range(1, parts)]
+    near, corner, bias_sum, bias_got, down_sum, gate_sum, out_returning = hold(
+        near, corner, bias_sum, bias_got, down_sum, gate_sum, out_returning
+    )
+    sides = plan.sum_sides(near, corner)
+    out_back = plan.over_groups(out_returning)
+    near, sides, out_back, down_sum, gate_sum = hold(near, sides, out_back, down_sum, gate_sum)
+
+    def along_tp(own):
+        return gather(own, [("tp", m, m) for m in plan.tp_masks[:0:-1]])
 
     grad_h1 = plan.sum_end(near, sides)
     grad_input = grad_second + norm_back(grad_h1, n_first, i_first, gains[0])
     back = plan.over_groups(plan.returning_rows(grad_input.astype(bf16)))
-    out_back = plan.over_groups(out_returning)
-    gate_home = plan.collect_home(gate_sum)
-    down_home = plan.collect_home(down_sum)
-    back, out_back, grad_h1, bias_sum, gate_home, down_home = hold(
-        back, out_back, grad_h1, bias_sum, gate_home, down_home
-    )
-
-    def along_tp(own, steps):
-        pieces = {0: own}
-        for mask in steps:
-            for k in sorted(pieces):
-                pieces[k | mask] = swap(pieces[k], "tp", mask)
-        return pieces
-
-    own = plan.returned_rows(back, quarter, inputs.shape[1])
-    out_own = plan.returned_rows(out_back, quarter, inputs.shape[1])
-    wide_masks, core_masks = plan.tp_masks[:0:-1], plan.tp_masks[:1]
-    pieces = gather(own, [("tp", m, m) for m in wide_masks])
-    out_pieces = gather(out_own, [("tp", m, m) for m in wide_masks])
+    grad_gate = plan.collect_home(gate_sum)
+    grad_down = plan.collect_home(down_sum)
+    out_pieces = along_tp(plan.returned_rows(out_back, quarter, inputs.shape[1]))
     sums = jnp.stack(
         [
             jnp.sum(grad_h1 * n_first, 0),
@@ -721,10 +721,29 @@
             jnp.sum(grad_h2, 0),
         ]
     )
+    back, grad_gate, grad_down, out_pieces, sums = hold(back, grad_gate, grad_down, out_pieces, sums)
+
+    def ordered_as(grad, *order):
+        return with_layout_constraint(grad, Layout(order))
+
+    beta = min(0.999, (1 + STEP) / (10 + STEP))
+
+    def stepped(index, grad, master, moment, average):
+        grad = grad + decays[index] * master
+        moment = 0.9 * moment + grad
+        weight = master - rates[index] * (grad + 0.9 * moment)
+        return moment, weight, beta * average + (1.0 - beta) * weight, weight.astype(bf16)
+
+    grad_gate = ordered_as(
+        joined([part.reshape(part.shape[0], 2, hidden) for part in grad_gate], -1), 0, 1, 2
+    )
+    gate = stepped(4, grad_gate, gate_master, moment_gate, average_gate)
+    grad_down = ordered_as(joined(grad_down, -1), 0, 1)
+    down = stepped(5, grad_down, down_master, moment_down, average_down)
+    wide_masks, core_masks = plan.tp_masks[:0:-1], plan.tp_masks[:1]
+    pieces = along_tp(plan.returned_rows(back, quarter, inputs.shape[1]))
     for mask in core_masks:
         sums = sums + swap(sums, "tp", mask)
-    grad_gate, grad_down = gate_home, down_home
-    pieces, out_pieces, sums = hold(pieces, out_pieces, sums)
 
     def across_cores(pieces):
         keys = sorted(pieces)
@@ -733,17 +752,12 @@
         pieces = {**pieces, **{k | core_masks[0]: got[i * size : (i + 1) * size] for i, k in enumerate(keys)}}
         return plan.of_tp(pieces).reshape(inputs.shape)
 
+    layer_out = across_cores(out_pieces)
+    pieces, sums, layer_out, gate, down, attn_sum = hold(pieces, sums, layer_out, gate, down, attn_sum)
+
     input_grad = across_cores(pieces)
-    layer_out = across_cores(out_pieces)
-    attn_home = plan.collect_home(attn_sum)
-    grad_entry = [part[:, : 3 * head_width] for part in attn_home]
-    grad_output = [part[:, 3 * head_width :] for part in attn_home]
-
-    bias_sum = jnp.sum(bias_sum[:, 0], 0)
-    for mask in plan.outer:
-        bias_sum = bias_sum + swap(bias_sum, "seq", mask)
-    bias_sum = bias_sum.reshape(3, heads_here, HD)
-    got = [bias_sum] + [swap(bias_sum, "seq", plan.inner_mask(j)) for j in range(1, parts)]
+
+    got = [part.reshape(3, heads_here, HD) for part in [bias_sum] + bias_got]
     bias_sum = joined(pick(got, plan.part_flags), 1)
     grad_bias = lax.dynamic_slice_in_dim(bias_sum, plan.seq * slim, slim, 2)
     for mask in wide_masks:
@@ -754,42 +768,18 @@
     slim = norm_params.shape[1]
     grad_norm = lax.dynamic_slice_in_dim(sums, plan.seq * slim, slim, 1)
 
-    def ordered_as(grad, *order):
-        return with_layout_constraint(grad, Layout(order))
-
-    reduced = (
-        grad_norm,
-        ordered_as(
-            joined([part.reshape(part.shape[0], 3, head_width) for part in grad_entry], -1), 1, 0, 2
-        ),
-        grad_bias,
-        ordered_as(joined(grad_output, -1), 0, 1),
-        ordered_as(
-            joined([part.reshape(part.shape[0], 2, hidden) for part in grad_gate], -1), 0, 1, 2
-        ),
-        ordered_as(joined(grad_down, -1), 0, 1),
-    )
-    masters = (norm_params, entry_weight, entry_bias, output_weight, gate_weight, down_weight)
-    moments = (moment_norm, moment_entry, moment_bias, moment_output, moment_gate, moment_down)
-    averages = (
-        average_norm,
-        average_entry,
-        average_bias,
-        average_output,
-        average_gate,
-        average_down,
-    )
-    beta = min(0.999, (1 + STEP) / (10 + STEP))
-    news, new_weights, smooths, copies = ([], [], [], [])
-    for index in range(6):
-        grad = reduced[index] + decays[index] * masters[index]
-        moment = 0.9 * moments[index] + grad
-        weight = masters[index] - rates[index] * (grad + 0.9 * moment)
-        news.append(moment)
-        new_weights.append(weight)
-        smooths.append(beta * averages[index] + (1.0 - beta) * weight)
-        copies.append(weight.astype(bf16))
-    return (layer_out, input_grad, *news, *new_weights, *smooths, *copies)
+    norm = stepped(0, grad_norm, norm_params, moment_norm, average_norm)
+    bias = stepped(2, grad_bias, entry_bias, moment_bias, average_bias)
+    attn_home = plan.collect_home(attn_sum)
+    grad_entry = [part[:, : 3 * head_width] for part in attn_home]
+    grad_entry = ordered_as(
+        joined([part.reshape(part.shape[0], 3, head_width) for part in grad_entry], -1), 1, 0, 2
+    )
+    grad_output = ordered_as(joined([part[:, 3 * head_width :] for part in attn_home], -1), 0, 1)
+    entry = stepped(1, grad_entry, entry_weight, moment_entry, average_entry)
+    output = stepped(3, grad_output, output_weight, moment_output, average_output)
+    kinds = zip(norm, entry, bias, output, gate, down)
+    return (layer_out, input_grad, *(array for kind in kinds for array in kind))
 
 
 def solution(mesh):

time: 690 us -> 652 us (0.945)
  local copies, waits for them, and re-layouts: 80.8 us -> 61.8 us
  waiting for transfers between devices: 301 us -> 282 us
  matrix products: 85.3 us -> 101 us
  other arithmetic: 100 us -> 92.1 us
    unnamed x291 -> x276, local copies, waits for them, and re-layouts: 44.5 us -> 22.9 us
    another operation x14 -> x10, other arithmetic: 21.2 us -> 3.75 us
    all_gather x3 -> x2, waiting for transfers between devices: 69.6 us -> 55.4 us  [all_blocks(): lax.all_gather(block, 'seq', axis_index_groups=self.lists(), axis=0, tile...]
    select_n x15, other arithmetic: 18.9 us -> 11.7 us  [pick(): parts = [jnp.where(flag, parts[j ^ bit], parts[j]) for j in range(count)]]
    ppermute x74 -> x75, waiting for transfers between devices: 198 us -> 193 us  [swap(): return lax.ppermute(array, axis, pairs)]
    convert_element_type x6 -> x10, other arithmetic: 16.1 us -> 21.2 us  [the longest x6 16.4 us: stepped(): weight.astype(bf16)]
    ppermute x74 -> x75, starting transfers between devices: 76.6 us -> 72 us  [swap(): return lax.ppermute(array, axis, pairs)]
    add x8 -> x10, other arithmetic: 11.6 us -> 16 us  [the longest x6 10.2 us: stepped(): beta * average + (1.0 - beta) * weight]
  transfers between devices with their start and end apart: 80 -> 80, of which waited for: 50 -> 42; matrix products, arithmetic and copies ran while one was open for 31% -> 32% of each run, Pallas kernels for 2% -> 2%
where the time goes in v3:
time: 652 us; the launch traced here: 641 us
  waiting for transfers between devices  282 us (43%)
  matrix products  101 us (15%)
  other arithmetic  92.1 us (14%)
  starting transfers between devices  72.6 us (11%)
  local copies, waits for them, and re-layouts  61.8 us (9%)
  between operations  16.5 us (3%)
  Pallas kernels  15.8 us (2%)
    ppermute x75, waiting for transfers between devices, swap(): return lax.ppermute(array, axis, pairs)  193 us
    ppermute x75, starting transfers between devices, swap(): return lax.ppermute(array, axis, pairs)  72 us
    all_gather x2, waiting for transfers between devices, all_blocks(): lax.all_gather(block, 'seq', axis_index_groups=self.lists(), axis=0, tile...  55.4 us
    reduce_scatter x3, waiting for transfers between devices, sum_blocks(): lax.psum_scatter(product, 'seq', scatter_dimension=0, axis_index_groups=s...  33.2 us
    unnamed x276, local copies, waits for them, and re-layouts  22.9 us
    convert_element_type x6, other arithmetic, stepped(): weight.astype(bf16)  16.4 us
    dot_general x2, matrix products, gate_product(): jnp.einsum('tf,df->td', grad_gated[lo:hi], w_gate, preferred_element_type...  13.4 us
  transfers between devices with their start and end apart: 80, of which 42 were waited for; matrix products, arithmetic and copies ran while one was open for 32% of the time, Pallas kernels for 2%

profile of v3, /device:TPU:16, one launch (start us, length us, event | category | flops | bytes accessed | tf_op | source)
XLA Modules:
  0.0 641.1 jit_solution(3436108802760854136)
XLA Ops:
  23.7 4.8 collective-permute-done
  31.1 3.2 copy.61
  39.0 3.8 collective-permute-start.3
  44.8 10.4 %collective-permute-done.7 = bf16[256,1408]{1,0:T(8,128)(2,1)} collective-permute-done((bf16[256,1408]{1,0:T(8,128)(2,1)}, bf16[256,1408]{1,0:T(8,128)(2,1)}, u32[]{:S(2)}, u32[]{:S(2)}) %collective-permute-start.7) | collective-permute-done | bytes 720928 | tf_op jit(solution)/shard_map/ppermute | solution.py:24
  59.7 11.0 %collective-permute-done.5 = bf16[32,2048]{1,0:T(8,128)(2,1)S(1)} collective-permute-done((bf16[32,2048]{1,0:T(8,128)(2,1)}, bf16[32,2048]{1,0:T(8,128)(2,1)S(1)}, u32[]{:S(2)}, u32[]{:S(2)}) %collective-permute-start.5) | collective-permute-done | bytes 131104 | tf_op jit(solution)/shard_map/ppermute | solution.py:24
  70.7 15.4 %collective-permute-done.6 = bf16[32,2048]{1,0:T(8,128)(2,1)S(1)} collective-permute-done((bf16[32,2048]{1,0:T(8,128)(2,1)S(1)}, bf16[32,2048]{1,0:T(8,128)(2,1)S(1)}, u32[]{:S(2)}, u32[]{:S(2)}) %collective-permute-start.6) | collective-permute-done | bytes 131104 | tf_op jit(solution)/shard_map/ppermute | solution.py:24
  89.5 4.8 collective-permute-done.9
  105.8 4.5 collective-permute-done.11
  139.6 6.1 fusion.21
  145.7 6.9 %attend_forward.1 = (bf16[32,2,16,768]{3,2,1,0:T(8,128)(2,1)S(1)}, bf16[32,2,16,256]{3,2,1,0:T(8,128)(2,1)S(1)}, f32[32,2,16,256]{3,2,1,0:T(8,128)S(1)}, f32[2,512,128]{2,1,0:T(8,128)S(1)}) custom-call(s32[2]{0:T(128)S(1)} %dynamic_slice.15.lens, f32[32,2,16,768]{3,2,1,0:T(8,128)S(1)} %bitcast.58, f32[1,768]{1,0:T(1,128)S(1)} %fusion.97.shift, ...), custom_call_target="tpu_custom_call" | custom-call | tf_op jit(solution)/shard_map/attend_forward/pallas_call | solution.py:374
  154.9 3.3 convolution_convert_fusion.3
  168.4 14.7 %collective-permute-done.19 = bf16[64,2048]{1,0:T(8,128)(2,1)S(1)} collective-permute-done((bf16[64,2048]{1,0:T(8,128)(2,1)S(1)}, bf16[64,2048]{1,0:T(8,128)(2,1)S(1)}, u32[]{:S(2)}, u32[]{:S(2)}) %collective-permute-start.19) | collective-permute-done | bytes 262176 | tf_op jit(solution)/shard_map/ppermute | solution.py:24
  190.6 14.8 %collective-permute-done.25 = bf16[64,2048]{1,0:T(8,128)(2,1)S(1)} collective-permute-done((bf16[64,2048]{1,0:T(8,128)(2,1)S(1)}, bf16[64,2048]{1,0:T(8,128)(2,1)S(1)}, u32[]{:S(2)}, u32[]{:S(2)}) %collective-permute-start.25) | collective-permute-done | bytes 262176 | tf_op jit(solution)/shard_map/ppermute | solution.py:24
  210.4 12.3 %collective-permute-done.27 = bf16[128,2048]{1,0:T(8,128)(2,1)S(1)} collective-permute-done((bf16[128,2048]{1,0:T(8,128)(2,1)S(1)}, bf16[128,2048]{1,0:T(8,128)(2,1)S(1)}, u32[]{:S(2)}, u32[]{:S(2)}) %collective-permute-start.27) | collective-permute-done | bytes 524320 | tf_op jit(solution)/shard_map/ppermute | solution.py:24
  227.9 3.8 collective-permute-done.30
  236.3 4.2 collective-permute-done.32
  241.9 55.4 %all-gather.5.cloned.1.call-done = bf16[2048,2176]{1,0:T(8,128)(2,1)} async-done(((bf16[512,2176]{1,0:T(8,128)(2,1)}), bf16[2048,2176]{1,0:T(8,128)(2,1)}) %all-gather.5.cloned.1.call-update) | async-done | bytes 8912912 | tf_op jit(solution)/shard_map/all_gather | solution.py:221
  297.3 10.7 %fusion.4 = f32[1024,1408]{1,0:T(8,128)S(1)} fusion(bf16[1024,2048]{1,0:T(8,128)(2,1)} %constant_dynamic-update-slice_fusion.21, bf16[2048,2176]{1,0:T(8,128)(2,1)} %all-gather.5.cloned.1.call-done), kind=kOutput, calls=%fused_computation.5 | convolution fusion | flops 5905580032 | bytes 15728640 | tf_op jit(solution)/shard_map/td,df->tf/dot_general | solution.py:605
  313.2 5.0 convolution_convert_fusion.2
  318.3 9.2 %fusion.7 = (bf16[1024,704]{1,0:T(8,128)(2,1)S(1)}, bf16[1024,704]{1,0:T(8,128)(2,1)S(1)}) fusion(f32[1024,1408]{1,0:T(8,128)} %copy-done.14, bf16[1024,2048]{1,0:T(8,128)(2,1)} %pad_maximum_fusion, bf16[2048,2176]{1,0:T(8,128)(2,1)} %all-gather.5.cloned.1.call-done), kind=kOutput, calls=%fused_computation.17 | convolution fusion | flops 2963603456 | bytes 16515072 | tf_op jit(solution)/shard_map/td,df->tf/dot_general | solution.py:615
  328.4 8.4 %fusion.10 = bf16[512,2048]{1,0:T(8,128)(2,1)} fusion(bf16[2048,2176]{1,0:T(8,128)(2,1)} %all-gather.5.cloned.1.call-done, bf16[1024,704]{1,0:T(8,128)(2,1)S(1)} %get-tuple-element.459, bf16[1024,704]{1,0:T(8,128)(2,1)S(1)} %get-tuple-element.460), kind=kOutput, calls=%fused_computation.25 | convolution fusion | flops 2956722176 | bytes 10747904 | tf_op jit(solution)/shard_map/tf,df->td/dot_general | solution.py:623
  336.8 5.0 fusion
  341.9 10.8 %convolution_convert_fusion = bf16[2048,1408]{1,0:T(8,128)(2,1)} fusion(bf16[1024,2048]{1,0:T(8,128)(2,1)} %constant_dynamic-update-slice_fusion.21, bf16[1024,1408]{1,0:T(8,128)(2,1)S(1)} %pad_maximum_fusion.2), kind=kOutput, calls=%fused_computation | convolution fusion | flops 5908463616 | bytes 12845056 | tf_op jit(solution)/shard_map/td,tf->df/dot_general | solution.py:633
  352.7 26.0 %reduce-scatter.4.cloned.1.call-done = bf16[512,704]{1,0:T(8,128)(2,1)} async-done(((bf16[2048,704]{1,0:T(8,128)(2,1)}), bf16[512,704]{1,0:T(8,128)(2,1)}) %reduce-scatter.4.cloned.1.call-update) | async-done | bytes 720912 | tf_op jit(solution)/shard_map/reduce_scatter | solution.py:224
  384.1 5.2 collective-permute-done.34
  397.2 3.8 convolution_convert_fusion.5
  401.0 5.7 collective-permute-done.37
  414.7 3.8 fusion.13
  418.5 8.0 %collective-permute-done.38 = bf16[128,2048]{1,0:T(8,128)(2,1)S(1)} collective-permute-done((bf16[128,2048]{1,0:T(8,128)(2,1)S(1)}, bf16[128,2048]{1,0:T(8,128)(2,1)S(1)}, u32[]{:S(2)}, u32[]{:S(2)}) %collective-permute-start.38) | collective-permute-done | bytes 524320 | tf_op jit(solution)/shard_map/ppermute | solution.py:24
  431.7 5.0 collective-permute-done.43
  437.8 3.8 collective-permute-done.41
  446.5 3.4 convolution_convert_fusion.17
  449.9 8.9 %attend_backward.1 = (bf16[32,2,16,768]{3,2,1,0:T(8,128)(2,1)S(1)}, f32[2,8,768]{2,1,0:T(8,128)S(1)}) custom-call(s32[2]{0:T(128)S(1)} %dynamic_slice.15.lens, bf16[32,2,16,768]{3,2,1,0:T(8,128)(2,1)S(1)} %get-tuple-element.335.qkv, bf16[32,2,16,256]{3,2,1,0:T(8,128)(2,1)S(1)} %bitcast.59, f32[32,2,16,256]{3,2,1,0:T(8,128)S(1)} %get-tuple-element.348.full, ...), custom_call_target="tpu_custom_call" | custom-call | tf_op jit(solution)/shard_map/attend_backward/pallas_call | solution.py:396
  458.9 5.2 convolution_convert_fusion.4
  469.9 3.9 fusion.18
  476.3 4.1 convolution_convert_fusion.1
  490.8 5.1 collective-permute-done.54
  508.8 3.3 collective-permute-done.58
  512.2 9.5 %collective-permute-done.59 = bf16[32,2048]{1,0:T(8,128)(2,1)} collective-permute-done((bf16[32,2048]{1,0:T(8,128)(2,1)}, bf16[32,2048]{1,0:T(8,128)(2,1)}, u32[]{:S(2)}, u32[]{:S(2)}) %collective-permute-start.59) | collective-permute-done | bytes 131104 | tf_op jit(solution)/shard_map/ppermute | solution.py:24
  531.9 4.1 collective-permute-done.64
  537.5 6.2 collective-permute-done.63
  545.1 11.8 %collective-permute-done.62 = bf16[32,2048]{1,0:T(8,128)(2,1)S(1)} collective-permute-done((bf16[32,2048]{1,0:T(8,128)(2,1)S(1)}, bf16[32,2048]{1,0:T(8,128)(2,1)S(1)}, u32[]{:S(2)}, u32[]{:S(2)}) %collective-permute-start.62) | collective-permute-done | bytes 131104 | tf_op jit(solution)/shard_map/ppermute | solution.py:24
  563.2 3.7 copy.74
  571.5 8.5 %fusion.130 = (bf16[256,2,1408]{2,1,0:T(2,128)(2,1)}, f32[256,2,1408]{2,1,0:T(2,128)S(1)}, f32[256,2,1408]{2,1,0:T(2,128)}) fusion(f32[256,2,1408]{2,1,0:T(2,128)S(1)} %copy-done.10, f32[256,2,1408]{2,1,0:T(2,128)} %param.37, f32[256,2,704]{2,1,0:T(2,128)S(1)} %copy-done.18, f32[256,2,704]{2,1,0:T(2,128)S(1)} %copy-done.17), kind=kLoop, calls=%fused_computation.359 | loop fusion | flops 7208960 | bytes 15859712 | tf_op jit(solution)/shard_map/convert_element_type | solution.py:735
  580.1 4.1 multiply_add_fusion
  590.5 5.2 reduce-scatter.8.cloned.1.call-done
  613.7 3.0 collective-permute-done.74
  625.8 3.5 fusion.127
  (597 shorter events, 241.6 us)
Async XLA Ops:
  7.2 128.6 %all-gather.3.cloned.1.call-start = ((), (), s32[]{:S(2)}) async-start(), calls=%async_computation.3 | async-start | bytes 5242880 | tf_op jit(solution)/shard_map/all_gather | solution.py:221
  36.8 18.4 %collective-permute-start.7 = (bf16[256,1408]{1,0:T(8,128)(2,1)}, bf16[256,1408]{1,0:T(8,128)(2,1)}, u32[]{:S(2)}, u32[]{:S(2)}) collective-permute-start(bf16[256,1408]{1,0:T(8,128)(2,1)} %copy.62), channel_id=1, source_target_pairs={{0,4},{4,0},{8,12},{12,8},{16,20},{20,16},{24,28},{28,24},{1,5},{5... | collective-permute-start | bytes 2162696 | tf_op jit(solution)/shard_map/ppermute | solution.py:24
  38.3 18.5 %collective-permute-start.1 = (bf16[5,2048]{1,0:T(8,128)(2,1)}, bf16[5,2048]{1,0:T(8,128)(2,1)}, u32[]{:S(2)}, u32[]{:S(2)}) collective-permute-start(bf16[5,2048]{1,0:T(8,128)(2,1)} %fusion.84), channel_id=1, source_target_pairs={{0,4},{4,0},{8,12},{12,8},{16,20},{20,16},{24,28},{28,24},{1,5},{5... | collective-permute-start | bytes 61448 | tf_op jit(solution)/shard_map/ppermute | solution.py:24
  38.8 20.8 %collective-permute-start.2 = (bf16[5,2048]{1,0:T(8,128)(2,1)}, bf16[5,2048]{1,0:T(8,128)(2,1)}, u32[]{:S(2)}, u32[]{:S(2)}) collective-permute-start(bf16[5,2048]{1,0:T(8,128)(2,1)} %fusion.84), channel_id=1, source_target_pairs={{0,16},{4,20},{8,24},{12,28},{16,0},{20,4},{24,8},{28,12},{1,17},{... | collective-permute-start | bytes 61448 | tf_op jit(solution)/shard_map/ppermute | solution.py:24
  39.0 20.7 %collective-permute-start.3 = (bf16[5,2048]{1,0:T(8,128)(2,1)}, bf16[5,2048]{1,0:T(8,128)(2,1)}, u32[]{:S(2)}, u32[]{:S(2)}) collective-permute-start(bf16[5,2048]{1,0:T(8,128)(2,1)} %fusion.84), channel_id=1, source_target_pairs={{0,20},{4,16},{8,28},{12,24},{16,4},{20,0},{24,12},{28,8},{1,21},{... | collective-permute-start | bytes 61448 | tf_op jit(solution)/shard_map/ppermute | solution.py:24
  43.1 16.6 %collective-permute-start.4 = (bf16[32,2048]{1,0:T(8,128)(2,1)}, bf16[32,2048]{1,0:T(8,128)(2,1)S(1)}, u32[]{:S(2)}, u32[]{:S(2)}) collective-permute-start(bf16[32,2048]{1,0:T(8,128)(2,1)} %convolution_convert_fusion.15), channel_id=1, source_target_pairs={{0,8},{4,12},{8,0},{12,4},{16,24},{20,28},{24,16},{28,20},{1,9},{5... | collective-permute-start | bytes 393224 | tf_op jit(solution)/shard_map/ppermute | solution.py:24
  44.7 252.6 %all-gather.5.cloned.1.call-start = ((), (), s32[]{:S(2)}) async-start(), calls=%async_computation.4 | async-start | bytes 11141120 | tf_op jit(solution)/shard_map/all_gather | solution.py:221
  55.2 15.5 %collective-permute-start.5 = (bf16[32,2048]{1,0:T(8,128)(2,1)}, bf16[32,2048]{1,0:T(8,128)(2,1)S(1)}, u32[]{:S(2)}, u32[]{:S(2)}) collective-permute-start(bf16[32,2048]{1,0:T(8,128)(2,1)} %convolution_convert_fusion.14), channel_id=1, source_target_pairs={{0,16},{4,20},{8,24},{12,28},{16,0},{20,4},{24,8},{28,12},{1,17},{... | collective-permute-start | bytes 393224 | tf_op jit(solution)/shard_map/ppermute | solution.py:24
  56.9 29.3 %collective-permute-start.6 = (bf16[32,2048]{1,0:T(8,128)(2,1)S(1)}, bf16[32,2048]{1,0:T(8,128)(2,1)S(1)}, u32[]{:S(2)}, u32[]{:S(2)}) collective-permute-start(bf16[32,2048]{1,0:T(8,128)(2,1)S(1)} %copy-done.69), channel_id=1, source_target_pairs={{0,24},{4,28},{8,16},{12,20},{16,8},{20,12},{24,0},{28,4},{1,25},{... | collective-permute-start | bytes 393224 | tf_op jit(solution)/shard_map/ppermute | solution.py:24
  135.8 22.4 %collective-permute-start.15 = (bf16[32,2048]{1,0:T(8,128)(2,1)}, bf16[32,2048]{1,0:T(8,128)(2,1)}, u32[]{:S(2)}, u32[]{:S(2)}) collective-permute-start(bf16[32,2048]{1,0:T(8,128)(2,1)} %convolution_convert_fusion.11), channel_id=1, source_target_pairs={{0,8},{4,12},{8,0},{12,4},{16,24},{20,28},{24,16},{28,20},{1,9},{5... | collective-permute-start | bytes 393224 | tf_op jit(solution)/shard_map/ppermute | solution.py:24
  136.3 21.9 %collective-permute-start.16 = (bf16[32,2048]{1,0:T(8,128)(2,1)}, bf16[32,2048]{1,0:T(8,128)(2,1)}, u32[]{:S(2)}, u32[]{:S(2)}) collective-permute-start(bf16[32,2048]{1,0:T(8,128)(2,1)} %convolution_convert_fusion.10), channel_id=1, source_target_pairs={{0,16},{4,20},{8,24},{12,28},{16,0},{20,4},{24,8},{28,12},{1,17},{... | collective-permute-start | bytes 393224 | tf_op jit(solution)/shard_map/ppermute | solution.py:24
  138.2 20.0 %collective-permute-start.17 = (bf16[32,2048]{1,0:T(8,128)(2,1)}, bf16[32,2048]{1,0:T(8,128)(2,1)}, u32[]{:S(2)}, u32[]{:S(2)}) collective-permute-start(bf16[32,2048]{1,0:T(8,128)(2,1)} %convolution_convert_fusion.9), channel_id=1, source_target_pairs={{0,24},{4,28},{8,16},{12,20},{16,8},{20,12},{24,0},{28,4},{1,25},{... | collective-permute-start | bytes 393224 | tf_op jit(solution)/shard_map/ppermute | solution.py:24
  139.3 239.4 %reduce-scatter.4.cloned.1.call-start = ((), (), s32[]{:S(2)}) async-start(), calls=%async_computation.5 | async-start | bytes 3932160 | tf_op jit(solution)/shard_map/reduce_scatter | solution.py:224
  163.0 21.2 %collective-permute-start.21 = (bf16[128,2048]{1,0:T(8,128)(2,1)S(1)}, bf16[128,2048]{1,0:T(8,128)(2,1)S(1)}, u32[]{:S(2)}, u32[]{:S(2)}) collective-permute-start(bf16[128,2048]{1,0:T(8,128)(2,1)S(1)} %maximum_select_fusion), channel_id=1, source_target_pairs={{0,2},{1,3},{2,0},{3,1},{4,6},{5,7},{6,4},{7,5},{8,10},{9,11},{10,... | collective-permute-start | bytes 1572872 | tf_op jit(solution)/shard_map/ppermute | solution.py:24
  164.6 19.7 %collective-permute-start.22 = (bf16[128,2048]{1,0:T(8,128)(2,1)S(1)}, bf16[128,2048]{1,0:T(8,128)(2,1)S(1)}, u32[]{:S(2)}, u32[]{:S(2)}) collective-permute-start(bf16[128,2048]{1,0:T(8,128)(2,1)S(1)} %maximum_select_fusion), channel_id=1, source_target_pairs={{0,4},{4,0},{8,12},{12,8},{16,20},{20,16},{24,28},{28,24},{1,5},{5... | collective-permute-start | bytes 1572872 | tf_op jit(solution)/shard_map/ppermute | solution.py:24
  166.3 16.7 %collective-permute-start.19 = (bf16[64,2048]{1,0:T(8,128)(2,1)S(1)}, bf16[64,2048]{1,0:T(8,128)(2,1)S(1)}, u32[]{:S(2)}, u32[]{:S(2)}) collective-permute-start(bf16[64,2048]{1,0:T(8,128)(2,1)S(1)} %get-tuple-element.476), channel_id=1, source_target_pairs={{0,2},{1,3},{2,0},{3,1},{4,6},{5,7},{6,4},{7,5},{8,10},{9,11},{10,... | collective-permute-start | bytes 786440 | tf_op jit(solution)/shard_map/ppermute | solution.py:24
  166.9 17.3 %collective-permute-start.20 = (bf16[64,2048]{1,0:T(8,128)(2,1)S(1)}, bf16[64,2048]{1,0:T(8,128)(2,1)S(1)}, u32[]{:S(2)}, u32[]{:S(2)}) collective-permute-start(bf16[64,2048]{1,0:T(8,128)(2,1)S(1)} %get-tuple-element.475), channel_id=1, source_target_pairs={{0,4},{4,0},{8,12},{12,8},{16,20},{20,16},{24,28},{28,24},{1,5},{5... | collective-permute-start | bytes 786440 | tf_op jit(solution)/shard_map/ppermute | solution.py:24
  185.9 19.5 %collective-permute-start.24 = (bf16[128,2048]{1,0:T(8,128)(2,1)S(1)}, bf16[128,2048]{1,0:T(8,128)(2,1)S(1)}, u32[]{:S(2)}, u32[]{:S(2)}) collective-permute-start(bf16[128,2048]{1,0:T(8,128)(2,1)S(1)} %pad_maximum_fusion.12), channel_id=1, source_target_pairs={{0,2},{1,3},{2,0},{3,1},{4,6},{5,7},{6,4},{7,5},{8,10},{9,11},{10,... | collective-permute-start | bytes 1572872 | tf_op jit(solution)/shard_map/ppermute | solution.py:24
  186.7 18.7 %collective-permute-start.23 = (bf16[128,2048]{1,0:T(8,128)(2,1)S(1)}, bf16[128,2048]{1,0:T(8,128)(2,1)S(1)}, u32[]{:S(2)}, u32[]{:S(2)}) collective-permute-start(bf16[128,2048]{1,0:T(8,128)(2,1)S(1)} %pad_maximum_fusion.11), channel_id=1, source_target_pairs={{0,4},{4,0},{8,12},{12,8},{16,20},{20,16},{24,28},{28,24},{1,5},{5... | collective-permute-start | bytes 1572872 | tf_op jit(solution)/shard_map/ppermute | solution.py:24
  187.4 18.0 %collective-permute-start.25 = (bf16[64,2048]{1,0:T(8,128)(2,1)S(1)}, bf16[64,2048]{1,0:T(8,128)(2,1)S(1)}, u32[]{:S(2)}, u32[]{:S(2)}) collective-permute-start(bf16[64,2048]{1,0:T(8,128)(2,1)S(1)} %slice.490), channel_id=1, source_target_pairs={{0,4},{4,0},{8,12},{12,8},{16,20},{20,16},{24,28},{28,24},{1,5},{5... | collective-permute-start | bytes 786440 | tf_op jit(solution)/shard_map/ppermute | solution.py:24
  189.0 16.4 %collective-permute-start.26 = (bf16[64,2048]{1,0:T(8,128)(2,1)S(1)}, bf16[64,2048]{1,0:T(8,128)(2,1)S(1)}, u32[]{:S(2)}, u32[]{:S(2)}) collective-permute-start(bf16[64,2048]{1,0:T(8,128)(2,1)S(1)} %slice.491), channel_id=1, source_target_pairs={{0,2},{1,3},{2,0},{3,1},{4,6},{5,7},{6,4},{7,5},{8,10},{9,11},{10,... | collective-permute-start | bytes 786440 | tf_op jit(solution)/shard_map/ppermute | solution.py:24
  205.5 18.4 %collective-permute-start.29 = (bf16[512,2048]{1,0:T(8,128)(2,1)S(1)}, bf16[512,2048]{1,0:T(8,128)(2,1)S(1)}, u32[]{:S(2)}, u32[]{:S(2)}) collective-permute-start(bf16[512,2048]{1,0:T(8,128)(2,1)S(1)} %constant_dynamic-update-slice_fusion.11), channel_id=1, source_target_pairs={{0,1},{1,0},{2,3},{3,2},{4,5},{5,4},{6,7},{7,6},{8,9},{9,8},{10,11... | collective-permute-start | bytes 6291464 | tf_op jit(solution)/shard_map/ppermute | solution.py:24
  208.3 14.4 %collective-permute-start.27 = (bf16[128,2048]{1,0:T(8,128)(2,1)S(1)}, bf16[128,2048]{1,0:T(8,128)(2,1)S(1)}, u32[]{:S(2)}, u32[]{:S(2)}) collective-permute-start(bf16[128,2048]{1,0:T(8,128)(2,1)S(1)} %add_convert_fusion.1), channel_id=1, source_target_pairs={{0,2},{1,3},{2,0},{3,1},{4,6},{5,7},{6,4},{7,5},{8,10},{9,11},{10,... | collective-permute-start | bytes 1572872 | tf_op jit(solution)/shard_map/ppermute | solution.py:24
  209.9 14.0 %collective-permute-start.28 = (bf16[128,2048]{1,0:T(8,128)(2,1)S(1)}, bf16[128,2048]{1,0:T(8,128)(2,1)S(1)}, u32[]{:S(2)}, u32[]{:S(2)}) collective-permute-start(bf16[128,2048]{1,0:T(8,128)(2,1)S(1)} %add_convert_fusion.1), channel_id=1, source_target_pairs={{0,4},{4,0},{8,12},{12,8},{16,20},{20,16},{24,28},{28,24},{1,5},{5... | collective-permute-start | bytes 1572872 | tf_op jit(solution)/shard_map/ppermute | solution.py:24
  318.2 166.9 %reduce-scatter.6.cloned.1.call-start = ((), (), s32[]{:S(2)}) async-start(), calls=%async_computation.6 | async-start | bytes 7208960 | tf_op jit(solution)/shard_map/reduce_scatter | solution.py:224
  336.8 15.9 %collective-permute-start.33 = (bf16[512,2048]{1,0:T(8,128)(2,1)}, bf16[512,2048]{1,0:T(8,128)(2,1)}, u32[]{:S(2)}, u32[]{:S(2)}) collective-permute-start(bf16[512,2048]{1,0:T(8,128)(2,1)} %fusion.10), channel_id=1, source_target_pairs={{0,1},{1,0},{2,3},{3,2},{4,5},{5,4},{6,7},{7,6},{8,9},{9,8},{10,11... | collective-permute-start | bytes 6291464 | tf_op jit(solution)/shard_map/ppermute | solution.py:24
  383.8 211.9 %reduce-scatter.8.cloned.1.call-start = ((), (), s32[]{:S(2)}) async-start(), calls=%async_computation.7 | async-start | bytes 5242880 | tf_op jit(solution)/shard_map/reduce_scatter | solution.py:224
  408.6 18.7 %collective-permute-start.40 = (bf16[512,2048]{1,0:T(8,128)(2,1)S(1)}, bf16[512,2048]{1,0:T(8,128)(2,1)S(1)}, u32[]{:S(2)}, u32[]{:S(2)}) collective-permute-start(bf16[512,2048]{1,0:T(8,128)(2,1)S(1)} %convolution_convert_fusion.5), channel_id=1, source_target_pairs={{0,1},{1,0},{2,3},{3,2},{4,5},{5,4},{6,7},{7,6},{8,9},{9,8},{10,11... | collective-permute-start | bytes 6291464 | tf_op jit(solution)/shard_map/ppermute | solution.py:24
  412.2 14.3 %collective-permute-start.38 = (bf16[128,2048]{1,0:T(8,128)(2,1)S(1)}, bf16[128,2048]{1,0:T(8,128)(2,1)S(1)}, u32[]{:S(2)}, u32[]{:S(2)}) collective-permute-start(bf16[128,2048]{1,0:T(8,128)(2,1)S(1)} %get-tuple-element.341), channel_id=1, source_target_pairs={{0,2},{1,3},{2,0},{3,1},{4,6},{5,7},{6,4},{7,5},{8,10},{9,11},{10,... | collective-permute-start | bytes 1572872 | tf_op jit(solution)/shard_map/ppermute | solution.py:24
  413.2 14.0 %collective-permute-start.39 = (bf16[128,2048]{1,0:T(8,128)(2,1)S(1)}, bf16[128,2048]{1,0:T(8,128)(2,1)S(1)}, u32[]{:S(2)}, u32[]{:S(2)}) collective-permute-start(bf16[128,2048]{1,0:T(8,128)(2,1)S(1)} %get-tuple-element.341), channel_id=1, source_target_pairs={{0,4},{4,0},{8,12},{12,8},{16,20},{20,16},{24,28},{28,24},{1,5},{5... | collective-permute-start | bytes 1572872 | tf_op jit(solution)/shard_map/ppermute | solution.py:24
  443.2 20.9 %collective-permute-start.47 = (bf16[128,2048]{1,0:T(8,128)(2,1)}, bf16[128,2048]{1,0:T(8,128)(2,1)}, u32[]{:S(2)}, u32[]{:S(2)}) collective-permute-start(bf16[128,2048]{1,0:T(8,128)(2,1)} %pad_maximum_fusion.16), channel_id=1, source_target_pairs={{0,2},{1,3},{2,0},{3,1},{4,6},{5,7},{6,4},{7,5},{8,10},{9,11},{10,... | collective-permute-start | bytes 1572872 | tf_op jit(solution)/shard_map/ppermute | solution.py:24
  444.3 19.8 %collective-permute-start.46 = (bf16[128,2048]{1,0:T(8,128)(2,1)S(1)}, bf16[128,2048]{1,0:T(8,128)(2,1)S(1)}, u32[]{:S(2)}, u32[]{:S(2)}) collective-permute-start(bf16[128,2048]{1,0:T(8,128)(2,1)S(1)} %pad_maximum_fusion.15), channel_id=1, source_target_pairs={{0,4},{4,0},{8,12},{12,8},{16,20},{20,16},{24,28},{28,24},{1,5},{5... | collective-permute-start | bytes 1572872 | tf_op jit(solution)/shard_map/ppermute | solution.py:24
  464.1 18.9 %collective-permute-start.49 = (f32[1,768]{1,0:T(1,128)S(1)}, f32[1,768]{1,0:T(1,128)S(1)}, u32[]{:S(2)}, u32[]{:S(2)}) collective-permute-start(f32[1,768]{1,0:T(1,128)S(1)} %broadcast_in_dim.64), channel_id=1, source_target_pairs={{0,16},{4,20},{8,24},{12,28},{16,0},{20,4},{24,8},{28,12},{1,17},{... | collective-permute-start | bytes 9224 | tf_op jit(solution)/shard_map/ppermute | solution.py:24
  464.4 18.6 %collective-permute-start.50 = (f32[1,768]{1,0:T(1,128)S(1)}, f32[1,768]{1,0:T(1,128)S(1)}, u32[]{:S(2)}, u32[]{:S(2)}) collective-permute-start(f32[1,768]{1,0:T(1,128)S(1)} %broadcast_in_dim.64), channel_id=1, source_target_pairs={{0,8},{4,12},{8,0},{12,4},{16,24},{20,28},{24,16},{28,20},{1,9},{5... | collective-permute-start | bytes 9224 | tf_op jit(solution)/shard_map/ppermute | solution.py:24
  465.8 17.2 %collective-permute-start.51 = (f32[1,768]{1,0:T(1,128)S(1)}, f32[1,768]{1,0:T(1,128)S(1)}, u32[]{:S(2)}, u32[]{:S(2)}) collective-permute-start(f32[1,768]{1,0:T(1,128)S(1)} %broadcast_in_dim.64), channel_id=1, source_target_pairs={{0,24},{4,28},{8,16},{12,20},{16,8},{20,12},{24,0},{28,4},{1,25},{... | collective-permute-start | bytes 9224 | tf_op jit(solution)/shard_map/ppermute | solution.py:24
  467.7 15.4 %collective-permute-start.48 = (bf16[512,2048]{1,0:T(8,128)(2,1)}, bf16[512,2048]{1,0:T(8,128)(2,1)S(1)}, u32[]{:S(2)}, u32[]{:S(2)}) collective-permute-start(bf16[512,2048]{1,0:T(8,128)(2,1)} %convolution_convert_fusion.4), channel_id=1, source_target_pairs={{0,1},{1,0},{2,3},{3,2},{4,5},{5,4},{6,7},{7,6},{8,9},{9,8},{10,11... | collective-permute-start | bytes 6291464 | tf_op jit(solution)/shard_map/ppermute | solution.py:24
  498.5 23.2 %collective-permute-start.56 = (bf16[128,2048]{1,0:T(8,128)(2,1)S(1)}, bf16[128,2048]{1,0:T(8,128)(2,1)}, u32[]{:S(2)}, u32[]{:S(2)}) collective-permute-start(bf16[128,2048]{1,0:T(8,128)(2,1)S(1)} %pad_maximum_fusion.18), channel_id=1, source_target_pairs={{0,2},{1,3},{2,0},{3,1},{4,6},{5,7},{6,4},{7,5},{8,10},{9,11},{10,... | collective-permute-start | bytes 1572872 | tf_op jit(solution)/shard_map/ppermute | solution.py:24
  500.1 21.6 %collective-permute-start.55 = (bf16[128,2048]{1,0:T(8,128)(2,1)}, bf16[128,2048]{1,0:T(8,128)(2,1)}, u32[]{:S(2)}, u32[]{:S(2)}) collective-permute-start(bf16[128,2048]{1,0:T(8,128)(2,1)} %pad_maximum_fusion.17), channel_id=1, source_target_pairs={{0,4},{4,0},{8,12},{12,8},{16,20},{20,16},{24,28},{28,24},{1,5},{5... | collective-permute-start | bytes 1572872 | tf_op jit(solution)/shard_map/ppermute | solution.py:24
  503.9 17.8 %collective-permute-start.59 = (bf16[32,2048]{1,0:T(8,128)(2,1)}, bf16[32,2048]{1,0:T(8,128)(2,1)}, u32[]{:S(2)}, u32[]{:S(2)}) collective-permute-start(bf16[32,2048]{1,0:T(8,128)(2,1)} %get-tuple-element.385), channel_id=1, source_target_pairs={{0,24},{4,28},{8,16},{12,20},{16,8},{20,12},{24,0},{28,4},{1,25},{... | collective-permute-start | bytes 393224 | tf_op jit(solution)/shard_map/ppermute | solution.py:24
  523.3 33.7 %collective-permute-start.65 = (bf16[128,2048]{1,0:T(8,128)(2,1)S(1)}, bf16[128,2048]{1,0:T(8,128)(2,1)S(1)}, u32[]{:S(2)}, u32[]{:S(2)}) collective-permute-start(bf16[128,2048]{1,0:T(8,128)(2,1)S(1)} %convolution_convert_fusion.8), channel_id=1, source_target_pairs={{0,2},{1,3},{2,0},{3,1},{4,6},{5,7},{6,4},{7,5},{8,10},{9,11},{10,... | collective-permute-start | bytes 1572872 | tf_op jit(solution)/shard_map/ppermute | solution.py:24
  525.0 18.7 %collective-permute-start.63 = (bf16[256,1408]{1,0:T(8,128)(2,1)S(1)}, bf16[256,1408]{1,0:T(8,128)(2,1)S(1)}, u32[]{:S(2)}, u32[]{:S(2)}) collective-permute-start(bf16[256,1408]{1,0:T(8,128)(2,1)S(1)} %broadcast_select_fusion.3), channel_id=1, source_target_pairs={{0,4},{4,0},{8,12},{12,8},{16,20},{20,16},{24,28},{28,24},{1,5},{5... | collective-permute-start | bytes 2162696 | tf_op jit(solution)/shard_map/ppermute | solution.py:24
  530.2 14.9 %collective-permute-start.60 = (bf16[32,2048]{1,0:T(8,128)(2,1)S(1)}, bf16[32,2048]{1,0:T(8,128)(2,1)S(1)}, u32[]{:S(2)}, u32[]{:S(2)}) collective-permute-start(bf16[32,2048]{1,0:T(8,128)(2,1)S(1)} %get-tuple-element.504), channel_id=1, source_target_pairs={{0,8},{4,12},{8,0},{12,4},{16,24},{20,28},{24,16},{28,20},{1,9},{5... | collective-permute-start | bytes 393224 | tf_op jit(solution)/shard_map/ppermute | solution.py:24
  530.3 14.8 %collective-permute-start.61 = (bf16[32,2048]{1,0:T(8,128)(2,1)S(1)}, bf16[32,2048]{1,0:T(8,128)(2,1)S(1)}, u32[]{:S(2)}, u32[]{:S(2)}) collective-permute-start(bf16[32,2048]{1,0:T(8,128)(2,1)S(1)} %get-tuple-element.503), channel_id=1, source_target_pairs={{0,16},{4,20},{8,24},{12,28},{16,0},{20,4},{24,8},{28,12},{1,17},{... | collective-permute-start | bytes 393224 | tf_op jit(solution)/shard_map/ppermute | solution.py:24
  536.0 20.9 %collective-permute-start.62 = (bf16[32,2048]{1,0:T(8,128)(2,1)S(1)}, bf16[32,2048]{1,0:T(8,128)(2,1)S(1)}, u32[]{:S(2)}, u32[]{:S(2)}) collective-permute-start(bf16[32,2048]{1,0:T(8,128)(2,1)S(1)} %get-tuple-element.502), channel_id=1, source_target_pairs={{0,24},{4,28},{8,16},{12,20},{16,8},{20,12},{24,0},{28,4},{1,25},{... | collective-permute-start | bytes 393224 | tf_op jit(solution)/shard_map/ppermute | solution.py:24
  568.2 20.5 %collective-permute-start.68 = (bf16[256,2048]{1,0:T(8,128)(2,1)S(1)}, bf16[256,2048]{1,0:T(8,128)(2,1)S(1)}, u32[]{:S(2)}, u32[]{:S(2)}) collective-permute-start(bf16[256,2048]{1,0:T(8,128)(2,1)S(1)} %pad_maximum_fusion.5), channel_id=1, source_target_pairs={{0,1},{1,0},{2,3},{3,2},{4,5},{5,4},{6,7},{7,6},{8,9},{9,8},{10,11... | collective-permute-start | bytes 3145736 | tf_op jit(solution)/shard_map/ppermute | solution.py:24
  568.3 19.1 %collective-permute-start.67 = (f32[4,2048]{1,0:T(4,128)}, f32[4,2048]{1,0:T(4,128)S(1)}, u32[]{:S(2)}, u32[]{:S(2)}) collective-permute-start(f32[4,2048]{1,0:T(4,128)} %pad_maximum_fusion.19), channel_id=1, source_target_pairs={{0,1},{1,0},{2,3},{3,2},{4,5},{5,4},{6,7},{7,6},{8,9},{9,8},{10,11... | collective-permute-start | bytes 98312 | tf_op jit(solution)/shard_map/ppermute | solution.py:24
  570.2 20.3 %collective-permute-start.66 = (bf16[128,2048]{1,0:T(8,128)(2,1)S(1)}, bf16[128,2048]{1,0:T(8,128)(2,1)}, u32[]{:S(2)}, u32[]{:S(2)}) collective-permute-start(bf16[128,2048]{1,0:T(8,128)(2,1)S(1)} %convolution_convert_fusion.7), channel_id=1, source_target_pairs={{0,2},{1,3},{2,0},{3,1},{4,6},{5,7},{6,4},{7,5},{8,10},{9,11},{10,... | collective-permute-start | bytes 1572872 | tf_op jit(solution)/shard_map/ppermute | solution.py:24
  610.0 20.9 %collective-permute-start.69 = (bf16[256,2048]{1,0:T(8,128)(2,1)}, bf16[256,2048]{1,0:T(8,128)(2,1)}, u32[]{:S(2)}, u32[]{:S(2)}) collective-permute-start(bf16[256,2048]{1,0:T(8,128)(2,1)} %pad_maximum_fusion.6), channel_id=1, source_target_pairs={{0,1},{1,0},{2,3},{3,2},{4,5},{5,4},{6,7},{7,6},{8,9},{9,8},{10,11... | collective-permute-start | bytes 3145736 | tf_op jit(solution)/shard_map/ppermute | solution.py:24
  (160 other events, 1843.7 us)
Sparse Core Ops, SparseCore 0:
  44.9 87.7 all-gather.2
  139.4 157.8 all-gather.4
  318.4 60.2 reduce-scatter.3
  384.0 101.1 reduce-scatter.5
  506.8 88.8 reduce-scatter.7

commit v4 on v3

--- a/solution.py
+++ b/solution.py
@@ -502,14 +502,13 @@
         plan.part_flags,
     )
     attn_block = plan.spread_mine(attn_mine, 0)
-    outgoing = plan.outgoing_rows(inputs)
-    attn_block, outgoing, small, gate_weight, down_weight, cotangent, position = hold(
-        attn_block, outgoing, small, gate_weight, down_weight, cotangent, position
+    resid = plan.over_groups(plan.outgoing_rows(inputs))
+    attn_block, resid, small, gate_weight, down_weight, cotangent, position = hold(
+        attn_block, resid, small, gate_weight, down_weight, cotangent, position
     )
 
     w_attn = plan.all_blocks(attn_block)
     small_got = over_masks(small, first_masks)
-    resid = plan.over_groups(outgoing)
     gate_mine = pick([columns(gate_weight, h, hidden) for h in range(parts)], plan.part_flags)
     gate_block = plan.spread_mine(gate_mine, 0)
     small, small_got, resid, gate_block, cotangent, down_weight, position = hold(
@@ -687,9 +686,9 @@
     bias_sum = jnp.sum(bias_sum[:, 0], 0, keepdims=True)
     bias_got = over_masks(bias_sum, plan.outer)
     result = second + plan.sum_end(out_near, out_sides)
-    out_returning = plan.returning_rows(result.astype(bf16))
-    product, got, grad_attn, bias_sum, bias_got, down_sum, out_returning, gate_sum = hold(
-        product, got, grad_attn, bias_sum, bias_got, down_sum, out_returning, gate_sum
+    out_back = plan.over_groups(plan.returning_rows(result.astype(bf16)))
+    product, got, grad_attn, bias_sum, bias_got, down_sum, out_back, gate_sum = hold(
+        product, got, grad_attn, bias_sum, bias_got, down_sum, out_back, gate_sum
     )
     attn_sum = plan.sum_blocks(grad_attn)
 
@@ -697,11 +696,10 @@
     near = (product, got)
     corner = plan.sum_corner(near)
     bias_got = [swap(bias_sum, "seq", plan.inner_mask(j)) for j in range(1, parts)]
-    near, corner, bias_sum, bias_got, down_sum, gate_sum, out_returning = hold(
-        near, corner, bias_sum, bias_got, down_sum, gate_sum, out_returning
+    near, corner, bias_sum, bias_got, down_sum, gate_sum, out_back = hold(
+        near, corner, bias_sum, bias_got, down_sum, gate_sum, out_back
     )
     sides = plan.sum_sides(near, corner)
-    out_back = plan.over_groups(out_returning)
     near, sides, out_back, down_sum, gate_sum = hold(near, sides, out_back, down_sum, gate_sum)
 
     def along_tp(own):
@@ -721,7 +719,14 @@
             jnp.sum(grad_h2, 0),
         ]
     )
-    back, grad_gate, grad_down, out_pieces, sums = hold(back, grad_gate, grad_down, out_pieces, sums)
+    for mask in plan.tp_masks:
+        sums = sums + swap(sums, "tp", mask)
+    sums = plan.restored(sums)
+    for mask in seq_masks:
+        sums = sums + swap(sums, "seq", mask)
+    back, grad_gate, grad_down, out_pieces, sums, attn_sum = hold(
+        back, grad_gate, grad_down, out_pieces, sums, attn_sum
+    )
 
     def ordered_as(grad, *order):
         return with_layout_constraint(grad, Layout(order))
@@ -740,10 +745,9 @@
     gate = stepped(4, grad_gate, gate_master, moment_gate, average_gate)
     grad_down = ordered_as(joined(grad_down, -1), 0, 1)
     down = stepped(5, grad_down, down_master, moment_down, average_down)
-    wide_masks, core_masks = plan.tp_masks[:0:-1], plan.tp_masks[:1]
+    core_masks = plan.tp_masks[:1]
     pieces = along_tp(plan.returned_rows(back, quarter, inputs.shape[1]))
-    for mask in core_masks:
-        sums = sums + swap(sums, "tp", mask)
+    attn_home = plan.collect_home(attn_sum)
 
     def across_cores(pieces):
         keys = sorted(pieces)
@@ -753,30 +757,33 @@
         return plan.of_tp(pieces).reshape(inputs.shape)
 
     layer_out = across_cores(out_pieces)
-    pieces, sums, layer_out, gate, down, attn_sum = hold(pieces, sums, layer_out, gate, down, attn_sum)
+    pieces, sums, layer_out, gate, down, attn_home = hold(pieces, sums, layer_out, gate, down, attn_home)
 
     input_grad = across_cores(pieces)
 
     got = [part.reshape(3, heads_here, HD) for part in [bias_sum] + bias_got]
     bias_sum = joined(pick(got, plan.part_flags), 1)
     grad_bias = lax.dynamic_slice_in_dim(bias_sum, plan.seq * slim, slim, 2)
-    for mask in wide_masks:
-        sums = sums + swap(sums, "tp", mask)
-    sums = plan.restored(sums)
-    for mask in seq_masks:
-        sums = sums + swap(sums, "seq", mask)
     slim = norm_params.shape[1]
     grad_norm = lax.dynamic_slice_in_dim(sums, plan.seq * slim, slim, 1)
 
     norm = stepped(0, grad_norm, norm_params, moment_norm, average_norm)
     bias = stepped(2, grad_bias, entry_bias, moment_bias, average_bias)
-    attn_home = plan.collect_home(attn_sum)
-    grad_entry = [part[:, : 3 * head_width] for part in attn_home]
-    grad_entry = ordered_as(
-        joined([part.reshape(part.shape[0], 3, head_width) for part in grad_entry], -1), 1, 0, 2
+
+    def turned_over(array):
+        return jnp.swapaxes(array, 0, 1)
+
+    grad_entry = jnp.stack(
+        [
+            joined([part[:, c * head_width : (c + 1) * head_width] for part in attn_home], -1)
+            for c in range(3)
+        ]
     )
     grad_output = ordered_as(joined([part[:, 3 * head_width :] for part in attn_home], -1), 0, 1)
-    entry = stepped(1, grad_entry, entry_weight, moment_entry, average_entry)
+    entry = stepped(
+        1, grad_entry, turned_over(entry_weight), turned_over(moment_entry), turned_over(average_entry)
+    )
+    entry = [turned_over(array) for array in entry]
     output = stepped(3, grad_output, output_weight, moment_output, average_output)
     kinds = zip(norm, entry, bias, output, gate, down)
     return (layer_out, input_grad, *(array for kind in kinds for array in kind))

time: 652 us -> 635 us (0.974)
  other arithmetic: 92.1 us -> 81.1 us
  local copies, waits for them, and re-layouts: 61.8 us -> 53.2 us
    all_gather x2, waiting for transfers between devices: 55.4 us -> 71.7 us  [all_blocks(): lax.all_gather(block, 'seq', axis_index_groups=self.lists(), axis=0, tile...]
    ppermute x75, waiting for transfers between devices: 193 us -> 185 us  [swap(): return lax.ppermute(array, axis, pairs)]
    reduce_scatter x3, waiting for transfers between devices: 33.2 us -> 25.8 us  [sum_blocks(): lax.psum_scatter(product, 'seq', scatter_dimension=0, axis_index_groups=s...]
    convert_element_type x6 -> x5, other arithmetic: 16.4 us -> 12.9 us  [stepped(): weight.astype(bf16)]
    unnamed x276 -> x278, local copies, waits for them, and re-layouts: 22.9 us -> 22.9 us
  transfers between devices with their start and end apart: 80 -> 80, of which waited for: 42 -> 39; matrix products, arithmetic and copies ran while one was open for 32% -> 30% of each run, Pallas kernels for 2% -> 3%
where the time goes in v4:
time: 635 us; the launch traced here: 625 us
  waiting for transfers between devices  283 us (45%)
  matrix products  100 us (16%)
  other arithmetic  81.1 us (13%)
  starting transfers between devices  74.9 us (12%)
  local copies, waits for them, and re-layouts  53.2 us (8%)
  between operations  16.7 us (3%)
  Pallas kernels  15.8 us (2%)
    ppermute x75, waiting for transfers between devices, swap(): return lax.ppermute(array, axis, pairs)  185 us
    ppermute x75, starting transfers between devices, swap(): return lax.ppermute(array, axis, pairs)  74.3 us
    all_gather x2, waiting for transfers between devices, all_blocks(): lax.all_gather(block, 'seq', axis_index_groups=self.lists(), axis=0, tile...  71.7 us
    reduce_scatter x3, waiting for transfers between devices, sum_blocks(): lax.psum_scatter(product, 'seq', scatter_dimension=0, axis_index_groups=s...  25.8 us
    unnamed x278, local copies, waits for them, and re-layouts  22.9 us
    dot_general x2, matrix products, gate_product(): jnp.einsum('tf,df->td', grad_gated[lo:hi], w_gate, preferred_element_type...  13.5 us
    convert_element_type x5, other arithmetic, stepped(): weight.astype(bf16)  12.9 us
  transfers between devices with their start and end apart: 80, of which 39 were waited for; matrix products, arithmetic and copies ran while one was open for 30% of the time, Pallas kernels for 3%

profile of v4, /device:TPU:16, one launch (start us, length us, event | category | flops | bytes accessed | tf_op | source)
XLA Modules:
  0.0 624.7 jit_solution(3898855444227650771)
XLA Ops:
  24.3 3.3 collective-permute-done
  31.9 3.2 copy.59
  39.0 2.9 collective-permute-start.6
  42.3 12.8 %collective-permute-done.7 = bf16[256,1408]{1,0:T(8,128)(2,1)} collective-permute-done((bf16[256,1408]{1,0:T(8,128)(2,1)S(1)}, bf16[256,1408]{1,0:T(8,128)(2,1)}, u32[]{:S(2)}, u32[]{:S(2)}) %collective-permute-start.7) | collective-permute-done | bytes 720928 | tf_op jit(solution)/shard_map/ppermute | solution.py:24
  60.0 6.0 collective-permute-done.9
  72.1 2.9 concatenate.181
  75.0 4.1 collective-permute-done.10
  105.6 16.8 %all-gather.3.cloned.1.call-done = bf16[2048,1024]{1,0:T(8,128)(2,1)} async-done(((bf16[512,1024]{1,0:T(8,128)(2,1)}), bf16[2048,1024]{1,0:T(8,128)(2,1)}) %all-gather.3.cloned.1.call-update) | async-done | bytes 4194320 | tf_op jit(solution)/shard_map/all_gather | solution.py:221
  126.2 6.1 fusion.21
  132.4 6.9 %attend_forward.1 = (bf16[32,2,16,768]{3,2,1,0:T(8,128)(2,1)S(1)}, bf16[32,2,16,256]{3,2,1,0:T(8,128)(2,1)S(1)}, f32[32,2,16,256]{3,2,1,0:T(8,128)S(1)}, f32[2,512,128]{2,1,0:T(8,128)S(1)}) custom-call(s32[2]{0:T(128)S(1)} %dynamic_slice.15.lens, f32[32,2,16,768]{3,2,1,0:T(8,128)S(1)} %bitcast.90, f32[1,768]{1,0:T(1,128)S(1)} %fusion.98.shift, ...), custom_call_target="tpu_custom_call" | custom-call | tf_op jit(solution)/shard_map/attend_forward/pallas_call | solution.py:374
  140.1 3.4 convolution_convert_fusion.3
  153.7 14.7 %collective-permute-done.19 = bf16[64,2048]{1,0:T(8,128)(2,1)S(1)} collective-permute-done((bf16[64,2048]{1,0:T(8,128)(2,1)S(1)}, bf16[64,2048]{1,0:T(8,128)(2,1)S(1)}, u32[]{:S(2)}, u32[]{:S(2)}) %collective-permute-start.19) | collective-permute-done | bytes 262176 | tf_op jit(solution)/shard_map/ppermute | solution.py:24
  175.9 14.9 %collective-permute-done.25 = bf16[64,2048]{1,0:T(8,128)(2,1)S(1)} collective-permute-done((bf16[64,2048]{1,0:T(8,128)(2,1)S(1)}, bf16[64,2048]{1,0:T(8,128)(2,1)S(1)}, u32[]{:S(2)}, u32[]{:S(2)}) %collective-permute-start.25) | collective-permute-done | bytes 262176 | tf_op jit(solution)/shard_map/ppermute | solution.py:24
  196.5 11.5 %collective-permute-done.27 = bf16[128,2048]{1,0:T(8,128)(2,1)S(1)} collective-permute-done((bf16[128,2048]{1,0:T(8,128)(2,1)S(1)}, bf16[128,2048]{1,0:T(8,128)(2,1)S(1)}, u32[]{:S(2)}, u32[]{:S(2)}) %collective-permute-start.27) | collective-permute-done | bytes 524320 | tf_op jit(solution)/shard_map/ppermute | solution.py:24
  222.4 4.2 collective-permute-done.32
  228.0 54.9 %all-gather.5.cloned.1.call-done = bf16[2048,2176]{1,0:T(8,128)(2,1)} async-done(((bf16[512,2176]{1,0:T(8,128)(2,1)}), bf16[2048,2176]{1,0:T(8,128)(2,1)}) %all-gather.5.cloned.1.call-update) | async-done | bytes 8912912 | tf_op jit(solution)/shard_map/all_gather | solution.py:221
  282.9 10.7 %fusion.4 = f32[1024,1408]{1,0:T(8,128)S(1)} fusion(bf16[1024,2048]{1,0:T(8,128)(2,1)} %constant_dynamic-update-slice_fusion.21, bf16[2048,2176]{1,0:T(8,128)(2,1)} %all-gather.5.cloned.1.call-done), kind=kOutput, calls=%fused_computation.5 | convolution fusion | flops 5905580032 | bytes 15728640 | tf_op jit(solution)/shard_map/td,df->tf/dot_general | solution.py:604
  298.9 5.0 convolution_convert_fusion.2
  303.9 9.2 %fusion.7 = (bf16[1024,704]{1,0:T(8,128)(2,1)S(1)}, bf16[1024,704]{1,0:T(8,128)(2,1)S(1)}) fusion(f32[1024,1408]{1,0:T(8,128)} %copy-done.14, bf16[1024,2048]{1,0:T(8,128)(2,1)} %pad_maximum_fusion, bf16[2048,2176]{1,0:T(8,128)(2,1)} %all-gather.5.cloned.1.call-done), kind=kOutput, calls=%fused_computation.17 | convolution fusion | flops 2963603456 | bytes 16515072 | tf_op jit(solution)/shard_map/td,df->tf/dot_general | solution.py:614
  314.1 8.4 %fusion.10 = bf16[512,2048]{1,0:T(8,128)(2,1)} fusion(bf16[2048,2176]{1,0:T(8,128)(2,1)} %all-gather.5.cloned.1.call-done, bf16[1024,704]{1,0:T(8,128)(2,1)S(1)} %get-tuple-element.462, bf16[1024,704]{1,0:T(8,128)(2,1)S(1)} %get-tuple-element.463), kind=kOutput, calls=%fused_computation.25 | convolution fusion | flops 2956722176 | bytes 10747904 | tf_op jit(solution)/shard_map/tf,df->td/dot_general | solution.py:622
  322.5 5.1 fusion
  327.6 10.9 %convolution_convert_fusion = bf16[2048,1408]{1,0:T(8,128)(2,1)} fusion(bf16[1024,2048]{1,0:T(8,128)(2,1)} %constant_dynamic-update-slice_fusion.21, bf16[1024,1408]{1,0:T(8,128)(2,1)S(1)} %pad_maximum_fusion.2), kind=kOutput, calls=%fused_computation | convolution fusion | flops 5908463616 | bytes 12845056 | tf_op jit(solution)/shard_map/td,tf->df/dot_general | solution.py:632
  338.4 25.8 %reduce-scatter.4.cloned.1.call-done = bf16[512,704]{1,0:T(8,128)(2,1)} async-done(((bf16[2048,704]{1,0:T(8,128)(2,1)}), bf16[512,704]{1,0:T(8,128)(2,1)}) %reduce-scatter.4.cloned.1.call-update) | async-done | bytes 720912 | tf_op jit(solution)/shard_map/reduce_scatter | solution.py:224
  369.7 5.2 collective-permute-done.34
  382.8 3.7 convolution_convert_fusion.5
  386.5 5.8 collective-permute-done.37
  400.3 3.8 fusion.13
  404.2 8.0 %collective-permute-done.38 = bf16[128,2048]{1,0:T(8,128)(2,1)S(1)} collective-permute-done((bf16[128,2048]{1,0:T(8,128)(2,1)S(1)}, bf16[128,2048]{1,0:T(8,128)(2,1)S(1)}, u32[]{:S(2)}, u32[]{:S(2)}) %collective-permute-start.38) | collective-permute-done | bytes 524320 | tf_op jit(solution)/shard_map/ppermute | solution.py:24
  417.3 5.0 collective-permute-done.43
  423.4 3.8 collective-permute-done.41
  432.1 3.4 convolution_convert_fusion.17
  435.5 8.9 %attend_backward.1 = (bf16[32,2,16,768]{3,2,1,0:T(8,128)(2,1)S(1)}, f32[2,8,768]{2,1,0:T(8,128)S(1)}) custom-call(s32[2]{0:T(128)S(1)} %dynamic_slice.15.lens, bf16[32,2,16,768]{3,2,1,0:T(8,128)(2,1)S(1)} %get-tuple-element.337.qkv, bf16[32,2,16,256]{3,2,1,0:T(8,128)(2,1)S(1)} %bitcast.91, f32[32,2,16,256]{3,2,1,0:T(8,128)S(1)} %get-tuple-element.350.full, ...), custom_call_target="tpu_custom_call" | custom-call | tf_op jit(solution)/shard_map/attend_backward/pallas_call | solution.py:396
  444.5 5.0 convolution_convert_fusion.4
  457.7 3.9 fusion.18
  461.5 4.1 convolution_convert_fusion.1
  471.5 2.9 collective-permute-done.53
  474.4 7.6 %collective-permute-done.54 = bf16[32,2048]{1,0:T(8,128)(2,1)} collective-permute-done((bf16[32,2048]{1,0:T(8,128)(2,1)S(1)}, bf16[32,2048]{1,0:T(8,128)(2,1)}, u32[]{:S(2)}, u32[]{:S(2)}) %collective-permute-start.54) | collective-permute-done | bytes 131104 | tf_op jit(solution)/shard_map/ppermute | solution.py:24
  490.2 5.0 collective-permute-done.57
  500.7 9.2 %collective-permute-done.59 = bf16[128,2048]{1,0:T(8,128)(2,1)} collective-permute-done((bf16[128,2048]{1,0:T(8,128)(2,1)S(1)}, bf16[128,2048]{1,0:T(8,128)(2,1)}, u32[]{:S(2)}, u32[]{:S(2)}) %collective-permute-start.59) | collective-permute-done | bytes 524320 | tf_op jit(solution)/shard_map/ppermute | solution.py:24
  518.7 10.5 %collective-permute-done.67 = f32[4,2048]{1,0:T(4,128)S(1)} collective-permute-done((f32[4,2048]{1,0:T(4,128)S(1)}, f32[4,2048]{1,0:T(4,128)S(1)}, u32[]{:S(2)}, u32[]{:S(2)}) %collective-permute-start.67) | collective-permute-done | bytes 32800 | tf_op jit(solution)/shard_map/ppermute | solution.py:24
  530.8 12.4 %collective-permute-done.68 = f32[4,2048]{1,0:T(4,128)S(1)} collective-permute-done((f32[4,2048]{1,0:T(4,128)S(1)}, f32[4,2048]{1,0:T(4,128)S(1)}, u32[]{:S(2)}, u32[]{:S(2)}) %collective-permute-start.68) | collective-permute-done | bytes 32800 | tf_op jit(solution)/shard_map/ppermute | solution.py:24
  543.9 4.2 collective-permute-done.69
  550.4 3.6 collective-permute-done.70
  561.5 6.2 collective-permute-done.61
  567.7 5.5 collective-permute-done.62
  578.6 2.9 copy.70
  587.2 8.7 %fusion.131 = (bf16[256,2,1408]{2,1,0:T(2,128)(2,1)}, f32[256,2,1408]{2,1,0:T(2,128)S(1)}, f32[256,2,1408]{2,1,0:T(2,128)}) fusion(f32[256,2,1408]{2,1,0:T(2,128)S(1)} %copy-done.10, f32[256,2,1408]{2,1,0:T(2,128)} %param.37, f32[256,2,704]{2,1,0:T(2,128)S(1)} %copy.72, f32[256,2,704]{2,1,0:T(2,128)S(1)} %copy.71), kind=kLoop, calls=%fused_computation.365 | loop fusion | flops 7208960 | bytes 15859712 | tf_op jit(solution)/shard_map/convert_element_type | solution.py:740
  596.0 4.1 multiply_add_fusion
  (597 shorter events, 221.0 us)
Async XLA Ops:
  7.2 115.2 %all-gather.3.cloned.1.call-start = ((), (), s32[]{:S(2)}) async-start(), calls=%async_computation.3 | async-start | bytes 5242880 | tf_op jit(solution)/shard_map/all_gather | solution.py:221
  13.6 14.0 %collective-permute-start = (bf16[256,1024]{1,0:T(8,128)(2,1)}, bf16[256,1024]{1,0:T(8,128)(2,1)}, u32[]{:S(2)}, u32[]{:S(2)}) collective-permute-start(bf16[256,1024]{1,0:T(8,128)(2,1)} %broadcast_select_fusion.27), channel_id=1, source_target_pairs={{0,4},{4,0},{8,12},{12,8},{16,20},{20,16},{24,28},{28,24},{1,5},{5... | collective-permute-start | bytes 1572872 | tf_op jit(solution)/shard_map/ppermute | solution.py:24
  16.2 14.0 %collective-permute-start.1 = (bf16[32,2048]{1,0:T(8,128)(2,1)}, bf16[32,2048]{1,0:T(8,128)(2,1)S(1)}, u32[]{:S(2)}, u32[]{:S(2)}) collective-permute-start(bf16[32,2048]{1,0:T(8,128)(2,1)} %convolution_convert_fusion.15), channel_id=1, source_target_pairs={{0,8},{4,12},{8,0},{12,4},{16,24},{20,28},{24,16},{28,20},{1,9},{5... | collective-permute-start | bytes 393224 | tf_op jit(solution)/shard_map/ppermute | solution.py:24
  36.9 18.2 %collective-permute-start.7 = (bf16[256,1408]{1,0:T(8,128)(2,1)S(1)}, bf16[256,1408]{1,0:T(8,128)(2,1)}, u32[]{:S(2)}, u32[]{:S(2)}) collective-permute-start(bf16[256,1408]{1,0:T(8,128)(2,1)S(1)} %copy.60), channel_id=1, source_target_pairs={{0,4},{4,0},{8,12},{12,8},{16,20},{20,16},{24,28},{28,24},{1,5},{5... | collective-permute-start | bytes 2162696 | tf_op jit(solution)/shard_map/ppermute | solution.py:24
  37.5 19.0 %collective-permute-start.4 = (bf16[5,2048]{1,0:T(8,128)(2,1)S(1)}, bf16[5,2048]{1,0:T(8,128)(2,1)S(1)}, u32[]{:S(2)}, u32[]{:S(2)}) collective-permute-start(bf16[5,2048]{1,0:T(8,128)(2,1)S(1)} %copy-done.70), channel_id=1, source_target_pairs={{0,4},{4,0},{8,12},{12,8},{16,20},{20,16},{24,28},{28,24},{1,5},{5... | collective-permute-start | bytes 61448 | tf_op jit(solution)/shard_map/ppermute | solution.py:24
  39.0 17.5 %collective-permute-start.5 = (bf16[5,2048]{1,0:T(8,128)(2,1)S(1)}, bf16[5,2048]{1,0:T(8,128)(2,1)S(1)}, u32[]{:S(2)}, u32[]{:S(2)}) collective-permute-start(bf16[5,2048]{1,0:T(8,128)(2,1)S(1)} %copy-done.70), channel_id=1, source_target_pairs={{0,16},{4,20},{8,24},{12,28},{16,0},{20,4},{24,8},{28,12},{1,17},{... | collective-permute-start | bytes 61448 | tf_op jit(solution)/shard_map/ppermute | solution.py:24
  39.0 17.5 %collective-permute-start.6 = (bf16[5,2048]{1,0:T(8,128)(2,1)S(1)}, bf16[5,2048]{1,0:T(8,128)(2,1)S(1)}, u32[]{:S(2)}, u32[]{:S(2)}) collective-permute-start(bf16[5,2048]{1,0:T(8,128)(2,1)S(1)} %copy-done.70), channel_id=1, source_target_pairs={{0,20},{4,16},{8,28},{12,24},{16,4},{20,0},{24,12},{28,8},{1,21},{... | collective-permute-start | bytes 61448 | tf_op jit(solution)/shard_map/ppermute | solution.py:24
  42.3 240.7 %all-gather.5.cloned.1.call-start = ((), (), s32[]{:S(2)}) async-start(), calls=%async_computation.4 | async-start | bytes 11141120 | tf_op jit(solution)/shard_map/all_gather | solution.py:221
  122.5 21.0 %collective-permute-start.15 = (bf16[32,2048]{1,0:T(8,128)(2,1)}, bf16[32,2048]{1,0:T(8,128)(2,1)}, u32[]{:S(2)}, u32[]{:S(2)}) collective-permute-start(bf16[32,2048]{1,0:T(8,128)(2,1)} %convolution_convert_fusion.11), channel_id=1, source_target_pairs={{0,8},{4,12},{8,0},{12,4},{16,24},{20,28},{24,16},{28,20},{1,9},{5... | collective-permute-start | bytes 393224 | tf_op jit(solution)/shard_map/ppermute | solution.py:24
  122.5 21.0 %collective-permute-start.16 = (bf16[32,2048]{1,0:T(8,128)(2,1)}, bf16[32,2048]{1,0:T(8,128)(2,1)}, u32[]{:S(2)}, u32[]{:S(2)}) collective-permute-start(bf16[32,2048]{1,0:T(8,128)(2,1)} %convolution_convert_fusion.10), channel_id=1, source_target_pairs={{0,16},{4,20},{8,24},{12,28},{16,0},{20,4},{24,8},{28,12},{1,17},{... | collective-permute-start | bytes 393224 | tf_op jit(solution)/shard_map/ppermute | solution.py:24
  123.7 19.8 %collective-permute-start.17 = (bf16[32,2048]{1,0:T(8,128)(2,1)}, bf16[32,2048]{1,0:T(8,128)(2,1)}, u32[]{:S(2)}, u32[]{:S(2)}) collective-permute-start(bf16[32,2048]{1,0:T(8,128)(2,1)} %convolution_convert_fusion.9), channel_id=1, source_target_pairs={{0,24},{4,28},{8,16},{12,20},{16,8},{20,12},{24,0},{28,4},{1,25},{... | collective-permute-start | bytes 393224 | tf_op jit(solution)/shard_map/ppermute | solution.py:24
  126.0 238.3 %reduce-scatter.4.cloned.1.call-start = ((), (), s32[]{:S(2)}) async-start(), calls=%async_computation.5 | async-start | bytes 3932160 | tf_op jit(solution)/shard_map/reduce_scatter | solution.py:224
  148.3 21.2 %collective-permute-start.21 = (bf16[128,2048]{1,0:T(8,128)(2,1)S(1)}, bf16[128,2048]{1,0:T(8,128)(2,1)S(1)}, u32[]{:S(2)}, u32[]{:S(2)}) collective-permute-start(bf16[128,2048]{1,0:T(8,128)(2,1)S(1)} %maximum_select_fusion), channel_id=1, source_target_pairs={{0,2},{1,3},{2,0},{3,1},{4,6},{5,7},{6,4},{7,5},{8,10},{9,11},{10,... | collective-permute-start | bytes 1572872 | tf_op jit(solution)/shard_map/ppermute | solution.py:24
  149.8 19.7 %collective-permute-start.22 = (bf16[128,2048]{1,0:T(8,128)(2,1)S(1)}, bf16[128,2048]{1,0:T(8,128)(2,1)S(1)}, u32[]{:S(2)}, u32[]{:S(2)}) collective-permute-start(bf16[128,2048]{1,0:T(8,128)(2,1)S(1)} %maximum_select_fusion), channel_id=1, source_target_pairs={{0,4},{4,0},{8,12},{12,8},{16,20},{20,16},{24,28},{28,24},{1,5},{5... | collective-permute-start | bytes 1572872 | tf_op jit(solution)/shard_map/ppermute | solution.py:24
  152.5 15.8 %collective-permute-start.19 = (bf16[64,2048]{1,0:T(8,128)(2,1)S(1)}, bf16[64,2048]{1,0:T(8,128)(2,1)S(1)}, u32[]{:S(2)}, u32[]{:S(2)}) collective-permute-start(bf16[64,2048]{1,0:T(8,128)(2,1)S(1)} %get-tuple-element.479), channel_id=1, source_target_pairs={{0,2},{1,3},{2,0},{3,1},{4,6},{5,7},{6,4},{7,5},{8,10},{9,11},{10,... | collective-permute-start | bytes 786440 | tf_op jit(solution)/shard_map/ppermute | solution.py:24
  153.1 16.4 %collective-permute-start.20 = (bf16[64,2048]{1,0:T(8,128)(2,1)S(1)}, bf16[64,2048]{1,0:T(8,128)(2,1)S(1)}, u32[]{:S(2)}, u32[]{:S(2)}) collective-permute-start(bf16[64,2048]{1,0:T(8,128)(2,1)S(1)} %get-tuple-element.478), channel_id=1, source_target_pairs={{0,4},{4,0},{8,12},{12,8},{16,20},{20,16},{24,28},{28,24},{1,5},{5... | collective-permute-start | bytes 786440 | tf_op jit(solution)/shard_map/ppermute | solution.py:24
  171.2 19.5 %collective-permute-start.24 = (bf16[128,2048]{1,0:T(8,128)(2,1)S(1)}, bf16[128,2048]{1,0:T(8,128)(2,1)S(1)}, u32[]{:S(2)}, u32[]{:S(2)}) collective-permute-start(bf16[128,2048]{1,0:T(8,128)(2,1)S(1)} %pad_maximum_fusion.12), channel_id=1, source_target_pairs={{0,2},{1,3},{2,0},{3,1},{4,6},{5,7},{6,4},{7,5},{8,10},{9,11},{10,... | collective-permute-start | bytes 1572872 | tf_op jit(solution)/shard_map/ppermute | solution.py:24
  172.0 18.8 %collective-permute-start.23 = (bf16[128,2048]{1,0:T(8,128)(2,1)S(1)}, bf16[128,2048]{1,0:T(8,128)(2,1)S(1)}, u32[]{:S(2)}, u32[]{:S(2)}) collective-permute-start(bf16[128,2048]{1,0:T(8,128)(2,1)S(1)} %pad_maximum_fusion.11), channel_id=1, source_target_pairs={{0,4},{4,0},{8,12},{12,8},{16,20},{20,16},{24,28},{28,24},{1,5},{5... | collective-permute-start | bytes 1572872 | tf_op jit(solution)/shard_map/ppermute | solution.py:24
  173.6 17.1 %collective-permute-start.25 = (bf16[64,2048]{1,0:T(8,128)(2,1)S(1)}, bf16[64,2048]{1,0:T(8,128)(2,1)S(1)}, u32[]{:S(2)}, u32[]{:S(2)}) collective-permute-start(bf16[64,2048]{1,0:T(8,128)(2,1)S(1)} %slice.502), channel_id=1, source_target_pairs={{0,4},{4,0},{8,12},{12,8},{16,20},{20,16},{24,28},{28,24},{1,5},{5... | collective-permute-start | bytes 786440 | tf_op jit(solution)/shard_map/ppermute | solution.py:24
  174.3 16.5 %collective-permute-start.26 = (bf16[64,2048]{1,0:T(8,128)(2,1)S(1)}, bf16[64,2048]{1,0:T(8,128)(2,1)S(1)}, u32[]{:S(2)}, u32[]{:S(2)}) collective-permute-start(bf16[64,2048]{1,0:T(8,128)(2,1)S(1)} %slice.503), channel_id=1, source_target_pairs={{0,2},{1,3},{2,0},{3,1},{4,6},{5,7},{6,4},{7,5},{8,10},{9,11},{10,... | collective-permute-start | bytes 786440 | tf_op jit(solution)/shard_map/ppermute | solution.py:24
  190.8 18.2 %collective-permute-start.29 = (bf16[512,2048]{1,0:T(8,128)(2,1)S(1)}, bf16[512,2048]{1,0:T(8,128)(2,1)S(1)}, u32[]{:S(2)}, u32[]{:S(2)}) collective-permute-start(bf16[512,2048]{1,0:T(8,128)(2,1)S(1)} %constant_dynamic-update-slice_fusion.11), channel_id=1, source_target_pairs={{0,1},{1,0},{2,3},{3,2},{4,5},{5,4},{6,7},{7,6},{8,9},{9,8},{10,11... | collective-permute-start | bytes 6291464 | tf_op jit(solution)/shard_map/ppermute | solution.py:24
  193.7 14.4 %collective-permute-start.27 = (bf16[128,2048]{1,0:T(8,128)(2,1)S(1)}, bf16[128,2048]{1,0:T(8,128)(2,1)S(1)}, u32[]{:S(2)}, u32[]{:S(2)}) collective-permute-start(bf16[128,2048]{1,0:T(8,128)(2,1)S(1)} %add_convert_fusion.1), channel_id=1, source_target_pairs={{0,2},{1,3},{2,0},{3,1},{4,6},{5,7},{6,4},{7,5},{8,10},{9,11},{10,... | collective-permute-start | bytes 1572872 | tf_op jit(solution)/shard_map/ppermute | solution.py:24
  195.1 14.0 %collective-permute-start.28 = (bf16[128,2048]{1,0:T(8,128)(2,1)S(1)}, bf16[128,2048]{1,0:T(8,128)(2,1)S(1)}, u32[]{:S(2)}, u32[]{:S(2)}) collective-permute-start(bf16[128,2048]{1,0:T(8,128)(2,1)S(1)} %add_convert_fusion.1), channel_id=1, source_target_pairs={{0,4},{4,0},{8,12},{12,8},{16,20},{20,16},{24,28},{28,24},{1,5},{5... | collective-permute-start | bytes 1572872 | tf_op jit(solution)/shard_map/ppermute | solution.py:24
  303.9 178.2 %reduce-scatter.6.cloned.1.call-start = ((), (), s32[]{:S(2)}) async-start(), calls=%async_computation.6 | async-start | bytes 7208960 | tf_op jit(solution)/shard_map/reduce_scatter | solution.py:224
  322.4 16.0 %collective-permute-start.33 = (bf16[512,2048]{1,0:T(8,128)(2,1)}, bf16[512,2048]{1,0:T(8,128)(2,1)}, u32[]{:S(2)}, u32[]{:S(2)}) collective-permute-start(bf16[512,2048]{1,0:T(8,128)(2,1)} %fusion.10), channel_id=1, source_target_pairs={{0,1},{1,0},{2,3},{3,2},{4,5},{5,4},{6,7},{7,6},{8,9},{9,8},{10,11... | collective-permute-start | bytes 6291464 | tf_op jit(solution)/shard_map/ppermute | solution.py:24
  369.5 204.4 %reduce-scatter.8.cloned.1.call-start = ((), (), s32[]{:S(2)}) async-start(), calls=%async_computation.7 | async-start | bytes 5242880 | tf_op jit(solution)/shard_map/reduce_scatter | solution.py:224
  381.2 13.0 %collective-permute-start.36 = (bf16[128,2048]{1,0:T(8,128)(2,1)S(1)}, bf16[128,2048]{1,0:T(8,128)(2,1)S(1)}, u32[]{:S(2)}, u32[]{:S(2)}) collective-permute-start(bf16[128,2048]{1,0:T(8,128)(2,1)S(1)} %pad_maximum_fusion.13), channel_id=1, source_target_pairs={{0,4},{4,0},{8,12},{12,8},{16,20},{20,16},{24,28},{28,24},{1,5},{5... | collective-permute-start | bytes 1572872 | tf_op jit(solution)/shard_map/ppermute | solution.py:24
  394.2 18.7 %collective-permute-start.40 = (bf16[512,2048]{1,0:T(8,128)(2,1)S(1)}, bf16[512,2048]{1,0:T(8,128)(2,1)S(1)}, u32[]{:S(2)}, u32[]{:S(2)}) collective-permute-start(bf16[512,2048]{1,0:T(8,128)(2,1)S(1)} %convolution_convert_fusion.5), channel_id=1, source_target_pairs={{0,1},{1,0},{2,3},{3,2},{4,5},{5,4},{6,7},{7,6},{8,9},{9,8},{10,11... | collective-permute-start | bytes 6291464 | tf_op jit(solution)/shard_map/ppermute | solution.py:24
  397.9 14.3 %collective-permute-start.38 = (bf16[128,2048]{1,0:T(8,128)(2,1)S(1)}, bf16[128,2048]{1,0:T(8,128)(2,1)S(1)}, u32[]{:S(2)}, u32[]{:S(2)}) collective-permute-start(bf16[128,2048]{1,0:T(8,128)(2,1)S(1)} %get-tuple-element.343), channel_id=1, source_target_pairs={{0,2},{1,3},{2,0},{3,1},{4,6},{5,7},{6,4},{7,5},{8,10},{9,11},{10,... | collective-permute-start | bytes 1572872 | tf_op jit(solution)/shard_map/ppermute | solution.py:24
  398.9 14.0 %collective-permute-start.39 = (bf16[128,2048]{1,0:T(8,128)(2,1)S(1)}, bf16[128,2048]{1,0:T(8,128)(2,1)S(1)}, u32[]{:S(2)}, u32[]{:S(2)}) collective-permute-start(bf16[128,2048]{1,0:T(8,128)(2,1)S(1)} %get-tuple-element.343), channel_id=1, source_target_pairs={{0,4},{4,0},{8,12},{12,8},{16,20},{20,16},{24,28},{28,24},{1,5},{5... | collective-permute-start | bytes 1572872 | tf_op jit(solution)/shard_map/ppermute | solution.py:24
  428.8 20.7 %collective-permute-start.47 = (bf16[128,2048]{1,0:T(8,128)(2,1)}, bf16[128,2048]{1,0:T(8,128)(2,1)}, u32[]{:S(2)}, u32[]{:S(2)}) collective-permute-start(bf16[128,2048]{1,0:T(8,128)(2,1)} %pad_maximum_fusion.16), channel_id=1, source_target_pairs={{0,2},{1,3},{2,0},{3,1},{4,6},{5,7},{6,4},{7,5},{8,10},{9,11},{10,... | collective-permute-start | bytes 1572872 | tf_op jit(solution)/shard_map/ppermute | solution.py:24
  429.9 19.6 %collective-permute-start.46 = (bf16[128,2048]{1,0:T(8,128)(2,1)S(1)}, bf16[128,2048]{1,0:T(8,128)(2,1)S(1)}, u32[]{:S(2)}, u32[]{:S(2)}) collective-permute-start(bf16[128,2048]{1,0:T(8,128)(2,1)S(1)} %pad_maximum_fusion.15), channel_id=1, source_target_pairs={{0,4},{4,0},{8,12},{12,8},{16,20},{20,16},{24,28},{28,24},{1,5},{5... | collective-permute-start | bytes 1572872 | tf_op jit(solution)/shard_map/ppermute | solution.py:24
  450.1 16.9 %collective-permute-start.49 = (f32[1,768]{1,0:T(1,128)}, f32[1,768]{1,0:T(1,128)S(1)}, u32[]{:S(2)}, u32[]{:S(2)}) collective-permute-start(f32[1,768]{1,0:T(1,128)} %broadcast_in_dim.64), channel_id=1, source_target_pairs={{0,16},{4,20},{8,24},{12,28},{16,0},{20,4},{24,8},{28,12},{1,17},{... | collective-permute-start | bytes 9224 | tf_op jit(solution)/shard_map/ppermute | solution.py:24
  450.4 16.7 %collective-permute-start.50 = (f32[1,768]{1,0:T(1,128)}, f32[1,768]{1,0:T(1,128)S(1)}, u32[]{:S(2)}, u32[]{:S(2)}) collective-permute-start(f32[1,768]{1,0:T(1,128)} %broadcast_in_dim.64), channel_id=1, source_target_pairs={{0,8},{4,12},{8,0},{12,4},{16,24},{20,28},{24,16},{28,20},{1,9},{5... | collective-permute-start | bytes 9224 | tf_op jit(solution)/shard_map/ppermute | solution.py:24
  451.8 19.7 %collective-permute-start.51 = (f32[1,768]{1,0:T(1,128)}, f32[1,768]{1,0:T(1,128)}, u32[]{:S(2)}, u32[]{:S(2)}) collective-permute-start(f32[1,768]{1,0:T(1,128)} %broadcast_in_dim.64), channel_id=1, source_target_pairs={{0,24},{4,28},{8,16},{12,20},{16,8},{20,12},{24,0},{28,4},{1,25},{... | collective-permute-start | bytes 9224 | tf_op jit(solution)/shard_map/ppermute | solution.py:24
  453.6 28.5 %collective-permute-start.48 = (bf16[512,2048]{1,0:T(8,128)(2,1)}, bf16[512,2048]{1,0:T(8,128)(2,1)S(1)}, u32[]{:S(2)}, u32[]{:S(2)}) collective-permute-start(bf16[512,2048]{1,0:T(8,128)(2,1)} %convolution_convert_fusion.4), channel_id=1, source_target_pairs={{0,1},{1,0},{2,3},{3,2},{4,5},{5,4},{6,7},{7,6},{8,9},{9,8},{10,11... | collective-permute-start | bytes 6291464 | tf_op jit(solution)/shard_map/ppermute | solution.py:24
  455.9 15.6 %collective-permute-start.52 = (bf16[32,2048]{1,0:T(8,128)(2,1)}, bf16[32,2048]{1,0:T(8,128)(2,1)}, u32[]{:S(2)}, u32[]{:S(2)}) collective-permute-start(bf16[32,2048]{1,0:T(8,128)(2,1)} %get-tuple-element.520), channel_id=1, source_target_pairs={{0,8},{4,12},{8,0},{12,4},{16,24},{20,28},{24,16},{28,20},{1,9},{5... | collective-permute-start | bytes 393224 | tf_op jit(solution)/shard_map/ppermute | solution.py:24
  467.1 14.9 %collective-permute-start.54 = (bf16[32,2048]{1,0:T(8,128)(2,1)S(1)}, bf16[32,2048]{1,0:T(8,128)(2,1)}, u32[]{:S(2)}, u32[]{:S(2)}) collective-permute-start(bf16[32,2048]{1,0:T(8,128)(2,1)S(1)} %get-tuple-element.518), channel_id=1, source_target_pairs={{0,24},{4,28},{8,16},{12,20},{16,8},{20,12},{24,0},{28,4},{1,25},{... | collective-permute-start | bytes 393224 | tf_op jit(solution)/shard_map/ppermute | solution.py:24
  496.9 13.0 %collective-permute-start.59 = (bf16[128,2048]{1,0:T(8,128)(2,1)S(1)}, bf16[128,2048]{1,0:T(8,128)(2,1)}, u32[]{:S(2)}, u32[]{:S(2)}) collective-permute-start(bf16[128,2048]{1,0:T(8,128)(2,1)S(1)} %pad_maximum_fusion.18), channel_id=1, source_target_pairs={{0,2},{1,3},{2,0},{3,1},{4,6},{5,7},{6,4},{7,5},{8,10},{9,11},{10,... | collective-permute-start | bytes 1572872 | tf_op jit(solution)/shard_map/ppermute | solution.py:24
  514.2 59.7 %collective-permute-start.65 = (bf16[128,2048]{1,0:T(8,128)(2,1)S(1)}, bf16[128,2048]{1,0:T(8,128)(2,1)S(1)}, u32[]{:S(2)}, u32[]{:S(2)}) collective-permute-start(bf16[128,2048]{1,0:T(8,128)(2,1)S(1)} %convolution_convert_fusion.8), channel_id=1, source_target_pairs={{0,2},{1,3},{2,0},{3,1},{4,6},{5,7},{6,4},{7,5},{8,10},{9,11},{10,... | collective-permute-start | bytes 1572872 | tf_op jit(solution)/shard_map/ppermute | solution.py:24
  515.9 40.8 %collective-permute-start.64 = (bf16[256,704]{1,0:T(8,128)(2,1)S(1)}, bf16[256,704]{1,0:T(8,128)(2,1)S(1)}, u32[]{:S(2)}, u32[]{:S(2)}) collective-permute-start(bf16[256,704]{1,0:T(8,128)(2,1)S(1)} %broadcast_select_fusion.29), channel_id=1, source_target_pairs={{0,4},{4,0},{8,12},{12,8},{16,20},{20,16},{24,28},{28,24},{1,5},{5... | collective-permute-start | bytes 1081352 | tf_op jit(solution)/shard_map/ppermute | solution.py:24
  517.4 42.7 %collective-permute-start.63 = (bf16[256,1408]{1,0:T(8,128)(2,1)S(1)}, bf16[256,1408]{1,0:T(8,128)(2,1)S(1)}, u32[]{:S(2)}, u32[]{:S(2)}) collective-permute-start(bf16[256,1408]{1,0:T(8,128)(2,1)S(1)} %broadcast_select_fusion.3), channel_id=1, source_target_pairs={{0,4},{4,0},{8,12},{12,8},{16,20},{20,16},{24,28},{28,24},{1,5},{5... | collective-permute-start | bytes 2162696 | tf_op jit(solution)/shard_map/ppermute | solution.py:24
  529.2 13.9 %collective-permute-start.68 = (f32[4,2048]{1,0:T(4,128)S(1)}, f32[4,2048]{1,0:T(4,128)S(1)}, u32[]{:S(2)}, u32[]{:S(2)}) collective-permute-start(f32[4,2048]{1,0:T(4,128)S(1)} %fusion.158), channel_id=1, source_target_pairs={{0,4},{4,0},{8,12},{12,8},{16,20},{20,16},{24,28},{28,24},{1,5},{5... | collective-permute-start | bytes 98312 | tf_op jit(solution)/shard_map/ppermute | solution.py:24
  554.0 13.7 %collective-permute-start.61 = (bf16[32,2048]{1,0:T(8,128)(2,1)S(1)}, bf16[32,2048]{1,0:T(8,128)(2,1)S(1)}, u32[]{:S(2)}, u32[]{:S(2)}) collective-permute-start(bf16[32,2048]{1,0:T(8,128)(2,1)S(1)} %get-tuple-element.515), channel_id=1, source_target_pairs={{0,16},{4,20},{8,24},{12,28},{16,0},{20,4},{24,8},{28,12},{1,17},{... | collective-permute-start | bytes 393224 | tf_op jit(solution)/shard_map/ppermute | solution.py:24
  556.7 16.6 %collective-permute-start.62 = (bf16[32,2048]{1,0:T(8,128)(2,1)S(1)}, bf16[32,2048]{1,0:T(8,128)(2,1)S(1)}, u32[]{:S(2)}, u32[]{:S(2)}) collective-permute-start(bf16[32,2048]{1,0:T(8,128)(2,1)S(1)} %get-tuple-element.514), channel_id=1, source_target_pairs={{0,24},{4,28},{8,16},{12,20},{16,8},{20,12},{24,0},{28,4},{1,25},{... | collective-permute-start | bytes 393224 | tf_op jit(solution)/shard_map/ppermute | solution.py:24
  576.1 27.1 %collective-permute-start.73 = (bf16[256,1024]{1,0:T(8,128)(2,1)}, bf16[256,1024]{1,0:T(8,128)(2,1)}, u32[]{:S(2)}, u32[]{:S(2)}) collective-permute-start(bf16[256,1024]{1,0:T(8,128)(2,1)} %broadcast_select_fusion.23), channel_id=1, source_target_pairs={{0,4},{4,0},{8,12},{12,8},{16,20},{20,16},{24,28},{28,24},{1,5},{5... | collective-permute-start | bytes 1572872 | tf_op jit(solution)/shard_map/ppermute | solution.py:24
  585.6 19.6 %collective-permute-start.72 = (bf16[256,2048]{1,0:T(8,128)(2,1)S(1)}, bf16[256,2048]{1,0:T(8,128)(2,1)S(1)}, u32[]{:S(2)}, u32[]{:S(2)}) collective-permute-start(bf16[256,2048]{1,0:T(8,128)(2,1)S(1)} %pad_maximum_fusion.5), channel_id=1, source_target_pairs={{0,1},{1,0},{2,3},{3,2},{4,5},{5,4},{6,7},{7,6},{8,9},{9,8},{10,11... | collective-permute-start | bytes 3145736 | tf_op jit(solution)/shard_map/ppermute | solution.py:24
  587.2 19.9 %collective-permute-start.71 = (bf16[128,2048]{1,0:T(8,128)(2,1)S(1)}, bf16[128,2048]{1,0:T(8,128)(2,1)S(1)}, u32[]{:S(2)}, u32[]{:S(2)}) collective-permute-start(bf16[128,2048]{1,0:T(8,128)(2,1)S(1)} %convolution_convert_fusion.7), channel_id=1, source_target_pairs={{0,2},{1,3},{2,0},{3,1},{4,6},{5,7},{6,4},{7,5},{8,10},{9,11},{10,... | collective-permute-start | bytes 1572872 | tf_op jit(solution)/shard_map/ppermute | solution.py:24
  (161 other events, 1714.7 us)
Sparse Core Ops, SparseCore 0:
  42.4 80.0 all-gather.2
  126.1 156.7 all-gather.4
  304.0 60.2 reduce-scatter.3
  369.6 106.2 reduce-scatter.5
  483.6 87.1 reduce-scatter.7

commit v5 on v4

--- a/solution.py
+++ b/solution.py
@@ -461,11 +461,11 @@
     )
     lens = lax.dynamic_slice_in_dim(lengths, plan.group * rows, rows, 0)
 
-    def over_masks(array, masks):
+    def over_masks(array, masks, axis="seq"):
         sums = [0]
         for mask in masks:
             sums = sums + [m | mask for m in sums]
-        return [swap(array, "seq", m) for m in sums[1:]]
+        return [swap(array, axis, m) for m in sums[1:]]
 
     def total_of(array, got):
         for other in got:
@@ -686,9 +686,9 @@
     bias_sum = jnp.sum(bias_sum[:, 0], 0, keepdims=True)
     bias_got = over_masks(bias_sum, plan.outer)
     result = second + plan.sum_end(out_near, out_sides)
-    out_back = plan.over_groups(plan.returning_rows(result.astype(bf16)))
-    product, got, grad_attn, bias_sum, bias_got, down_sum, out_back, gate_sum = hold(
-        product, got, grad_attn, bias_sum, bias_got, down_sum, out_back, gate_sum
+    out_returning = plan.returning_rows(result.astype(bf16))
+    product, got, grad_attn, bias_sum, bias_got, down_sum, out_returning, gate_sum = hold(
+        product, got, grad_attn, bias_sum, bias_got, down_sum, out_returning, gate_sum
     )
     attn_sum = plan.sum_blocks(grad_attn)
 
@@ -696,21 +696,33 @@
     near = (product, got)
     corner = plan.sum_corner(near)
     bias_got = [swap(bias_sum, "seq", plan.inner_mask(j)) for j in range(1, parts)]
-    near, corner, bias_sum, bias_got, down_sum, gate_sum, out_back = hold(
-        near, corner, bias_sum, bias_got, down_sum, gate_sum, out_back
-    )
+    near, corner, bias_sum, bias_got, down_sum, gate_sum, out_returning = hold(
+        near, corner, bias_sum, bias_got, down_sum, gate_sum, out_returning
+    )
+    out_back = plan.over_groups(out_returning)
     sides = plan.sum_sides(near, corner)
     near, sides, out_back, down_sum, gate_sum = hold(near, sides, out_back, down_sum, gate_sum)
 
+    def ordered_as(grad, *order):
+        return with_layout_constraint(grad, Layout(order))
+
+    beta = min(0.999, (1 + STEP) / (10 + STEP))
+
+    def stepped(index, grad, master, moment, average):
+        grad = grad + decays[index] * master
+        moment = 0.9 * moment + grad
+        weight = master - rates[index] * (grad + 0.9 * moment)
+        return moment, weight, beta * average + (1.0 - beta) * weight, weight.astype(bf16)
+
     def along_tp(own):
         return gather(own, [("tp", m, m) for m in plan.tp_masks[:0:-1]])
 
+    out_pieces = along_tp(plan.returned_rows(out_back, quarter, inputs.shape[1]))
     grad_h1 = plan.sum_end(near, sides)
     grad_input = grad_second + norm_back(grad_h1, n_first, i_first, gains[0])
     back = plan.over_groups(plan.returning_rows(grad_input.astype(bf16)))
     grad_gate = plan.collect_home(gate_sum)
     grad_down = plan.collect_home(down_sum)
-    out_pieces = along_tp(plan.returned_rows(out_back, quarter, inputs.shape[1]))
     sums = jnp.stack(
         [
             jnp.sum(grad_h1 * n_first, 0),
@@ -719,25 +731,17 @@
             jnp.sum(grad_h2, 0),
         ]
     )
-    for mask in plan.tp_masks:
-        sums = sums + swap(sums, "tp", mask)
-    sums = plan.restored(sums)
-    for mask in seq_masks:
-        sums = sums + swap(sums, "seq", mask)
-    back, grad_gate, grad_down, out_pieces, sums, attn_sum = hold(
-        back, grad_gate, grad_down, out_pieces, sums, attn_sum
-    )
-
-    def ordered_as(grad, *order):
-        return with_layout_constraint(grad, Layout(order))
-
-    beta = min(0.999, (1 + STEP) / (10 + STEP))
-
-    def stepped(index, grad, master, moment, average):
-        grad = grad + decays[index] * master
-        moment = 0.9 * moment + grad
-        weight = master - rates[index] * (grad + 0.9 * moment)
-        return moment, weight, beta * average + (1.0 - beta) * weight, weight.astype(bf16)
+    sums_got = over_masks(sums, plan.outer)
+    back, grad_gate, grad_down, sums, sums_got, out_pieces = hold(
+        back, grad_gate, grad_down, sums, sums_got, out_pieces
+    )
+
+    pieces = along_tp(plan.returned_rows(back, quarter, inputs.shape[1]))
+    sums = total_of(sums, sums_got)
+    sums_got = over_masks(sums, plan.tp_masks, "tp")
+    pieces, out_pieces, sums, sums_got, grad_gate, grad_down, attn_sum = hold(
+        pieces, out_pieces, sums, sums_got, grad_gate, grad_down, attn_sum
+    )
 
     grad_gate = ordered_as(
         joined([part.reshape(part.shape[0], 2, hidden) for part in grad_gate], -1), 0, 1, 2
@@ -745,21 +749,26 @@
     gate = stepped(4, grad_gate, gate_master, moment_gate, average_gate)
     grad_down = ordered_as(joined(grad_down, -1), 0, 1)
     down = stepped(5, grad_down, down_master, moment_down, average_down)
-    core_masks = plan.tp_masks[:1]
-    pieces = along_tp(plan.returned_rows(back, quarter, inputs.shape[1]))
     attn_home = plan.collect_home(attn_sum)
-
-    def across_cores(pieces):
-        keys = sorted(pieces)
-        got = swap(joined([pieces[k] for k in keys]), "tp", core_masks[0])
-        size = got.shape[0] // len(keys)
-        pieces = {**pieces, **{k | core_masks[0]: got[i * size : (i + 1) * size] for i, k in enumerate(keys)}}
-        return plan.of_tp(pieces).reshape(inputs.shape)
-
-    layer_out = across_cores(out_pieces)
-    pieces, sums, layer_out, gate, down, attn_home = hold(pieces, sums, layer_out, gate, down, attn_home)
-
-    input_grad = across_cores(pieces)
+    sums = plan.restored(total_of(sums, sums_got))
+    sums_got = over_masks(sums, plan.inner)
+    keys = sorted(pieces)
+    core = plan.tp_masks[0]
+    near = joined([pieces[k] for k in keys] + [out_pieces[k] for k in keys])
+    other = swap(near, "tp", core)
+    attn_home, sums, sums_got, near, other, gate, down = hold(
+        attn_home, sums, sums_got, near, other, gate, down
+    )
+
+    sums = total_of(sums, sums_got)
+    size = pieces[0].shape[0]
+    whole = []
+    for part in range(2):
+        at = part * len(keys)
+        found = {k: near[(at + i) * size : (at + i + 1) * size] for i, k in enumerate(keys)}
+        found.update({k | core: other[(at + i) * size : (at + i + 1) * size] for i, k in enumerate(keys)})
+        whole.append(plan.of_tp(found).reshape(inputs.shape))
+    input_grad, layer_out = whole
 
     got = [part.reshape(3, heads_here, HD) for part in [bias_sum] + bias_got]
     bias_sum = joined(pick(got, plan.part_flags), 1)

time: 635 us -> 643 us (1.013)
  waiting for transfers between devices: 283 us -> 294 us
  local copies, waits for them, and re-layouts: 53.2 us -> 59.9 us
    ppermute x75 -> x76, waiting for transfers between devices: 185 us -> 195 us  [swap(): return lax.ppermute(array, axis, pairs)]
    unnamed x278 -> x273, local copies, waits for them, and re-layouts: 22.9 us -> 30.8 us
    ppermute x75 -> x76, starting transfers between devices: 74.3 us -> 74.1 us  [swap(): return lax.ppermute(array, axis, pairs)]
  transfers between devices with their start and end apart: 80 -> 81, of which waited for: 39 -> 38; matrix products, arithmetic and copies ran while one was open for 30% -> 26% of each run, Pallas kernels for 3% -> 2%
where the time goes in v5:
time: 643 us; the launch traced here: 635 us
  waiting for transfers between devices  294 us (46%)
  matrix products  96.7 us (15%)
  other arithmetic  76.8 us (12%)
  starting transfers between devices  74.7 us (12%)
  local copies, waits for them, and re-layouts  59.9 us (9%)
  between operations  16.6 us (3%)
  Pallas kernels  15.8 us (2%)
    ppermute x76, waiting for transfers between devices, swap(): return lax.ppermute(array, axis, pairs)  195 us
    ppermute x76, starting transfers between devices, swap(): return lax.ppermute(array, axis, pairs)  74.1 us
    all_gather x2, waiting for transfers between devices, all_blocks(): lax.all_gather(block, 'seq', axis_index_groups=self.lists(), axis=0, tile...  72.2 us
    unnamed x273, local copies, waits for them, and re-layouts  30.8 us
    reduce_scatter x3, waiting for transfers between devices, sum_blocks(): lax.psum_scatter(product, 'seq', scatter_dimension=0, axis_index_groups=s...  27.3 us
    dot_general x2, matrix products, gate_product(): jnp.einsum('tf,df->td', grad_gated[lo:hi], w_gate, preferred_element_type...  13.4 us
    convert_element_type x5, other arithmetic, stepped(): weight.astype(bf16)  12.9 us
  transfers between devices with their start and end apart: 81, of which 38 were waited for; matrix products, arithmetic and copies ran while one was open for 26% of the time, Pallas kernels for 2%

profile of v5, /device:TPU:16, one launch (start us, length us, event | category | flops | bytes accessed | tf_op | source)
XLA Modules:
  0.0 634.8 jit_solution(3438691019009854701)
XLA Ops:
  24.3 3.3 collective-permute-done
  31.9 3.2 copy.59
  39.0 2.9 collective-permute-start.6
  42.3 12.9 %collective-permute-done.7 = bf16[256,1408]{1,0:T(8,128)(2,1)} collective-permute-done((bf16[256,1408]{1,0:T(8,128)(2,1)S(1)}, bf16[256,1408]{1,0:T(8,128)(2,1)}, u32[]{:S(2)}, u32[]{:S(2)}) %collective-permute-start.7) | collective-permute-done | bytes 720928 | tf_op jit(solution)/shard_map/ppermute | solution.py:24
  60.1 6.8 %collective-permute-done.9 = bf16[256,704]{1,0:T(8,128)(2,1)S(1)} collective-permute-done((bf16[256,704]{1,0:T(8,128)(2,1)S(1)}, bf16[256,704]{1,0:T(8,128)(2,1)S(1)}, u32[]{:S(2)}, u32[]{:S(2)}) %collective-permute-start.9) | collective-permute-done | bytes 360480 | tf_op jit(solution)/shard_map/ppermute | solution.py:24
  73.0 2.9 concatenate.178
  75.9 4.2 collective-permute-done.10
  80.0 2.7 collective-permute-done.11
  100.3 3.3 collective-permute-done.14
  105.1 17.3 %all-gather.3.cloned.1.call-done = bf16[2048,1024]{1,0:T(8,128)(2,1)} async-done(((bf16[512,1024]{1,0:T(8,128)(2,1)}), bf16[2048,1024]{1,0:T(8,128)(2,1)}) %all-gather.3.cloned.1.call-update) | async-done | bytes 4194320 | tf_op jit(solution)/shard_map/all_gather | solution.py:221
  126.2 6.1 fusion.21
  132.3 6.9 %attend_forward.1 = (bf16[32,2,16,768]{3,2,1,0:T(8,128)(2,1)S(1)}, bf16[32,2,16,256]{3,2,1,0:T(8,128)(2,1)S(1)}, f32[32,2,16,256]{3,2,1,0:T(8,128)S(1)}, f32[2,512,128]{2,1,0:T(8,128)S(1)}) custom-call(s32[2]{0:T(128)S(1)} %dynamic_slice.15.lens, f32[32,2,16,768]{3,2,1,0:T(8,128)S(1)} %bitcast.90, f32[1,768]{1,0:T(1,128)S(1)} %fusion.99.shift, ...), custom_call_target="tpu_custom_call" | custom-call | tf_op jit(solution)/shard_map/attend_forward/pallas_call | solution.py:374
  140.1 3.4 convolution_convert_fusion.3
  153.6 14.7 %collective-permute-done.19 = bf16[64,2048]{1,0:T(8,128)(2,1)S(1)} collective-permute-done((bf16[64,2048]{1,0:T(8,128)(2,1)S(1)}, bf16[64,2048]{1,0:T(8,128)(2,1)S(1)}, u32[]{:S(2)}, u32[]{:S(2)}) %collective-permute-start.19) | collective-permute-done | bytes 262176 | tf_op jit(solution)/shard_map/ppermute | solution.py:24
  175.8 14.9 %collective-permute-done.25 = bf16[64,2048]{1,0:T(8,128)(2,1)S(1)} collective-permute-done((bf16[64,2048]{1,0:T(8,128)(2,1)S(1)}, bf16[64,2048]{1,0:T(8,128)(2,1)S(1)}, u32[]{:S(2)}, u32[]{:S(2)}) %collective-permute-start.25) | collective-permute-done | bytes 262176 | tf_op jit(solution)/shard_map/ppermute | solution.py:24
  196.5 11.5 %collective-permute-done.27 = bf16[128,2048]{1,0:T(8,128)(2,1)S(1)} collective-permute-done((bf16[128,2048]{1,0:T(8,128)(2,1)S(1)}, bf16[128,2048]{1,0:T(8,128)(2,1)S(1)}, u32[]{:S(2)}, u32[]{:S(2)}) %collective-permute-start.27) | collective-permute-done | bytes 524320 | tf_op jit(solution)/shard_map/ppermute | solution.py:24
  214.0 2.8 collective-permute-done.30
  222.4 4.2 collective-permute-done.32
  228.0 54.9 %all-gather.5.cloned.1.call-done = bf16[2048,2176]{1,0:T(8,128)(2,1)} async-done(((bf16[512,2176]{1,0:T(8,128)(2,1)}), bf16[2048,2176]{1,0:T(8,128)(2,1)}) %all-gather.5.cloned.1.call-update) | async-done | bytes 8912912 | tf_op jit(solution)/shard_map/all_gather | solution.py:221
  282.9 10.7 %fusion.4 = f32[1024,1408]{1,0:T(8,128)S(1)} fusion(bf16[1024,2048]{1,0:T(8,128)(2,1)} %constant_dynamic-update-slice_fusion.21, bf16[2048,2176]{1,0:T(8,128)(2,1)} %all-gather.5.cloned.1.call-done), kind=kOutput, calls=%fused_computation.5 | convolution fusion | flops 5905580032 | bytes 15728640 | tf_op jit(solution)/shard_map/td,df->tf/dot_general | solution.py:604
  298.8 5.0 convolution_convert_fusion.2
  303.9 9.2 %fusion.7 = (bf16[1024,704]{1,0:T(8,128)(2,1)S(1)}, bf16[1024,704]{1,0:T(8,128)(2,1)S(1)}) fusion(f32[1024,1408]{1,0:T(8,128)} %copy-done.14, bf16[1024,2048]{1,0:T(8,128)(2,1)} %pad_maximum_fusion, bf16[2048,2176]{1,0:T(8,128)(2,1)} %all-gather.5.cloned.1.call-done), kind=kOutput, calls=%fused_computation.17 | convolution fusion | flops 2963603456 | bytes 16515072 | tf_op jit(solution)/shard_map/td,df->tf/dot_general | solution.py:614
  314.0 8.4 %fusion.10 = bf16[512,2048]{1,0:T(8,128)(2,1)} fusion(bf16[2048,2176]{1,0:T(8,128)(2,1)} %all-gather.5.cloned.1.call-done, bf16[1024,704]{1,0:T(8,128)(2,1)S(1)} %get-tuple-element.492, bf16[1024,704]{1,0:T(8,128)(2,1)S(1)} %get-tuple-element.493), kind=kOutput, calls=%fused_computation.25 | convolution fusion | flops 2956722176 | bytes 10747904 | tf_op jit(solution)/shard_map/tf,df->td/dot_general | solution.py:622
  322.4 5.0 fusion
  327.5 10.8 %convolution_convert_fusion = bf16[2048,1408]{1,0:T(8,128)(2,1)} fusion(bf16[1024,2048]{1,0:T(8,128)(2,1)} %constant_dynamic-update-slice_fusion.21, bf16[1024,1408]{1,0:T(8,128)(2,1)S(1)} %pad_maximum_fusion.2), kind=kOutput, calls=%fused_computation | convolution fusion | flops 5908463616 | bytes 12845056 | tf_op jit(solution)/shard_map/td,tf->df/dot_general | solution.py:632
  338.3 25.9 %reduce-scatter.4.cloned.1.call-done = bf16[512,704]{1,0:T(8,128)(2,1)} async-done(((bf16[2048,704]{1,0:T(8,128)(2,1)}), bf16[512,704]{1,0:T(8,128)(2,1)}) %reduce-scatter.4.cloned.1.call-update) | async-done | bytes 720912 | tf_op jit(solution)/shard_map/reduce_scatter | solution.py:224
  369.7 5.2 collective-permute-done.34
  382.7 3.8 convolution_convert_fusion.5
  386.4 5.7 collective-permute-done.37
  400.2 3.8 fusion.13
  404.0 8.0 %collective-permute-done.38 = bf16[128,2048]{1,0:T(8,128)(2,1)S(1)} collective-permute-done((bf16[128,2048]{1,0:T(8,128)(2,1)S(1)}, bf16[128,2048]{1,0:T(8,128)(2,1)S(1)}, u32[]{:S(2)}, u32[]{:S(2)}) %collective-permute-start.38) | collective-permute-done | bytes 524320 | tf_op jit(solution)/shard_map/ppermute | solution.py:24
  417.2 5.0 collective-permute-done.43
  423.3 3.8 collective-permute-done.41
  432.6 3.4 convolution_convert_fusion.17
  436.0 8.9 %attend_backward.1 = (bf16[32,2,16,768]{3,2,1,0:T(8,128)(2,1)S(1)}, f32[2,8,768]{2,1,0:T(8,128)S(1)}) custom-call(s32[2]{0:T(128)S(1)} %dynamic_slice.15.lens, bf16[32,2,16,768]{3,2,1,0:T(8,128)(2,1)S(1)} %get-tuple-element.352.qkv, bf16[32,2,16,256]{3,2,1,0:T(8,128)(2,1)S(1)} %bitcast.91, f32[32,2,16,256]{3,2,1,0:T(8,128)S(1)} %get-tuple-element.365.full, ...), custom_call_target="tpu_custom_call" | custom-call | tf_op jit(solution)/shard_map/attend_backward/pallas_call | solution.py:396
  444.9 5.2 convolution_convert_fusion.4
  456.0 3.9 fusion.18
  462.6 4.1 convolution_convert_fusion.1
  476.5 5.1 collective-permute-done.54
  491.0 8.6 %collective-permute-done.57 = bf16[32,2048]{1,0:T(8,128)(2,1)S(1)} collective-permute-done((bf16[32,2048]{1,0:T(8,128)(2,1)}, bf16[32,2048]{1,0:T(8,128)(2,1)S(1)}, u32[]{:S(2)}, u32[]{:S(2)}) %collective-permute-start.57) | collective-permute-done | bytes 131104 | tf_op jit(solution)/shard_map/ppermute | solution.py:24
  501.4 16.1 %collective-permute-done.59 = bf16[32,2048]{1,0:T(8,128)(2,1)S(1)} collective-permute-done((bf16[32,2048]{1,0:T(8,128)(2,1)}, bf16[32,2048]{1,0:T(8,128)(2,1)S(1)}, u32[]{:S(2)}, u32[]{:S(2)}) %collective-permute-start.59) | collective-permute-done | bytes 131104 | tf_op jit(solution)/shard_map/ppermute | solution.py:24
  527.7 8.8 %collective-permute-done.64 = bf16[256,704]{1,0:T(8,128)(2,1)S(1)} collective-permute-done((bf16[256,704]{1,0:T(8,128)(2,1)S(1)}, bf16[256,704]{1,0:T(8,128)(2,1)S(1)}, u32[]{:S(2)}, u32[]{:S(2)}) %collective-permute-start.64) | collective-permute-done | bytes 360480 | tf_op jit(solution)/shard_map/ppermute | solution.py:24
  541.1 8.2 %collective-permute-done.63 = bf16[256,1408]{1,0:T(8,128)(2,1)S(1)} collective-permute-done((bf16[256,1408]{1,0:T(8,128)(2,1)S(1)}, bf16[256,1408]{1,0:T(8,128)(2,1)S(1)}, u32[]{:S(2)}, u32[]{:S(2)}) %collective-permute-start.63) | collective-permute-done | bytes 720928 | tf_op jit(solution)/shard_map/ppermute | solution.py:24
  551.7 15.7 %collective-permute-done.62 = bf16[32,2048]{1,0:T(8,128)(2,1)S(1)} collective-permute-done((bf16[32,2048]{1,0:T(8,128)(2,1)S(1)}, bf16[32,2048]{1,0:T(8,128)(2,1)S(1)}, u32[]{:S(2)}, u32[]{:S(2)}) %collective-permute-start.62) | collective-permute-done | bytes 131104 | tf_op jit(solution)/shard_map/ppermute | solution.py:24
  573.4 10.1 %collective-permute-done.71 = f32[4,2048]{1,0:T(4,128)S(1)} collective-permute-done((f32[4,2048]{1,0:T(4,128)S(1)}, f32[4,2048]{1,0:T(4,128)S(1)}, u32[]{:S(2)}, u32[]{:S(2)}) %collective-permute-start.71) | collective-permute-done | bytes 32800 | tf_op jit(solution)/shard_map/ppermute | solution.py:24
  585.0 2.9 copy.70
  595.5 8.7 %fusion.131 = (bf16[256,2,1408]{2,1,0:T(2,128)(2,1)}, f32[256,2,1408]{2,1,0:T(2,128)S(1)}, f32[256,2,1408]{2,1,0:T(2,128)}) fusion(f32[256,2,1408]{2,1,0:T(2,128)S(1)} %copy-done.10, f32[256,2,1408]{2,1,0:T(2,128)} %param.37, f32[256,2,704]{2,1,0:T(2,128)S(1)} %copy.72, f32[256,2,704]{2,1,0:T(2,128)S(1)} %copy.71), kind=kLoop, calls=%fused_computation.369 | loop fusion | flops 7208960 | bytes 15859712 | tf_op jit(solution)/shard_map/convert_element_type | solution.py:715
  608.3 4.0 multiply_add_fusion
  (590 shorter events, 215.2 us)
Async XLA Ops:
  7.2 115.2 %all-gather.3.cloned.1.call-start = ((), (), s32[]{:S(2)}) async-start(), calls=%async_computation.3 | async-start | bytes 5242880 | tf_op jit(solution)/shard_map/all_gather | solution.py:221
  13.6 14.0 %collective-permute-start = (bf16[256,1024]{1,0:T(8,128)(2,1)}, bf16[256,1024]{1,0:T(8,128)(2,1)}, u32[]{:S(2)}, u32[]{:S(2)}) collective-permute-start(bf16[256,1024]{1,0:T(8,128)(2,1)} %broadcast_select_fusion.11), channel_id=1, source_target_pairs={{0,4},{4,0},{8,12},{12,8},{16,20},{20,16},{24,28},{28,24},{1,5},{5... | collective-permute-start | bytes 1572872 | tf_op jit(solution)/shard_map/ppermute | solution.py:24
  16.2 14.0 %collective-permute-start.1 = (bf16[32,2048]{1,0:T(8,128)(2,1)}, bf16[32,2048]{1,0:T(8,128)(2,1)S(1)}, u32[]{:S(2)}, u32[]{:S(2)}) collective-permute-start(bf16[32,2048]{1,0:T(8,128)(2,1)} %convolution_convert_fusion.15), channel_id=1, source_target_pairs={{0,8},{4,12},{8,0},{12,4},{16,24},{20,28},{24,16},{28,20},{1,9},{5... | collective-permute-start | bytes 393224 | tf_op jit(solution)/shard_map/ppermute | solution.py:24
  36.9 18.2 %collective-permute-start.7 = (bf16[256,1408]{1,0:T(8,128)(2,1)S(1)}, bf16[256,1408]{1,0:T(8,128)(2,1)}, u32[]{:S(2)}, u32[]{:S(2)}) collective-permute-start(bf16[256,1408]{1,0:T(8,128)(2,1)S(1)} %copy.60), channel_id=1, source_target_pairs={{0,4},{4,0},{8,12},{12,8},{16,20},{20,16},{24,28},{28,24},{1,5},{5... | collective-permute-start | bytes 2162696 | tf_op jit(solution)/shard_map/ppermute | solution.py:24
  37.5 19.0 %collective-permute-start.4 = (bf16[5,2048]{1,0:T(8,128)(2,1)S(1)}, bf16[5,2048]{1,0:T(8,128)(2,1)S(1)}, u32[]{:S(2)}, u32[]{:S(2)}) collective-permute-start(bf16[5,2048]{1,0:T(8,128)(2,1)S(1)} %copy-done.70), channel_id=1, source_target_pairs={{0,4},{4,0},{8,12},{12,8},{16,20},{20,16},{24,28},{28,24},{1,5},{5... | collective-permute-start | bytes 61448 | tf_op jit(solution)/shard_map/ppermute | solution.py:24
  39.0 17.5 %collective-permute-start.5 = (bf16[5,2048]{1,0:T(8,128)(2,1)S(1)}, bf16[5,2048]{1,0:T(8,128)(2,1)S(1)}, u32[]{:S(2)}, u32[]{:S(2)}) collective-permute-start(bf16[5,2048]{1,0:T(8,128)(2,1)S(1)} %copy-done.70), channel_id=1, source_target_pairs={{0,16},{4,20},{8,24},{12,28},{16,0},{20,4},{24,8},{28,12},{1,17},{... | collective-permute-start | bytes 61448 | tf_op jit(solution)/shard_map/ppermute | solution.py:24
  39.0 17.5 %collective-permute-start.6 = (bf16[5,2048]{1,0:T(8,128)(2,1)S(1)}, bf16[5,2048]{1,0:T(8,128)(2,1)S(1)}, u32[]{:S(2)}, u32[]{:S(2)}) collective-permute-start(bf16[5,2048]{1,0:T(8,128)(2,1)S(1)} %copy-done.70), channel_id=1, source_target_pairs={{0,20},{4,16},{8,28},{12,24},{16,4},{20,0},{24,12},{28,8},{1,21},{... | collective-permute-start | bytes 61448 | tf_op jit(solution)/shard_map/ppermute | solution.py:24
  42.2 240.7 %all-gather.5.cloned.1.call-start = ((), (), s32[]{:S(2)}) async-start(), calls=%async_computation.4 | async-start | bytes 11141120 | tf_op jit(solution)/shard_map/all_gather | solution.py:221
  122.4 21.0 %collective-permute-start.15 = (bf16[32,2048]{1,0:T(8,128)(2,1)}, bf16[32,2048]{1,0:T(8,128)(2,1)}, u32[]{:S(2)}, u32[]{:S(2)}) collective-permute-start(bf16[32,2048]{1,0:T(8,128)(2,1)} %convolution_convert_fusion.11), channel_id=1, source_target_pairs={{0,8},{4,12},{8,0},{12,4},{16,24},{20,28},{24,16},{28,20},{1,9},{5... | collective-permute-start | bytes 393224 | tf_op jit(solution)/shard_map/ppermute | solution.py:24
  122.5 21.0 %collective-permute-start.16 = (bf16[32,2048]{1,0:T(8,128)(2,1)}, bf16[32,2048]{1,0:T(8,128)(2,1)}, u32[]{:S(2)}, u32[]{:S(2)}) collective-permute-start(bf16[32,2048]{1,0:T(8,128)(2,1)} %convolution_convert_fusion.10), channel_id=1, source_target_pairs={{0,16},{4,20},{8,24},{12,28},{16,0},{20,4},{24,8},{28,12},{1,17},{... | collective-permute-start | bytes 393224 | tf_op jit(solution)/shard_map/ppermute | solution.py:24
  123.7 19.8 %collective-permute-start.17 = (bf16[32,2048]{1,0:T(8,128)(2,1)}, bf16[32,2048]{1,0:T(8,128)(2,1)}, u32[]{:S(2)}, u32[]{:S(2)}) collective-permute-start(bf16[32,2048]{1,0:T(8,128)(2,1)} %convolution_convert_fusion.9), channel_id=1, source_target_pairs={{0,24},{4,28},{8,16},{12,20},{16,8},{20,12},{24,0},{28,4},{1,25},{... | collective-permute-start | bytes 393224 | tf_op jit(solution)/shard_map/ppermute | solution.py:24
  125.9 238.3 %reduce-scatter.4.cloned.1.call-start = ((), (), s32[]{:S(2)}) async-start(), calls=%async_computation.5 | async-start | bytes 3932160 | tf_op jit(solution)/shard_map/reduce_scatter | solution.py:224
  148.3 21.2 %collective-permute-start.21 = (bf16[128,2048]{1,0:T(8,128)(2,1)S(1)}, bf16[128,2048]{1,0:T(8,128)(2,1)S(1)}, u32[]{:S(2)}, u32[]{:S(2)}) collective-permute-start(bf16[128,2048]{1,0:T(8,128)(2,1)S(1)} %maximum_select_fusion), channel_id=1, source_target_pairs={{0,2},{1,3},{2,0},{3,1},{4,6},{5,7},{6,4},{7,5},{8,10},{9,11},{10,... | collective-permute-start | bytes 1572872 | tf_op jit(solution)/shard_map/ppermute | solution.py:24
  149.8 19.7 %collective-permute-start.22 = (bf16[128,2048]{1,0:T(8,128)(2,1)S(1)}, bf16[128,2048]{1,0:T(8,128)(2,1)S(1)}, u32[]{:S(2)}, u32[]{:S(2)}) collective-permute-start(bf16[128,2048]{1,0:T(8,128)(2,1)S(1)} %maximum_select_fusion), channel_id=1, source_target_pairs={{0,4},{4,0},{8,12},{12,8},{16,20},{20,16},{24,28},{28,24},{1,5},{5... | collective-permute-start | bytes 1572872 | tf_op jit(solution)/shard_map/ppermute | solution.py:24
  152.4 15.8 %collective-permute-start.19 = (bf16[64,2048]{1,0:T(8,128)(2,1)S(1)}, bf16[64,2048]{1,0:T(8,128)(2,1)S(1)}, u32[]{:S(2)}, u32[]{:S(2)}) collective-permute-start(bf16[64,2048]{1,0:T(8,128)(2,1)S(1)} %get-tuple-element.509), channel_id=1, source_target_pairs={{0,2},{1,3},{2,0},{3,1},{4,6},{5,7},{6,4},{7,5},{8,10},{9,11},{10,... | collective-permute-start | bytes 786440 | tf_op jit(solution)/shard_map/ppermute | solution.py:24
  153.1 16.4 %collective-permute-start.20 = (bf16[64,2048]{1,0:T(8,128)(2,1)S(1)}, bf16[64,2048]{1,0:T(8,128)(2,1)S(1)}, u32[]{:S(2)}, u32[]{:S(2)}) collective-permute-start(bf16[64,2048]{1,0:T(8,128)(2,1)S(1)} %get-tuple-element.508), channel_id=1, source_target_pairs={{0,4},{4,0},{8,12},{12,8},{16,20},{20,16},{24,28},{28,24},{1,5},{5... | collective-permute-start | bytes 786440 | tf_op jit(solution)/shard_map/ppermute | solution.py:24
  171.2 19.5 %collective-permute-start.24 = (bf16[128,2048]{1,0:T(8,128)(2,1)S(1)}, bf16[128,2048]{1,0:T(8,128)(2,1)S(1)}, u32[]{:S(2)}, u32[]{:S(2)}) collective-permute-start(bf16[128,2048]{1,0:T(8,128)(2,1)S(1)} %pad_maximum_fusion.10), channel_id=1, source_target_pairs={{0,2},{1,3},{2,0},{3,1},{4,6},{5,7},{6,4},{7,5},{8,10},{9,11},{10,... | collective-permute-start | bytes 1572872 | tf_op jit(solution)/shard_map/ppermute | solution.py:24
  171.9 18.8 %collective-permute-start.23 = (bf16[128,2048]{1,0:T(8,128)(2,1)S(1)}, bf16[128,2048]{1,0:T(8,128)(2,1)S(1)}, u32[]{:S(2)}, u32[]{:S(2)}) collective-permute-start(bf16[128,2048]{1,0:T(8,128)(2,1)S(1)} %pad_maximum_fusion.9), channel_id=1, source_target_pairs={{0,4},{4,0},{8,12},{12,8},{16,20},{20,16},{24,28},{28,24},{1,5},{5... | collective-permute-start | bytes 1572872 | tf_op jit(solution)/shard_map/ppermute | solution.py:24
  173.6 17.1 %collective-permute-start.25 = (bf16[64,2048]{1,0:T(8,128)(2,1)S(1)}, bf16[64,2048]{1,0:T(8,128)(2,1)S(1)}, u32[]{:S(2)}, u32[]{:S(2)}) collective-permute-start(bf16[64,2048]{1,0:T(8,128)(2,1)S(1)} %slice.514), channel_id=1, source_target_pairs={{0,4},{4,0},{8,12},{12,8},{16,20},{20,16},{24,28},{28,24},{1,5},{5... | collective-permute-start | bytes 786440 | tf_op jit(solution)/shard_map/ppermute | solution.py:24
  174.2 16.5 %collective-permute-start.26 = (bf16[64,2048]{1,0:T(8,128)(2,1)S(1)}, bf16[64,2048]{1,0:T(8,128)(2,1)S(1)}, u32[]{:S(2)}, u32[]{:S(2)}) collective-permute-start(bf16[64,2048]{1,0:T(8,128)(2,1)S(1)} %slice.515), channel_id=1, source_target_pairs={{0,2},{1,3},{2,0},{3,1},{4,6},{5,7},{6,4},{7,5},{8,10},{9,11},{10,... | collective-permute-start | bytes 786440 | tf_op jit(solution)/shard_map/ppermute | solution.py:24
  190.8 18.2 %collective-permute-start.29 = (bf16[512,2048]{1,0:T(8,128)(2,1)S(1)}, bf16[512,2048]{1,0:T(8,128)(2,1)S(1)}, u32[]{:S(2)}, u32[]{:S(2)}) collective-permute-start(bf16[512,2048]{1,0:T(8,128)(2,1)S(1)} %constant_dynamic-update-slice_fusion.11), channel_id=1, source_target_pairs={{0,1},{1,0},{2,3},{3,2},{4,5},{5,4},{6,7},{7,6},{8,9},{9,8},{10,11... | collective-permute-start | bytes 6291464 | tf_op jit(solution)/shard_map/ppermute | solution.py:24
  193.6 14.4 %collective-permute-start.27 = (bf16[128,2048]{1,0:T(8,128)(2,1)S(1)}, bf16[128,2048]{1,0:T(8,128)(2,1)S(1)}, u32[]{:S(2)}, u32[]{:S(2)}) collective-permute-start(bf16[128,2048]{1,0:T(8,128)(2,1)S(1)} %add_convert_fusion.1), channel_id=1, source_target_pairs={{0,2},{1,3},{2,0},{3,1},{4,6},{5,7},{6,4},{7,5},{8,10},{9,11},{10,... | collective-permute-start | bytes 1572872 | tf_op jit(solution)/shard_map/ppermute | solution.py:24
  195.0 14.0 %collective-permute-start.28 = (bf16[128,2048]{1,0:T(8,128)(2,1)S(1)}, bf16[128,2048]{1,0:T(8,128)(2,1)S(1)}, u32[]{:S(2)}, u32[]{:S(2)}) collective-permute-start(bf16[128,2048]{1,0:T(8,128)(2,1)S(1)} %add_convert_fusion.1), channel_id=1, source_target_pairs={{0,4},{4,0},{8,12},{12,8},{16,20},{20,16},{24,28},{28,24},{1,5},{5... | collective-permute-start | bytes 1572872 | tf_op jit(solution)/shard_map/ppermute | solution.py:24
  303.8 166.9 %reduce-scatter.6.cloned.1.call-start = ((), (), s32[]{:S(2)}) async-start(), calls=%async_computation.6 | async-start | bytes 7208960 | tf_op jit(solution)/shard_map/reduce_scatter | solution.py:224
  322.4 15.9 %collective-permute-start.33 = (bf16[512,2048]{1,0:T(8,128)(2,1)}, bf16[512,2048]{1,0:T(8,128)(2,1)}, u32[]{:S(2)}, u32[]{:S(2)}) collective-permute-start(bf16[512,2048]{1,0:T(8,128)(2,1)} %fusion.10), channel_id=1, source_target_pairs={{0,1},{1,0},{2,3},{3,2},{4,5},{5,4},{6,7},{7,6},{8,9},{9,8},{10,11... | collective-permute-start | bytes 6291464 | tf_op jit(solution)/shard_map/ppermute | solution.py:24
  369.4 214.1 %reduce-scatter.8.cloned.1.call-start = ((), (), s32[]{:S(2)}) async-start(), calls=%async_computation.7 | async-start | bytes 5242880 | tf_op jit(solution)/shard_map/reduce_scatter | solution.py:224
  394.1 18.6 %collective-permute-start.40 = (bf16[512,2048]{1,0:T(8,128)(2,1)S(1)}, bf16[512,2048]{1,0:T(8,128)(2,1)S(1)}, u32[]{:S(2)}, u32[]{:S(2)}) collective-permute-start(bf16[512,2048]{1,0:T(8,128)(2,1)S(1)} %convolution_convert_fusion.5), channel_id=1, source_target_pairs={{0,1},{1,0},{2,3},{3,2},{4,5},{5,4},{6,7},{7,6},{8,9},{9,8},{10,11... | collective-permute-start | bytes 6291464 | tf_op jit(solution)/shard_map/ppermute | solution.py:24
  397.7 14.3 %collective-permute-start.38 = (bf16[128,2048]{1,0:T(8,128)(2,1)S(1)}, bf16[128,2048]{1,0:T(8,128)(2,1)S(1)}, u32[]{:S(2)}, u32[]{:S(2)}) collective-permute-start(bf16[128,2048]{1,0:T(8,128)(2,1)S(1)} %get-tuple-element.358), channel_id=1, source_target_pairs={{0,2},{1,3},{2,0},{3,1},{4,6},{5,7},{6,4},{7,5},{8,10},{9,11},{10,... | collective-permute-start | bytes 1572872 | tf_op jit(solution)/shard_map/ppermute | solution.py:24
  398.7 14.0 %collective-permute-start.39 = (bf16[128,2048]{1,0:T(8,128)(2,1)S(1)}, bf16[128,2048]{1,0:T(8,128)(2,1)S(1)}, u32[]{:S(2)}, u32[]{:S(2)}) collective-permute-start(bf16[128,2048]{1,0:T(8,128)(2,1)S(1)} %get-tuple-element.358), channel_id=1, source_target_pairs={{0,4},{4,0},{8,12},{12,8},{16,20},{20,16},{24,28},{28,24},{1,5},{5... | collective-permute-start | bytes 1572872 | tf_op jit(solution)/shard_map/ppermute | solution.py:24
  428.7 21.5 %collective-permute-start.47 = (bf16[128,2048]{1,0:T(8,128)(2,1)}, bf16[128,2048]{1,0:T(8,128)(2,1)}, u32[]{:S(2)}, u32[]{:S(2)}) collective-permute-start(bf16[128,2048]{1,0:T(8,128)(2,1)} %pad_maximum_fusion.14), channel_id=1, source_target_pairs={{0,2},{1,3},{2,0},{3,1},{4,6},{5,7},{6,4},{7,5},{8,10},{9,11},{10,... | collective-permute-start | bytes 1572872 | tf_op jit(solution)/shard_map/ppermute | solution.py:24
  430.6 19.6 %collective-permute-start.46 = (bf16[128,2048]{1,0:T(8,128)(2,1)}, bf16[128,2048]{1,0:T(8,128)(2,1)}, u32[]{:S(2)}, u32[]{:S(2)}) collective-permute-start(bf16[128,2048]{1,0:T(8,128)(2,1)} %pad_maximum_fusion.13), channel_id=1, source_target_pairs={{0,4},{4,0},{8,12},{12,8},{16,20},{20,16},{24,28},{28,24},{1,5},{5... | collective-permute-start | bytes 1572872 | tf_op jit(solution)/shard_map/ppermute | solution.py:24
  450.2 19.2 %collective-permute-start.49 = (f32[1,768]{1,0:T(1,128)S(1)}, f32[1,768]{1,0:T(1,128)S(1)}, u32[]{:S(2)}, u32[]{:S(2)}) collective-permute-start(f32[1,768]{1,0:T(1,128)S(1)} %broadcast_in_dim.64), channel_id=1, source_target_pairs={{0,16},{4,20},{8,24},{12,28},{16,0},{20,4},{24,8},{28,12},{1,17},{... | collective-permute-start | bytes 9224 | tf_op jit(solution)/shard_map/ppermute | solution.py:24
  450.5 18.8 %collective-permute-start.50 = (f32[1,768]{1,0:T(1,128)S(1)}, f32[1,768]{1,0:T(1,128)S(1)}, u32[]{:S(2)}, u32[]{:S(2)}) collective-permute-start(f32[1,768]{1,0:T(1,128)S(1)} %broadcast_in_dim.64), channel_id=1, source_target_pairs={{0,8},{4,12},{8,0},{12,4},{16,24},{20,28},{24,16},{28,20},{1,9},{5... | collective-permute-start | bytes 9224 | tf_op jit(solution)/shard_map/ppermute | solution.py:24
  452.0 17.4 %collective-permute-start.51 = (f32[1,768]{1,0:T(1,128)S(1)}, f32[1,768]{1,0:T(1,128)S(1)}, u32[]{:S(2)}, u32[]{:S(2)}) collective-permute-start(f32[1,768]{1,0:T(1,128)S(1)} %broadcast_in_dim.64), channel_id=1, source_target_pairs={{0,24},{4,28},{8,16},{12,20},{16,8},{20,12},{24,0},{28,4},{1,25},{... | collective-permute-start | bytes 9224 | tf_op jit(solution)/shard_map/ppermute | solution.py:24
  453.7 15.6 %collective-permute-start.48 = (bf16[512,2048]{1,0:T(8,128)(2,1)}, bf16[512,2048]{1,0:T(8,128)(2,1)S(1)}, u32[]{:S(2)}, u32[]{:S(2)}) collective-permute-start(bf16[512,2048]{1,0:T(8,128)(2,1)} %convolution_convert_fusion.4), channel_id=1, source_target_pairs={{0,1},{1,0},{2,3},{3,2},{4,5},{5,4},{6,7},{7,6},{8,9},{9,8},{10,11... | collective-permute-start | bytes 6291464 | tf_op jit(solution)/shard_map/ppermute | solution.py:24
  483.9 33.6 %collective-permute-start.56 = (bf16[128,2048]{1,0:T(8,128)(2,1)S(1)}, bf16[128,2048]{1,0:T(8,128)(2,1)}, u32[]{:S(2)}, u32[]{:S(2)}) collective-permute-start(bf16[128,2048]{1,0:T(8,128)(2,1)S(1)} %pad_maximum_fusion.16), channel_id=1, source_target_pairs={{0,2},{1,3},{2,0},{3,1},{4,6},{5,7},{6,4},{7,5},{8,10},{9,11},{10,... | collective-permute-start | bytes 1572872 | tf_op jit(solution)/shard_map/ppermute | solution.py:24
  485.2 33.0 %collective-permute-start.55 = (bf16[128,2048]{1,0:T(8,128)(2,1)S(1)}, bf16[128,2048]{1,0:T(8,128)(2,1)}, u32[]{:S(2)}, u32[]{:S(2)}) collective-permute-start(bf16[128,2048]{1,0:T(8,128)(2,1)S(1)} %pad_maximum_fusion.15), channel_id=1, source_target_pairs={{0,4},{4,0},{8,12},{12,8},{16,20},{20,16},{24,28},{28,24},{1,5},{5... | collective-permute-start | bytes 1572872 | tf_op jit(solution)/shard_map/ppermute | solution.py:24
  488.2 29.3 %collective-permute-start.59 = (bf16[32,2048]{1,0:T(8,128)(2,1)}, bf16[32,2048]{1,0:T(8,128)(2,1)S(1)}, u32[]{:S(2)}, u32[]{:S(2)}) collective-permute-start(bf16[32,2048]{1,0:T(8,128)(2,1)} %get-tuple-element.402), channel_id=1, source_target_pairs={{0,24},{4,28},{8,16},{12,20},{16,8},{20,12},{24,0},{28,4},{1,25},{... | collective-permute-start | bytes 393224 | tf_op jit(solution)/shard_map/ppermute | solution.py:24
  520.7 18.9 %collective-permute-start.65 = (f32[4,2048]{1,0:T(4,128)S(1)}, f32[4,2048]{1,0:T(4,128)S(1)}, u32[]{:S(2)}, u32[]{:S(2)}) collective-permute-start(f32[4,2048]{1,0:T(4,128)S(1)} %pad_maximum_fusion.17), channel_id=1, source_target_pairs={{0,16},{4,20},{8,24},{12,28},{16,0},{20,4},{24,8},{28,12},{1,17},{... | collective-permute-start | bytes 98312 | tf_op jit(solution)/shard_map/ppermute | solution.py:24
  520.8 19.8 %collective-permute-start.66 = (f32[4,2048]{1,0:T(4,128)S(1)}, f32[4,2048]{1,0:T(4,128)S(1)}, u32[]{:S(2)}, u32[]{:S(2)}) collective-permute-start(f32[4,2048]{1,0:T(4,128)S(1)} %pad_maximum_fusion.17), channel_id=1, source_target_pairs={{0,8},{4,12},{8,0},{12,4},{16,24},{20,28},{24,16},{28,20},{1,9},{5... | collective-permute-start | bytes 98312 | tf_op jit(solution)/shard_map/ppermute | solution.py:24
  521.9 29.1 %collective-permute-start.67 = (f32[4,2048]{1,0:T(4,128)S(1)}, f32[4,2048]{1,0:T(4,128)S(1)}, u32[]{:S(2)}, u32[]{:S(2)}) collective-permute-start(f32[4,2048]{1,0:T(4,128)S(1)} %pad_maximum_fusion.17), channel_id=1, source_target_pairs={{0,24},{4,28},{8,16},{12,20},{16,8},{20,12},{24,0},{28,4},{1,25},{... | collective-permute-start | bytes 98312 | tf_op jit(solution)/shard_map/ppermute | solution.py:24
  526.2 23.1 %collective-permute-start.63 = (bf16[256,1408]{1,0:T(8,128)(2,1)S(1)}, bf16[256,1408]{1,0:T(8,128)(2,1)S(1)}, u32[]{:S(2)}, u32[]{:S(2)}) collective-permute-start(bf16[256,1408]{1,0:T(8,128)(2,1)S(1)} %broadcast_select_fusion.3), channel_id=1, source_target_pairs={{0,4},{4,0},{8,12},{12,8},{16,20},{20,16},{24,28},{28,24},{1,5},{5... | collective-permute-start | bytes 2162696 | tf_op jit(solution)/shard_map/ppermute | solution.py:24
  536.5 31.0 %collective-permute-start.68 = (bf16[128,2048]{1,0:T(8,128)(2,1)S(1)}, bf16[128,2048]{1,0:T(8,128)(2,1)S(1)}, u32[]{:S(2)}, u32[]{:S(2)}) collective-permute-start(bf16[128,2048]{1,0:T(8,128)(2,1)S(1)} %convolution_convert_fusion.8), channel_id=1, source_target_pairs={{0,2},{1,3},{2,0},{3,1},{4,6},{5,7},{6,4},{7,5},{8,10},{9,11},{10,... | collective-permute-start | bytes 1572872 | tf_op jit(solution)/shard_map/ppermute | solution.py:24
  549.3 18.1 %collective-permute-start.62 = (bf16[32,2048]{1,0:T(8,128)(2,1)S(1)}, bf16[32,2048]{1,0:T(8,128)(2,1)S(1)}, u32[]{:S(2)}, u32[]{:S(2)}) collective-permute-start(bf16[32,2048]{1,0:T(8,128)(2,1)S(1)} %get-tuple-element.544), channel_id=1, source_target_pairs={{0,24},{4,28},{8,16},{12,20},{16,8},{20,12},{24,0},{28,4},{1,25},{... | collective-permute-start | bytes 393224 | tf_op jit(solution)/shard_map/ppermute | solution.py:24
  569.4 14.1 %collective-permute-start.69 = (bf16[128,2048]{1,0:T(8,128)(2,1)S(1)}, bf16[128,2048]{1,0:T(8,128)(2,1)}, u32[]{:S(2)}, u32[]{:S(2)}) collective-permute-start(bf16[128,2048]{1,0:T(8,128)(2,1)S(1)} %convolution_convert_fusion.7), channel_id=1, source_target_pairs={{0,2},{1,3},{2,0},{3,1},{4,6},{5,7},{6,4},{7,5},{8,10},{9,11},{10,... | collective-permute-start | bytes 1572872 | tf_op jit(solution)/shard_map/ppermute | solution.py:24
  593.0 20.9 %collective-permute-start.75 = (bf16[512,2048]{1,0:T(8,128)(2,1)S(1)}, bf16[512,2048]{1,0:T(8,128)(2,1)S(1)}, u32[]{:S(2)}, u32[]{:S(2)}) collective-permute-start(bf16[512,2048]{1,0:T(8,128)(2,1)S(1)} %constant_dynamic-update-slice_fusion.34), channel_id=1, source_target_pairs={{0,1},{1,0},{2,3},{3,2},{4,5},{5,4},{6,7},{7,6},{8,9},{9,8},{10,11... | collective-permute-start | bytes 6291464 | tf_op jit(solution)/shard_map/ppermute | solution.py:24
  593.2 20.7 %collective-permute-start.74 = (f32[4,2048]{1,0:T(4,128)S(1)}, f32[4,2048]{1,0:T(4,128)S(1)}, u32[]{:S(2)}, u32[]{:S(2)}) collective-permute-start(f32[4,2048]{1,0:T(4,128)S(1)} %add_add_fusion), channel_id=1, source_target_pairs={{0,4},{4,0},{8,12},{12,8},{16,20},{20,16},{24,28},{28,24},{1,5},{5... | collective-permute-start | bytes 98312 | tf_op jit(solution)/shard_map/ppermute | solution.py:24
  595.1 18.5 %collective-permute-start.73 = (bf16[256,1024]{1,0:T(8,128)(2,1)S(1)}, bf16[256,1024]{1,0:T(8,128)(2,1)S(1)}, u32[]{:S(2)}, u32[]{:S(2)}) collective-permute-start(bf16[256,1024]{1,0:T(8,128)(2,1)S(1)} %broadcast_select_fusion.7), channel_id=1, source_target_pairs={{0,4},{4,0},{8,12},{12,8},{16,20},{20,16},{24,28},{28,24},{1,5},{5... | collective-permute-start | bytes 1572872 | tf_op jit(solution)/shard_map/ppermute | solution.py:24
  (158 other events, 1608.6 us)
Sparse Core Ops, SparseCore 0:
  42.4 80.0 all-gather.2
  126.0 156.8 all-gather.4
  304.0 60.2 reduce-scatter.3
  369.6 101.1 reduce-scatter.5
  472.9 101.0 reduce-scatter.7
